TPU v7x, 32 devices: a whole 2x2x4 slice. The times are simulated.
32 devices in a mesh: row: 4 (over z), col: 8 (over y, x, core).
Axes of the slice: x: 2, y: 2, z: 4, core: 2. Of those that a mesh axis runs over, the one named last changes fastest.
Arguments:
- amplitudes: float32 [4096, 4096], P('row', 'col'), may hold values from -1 to 1, as said below
- factors: float32 [4096, 256], P('row', 'col'), may hold values from -1.5 to 1.5
- occ_index: int32 [4096], replicated, may hold values from 0 to 63
- vir_index: int32 [4096], replicated, may hold values from 0 to 2047
- occ_energy: float32 [64], replicated, may hold values from -3 to -0.5
- vir_energy: float32 [2048], replicated, may hold values from 0.2 to 3
Outputs:
- new_amplitudes: float32 [4096, 4096], P('row', 'col')
Inputs may be any that keep to these rules, and one draw needn't show every extreme that they name: amplitudes is symmetric: amplitudes[p, q] equals amplitudes[q, p].
All inputs are finite; a program needn't handle non-finite values.
Results may differ from a plain program's by a relative error of at most 0.000096.
Values sent between devices are 32-bit elements; how exact they have to be, the bound alone decides.
No kernel may reach another device: no remote copies, remote signals or barrier semaphores. Data moves between devices by JAX's collectives and lax.ppermute only.
A program may use at most 64 MiB of HBM per device.

v0:
```python
import jax
import jax.numpy as jnp
from jax import lax
from jax.sharding import PartitionSpec as P


def pair_energy(occupied, virtual, occ_energy, vir_energy):
    occ_table = jnp.arange(occ_energy.shape[0], dtype=jnp.int32)
    vir_table = jnp.arange(vir_energy.shape[0], dtype=jnp.int32)
    picked_vir = jnp.sum(
        jnp.where(virtual[:, None] == vir_table[None, :], vir_energy[None, :], 0.0), axis=1
    )
    picked_occ = jnp.sum(
        jnp.where(occupied[:, None] == occ_table[None, :], occ_energy[None, :], 0.0), axis=1
    )
    return picked_vir - picked_occ


def local(amplitudes, factors, occ_index, vir_index, occ_energy, vir_energy):
    tile_rows = amplitudes.shape[0]
    tile_cols = amplitudes.shape[1]
    row_index = lax.axis_index("row")
    col_index = lax.axis_index("col")
    col_count = lax.axis_size("col")
    block_ratio = col_count // lax.axis_size("row")
    column_piece = lax.all_gather(factors, "col", axis=1, tiled=True)
    contracted = lax.dot_general(
        amplitudes,
        column_piece,
        (((0,), (0,)), ((), ())),
        precision=lax.Precision.HIGHEST,
        preferred_element_type=jnp.float32,
    )
    joined = jnp.concatenate([column_piece, contracted], axis=0)
    row_factors = joined[:tile_rows]
    partial_sum = joined[tile_rows:]
    owned_block = lax.dynamic_slice_in_dim(
        row_factors, col_index % block_ratio * tile_cols, tile_cols, 0
    )
    owner_flag = jnp.where(row_index == col_index // block_ratio, 1.0, 0.0).astype(jnp.float32)
    partial_sum = partial_sum + owner_flag * owned_block
    column_share = lax.psum_scatter(partial_sum, "row", scatter_dimension=1, tiled=True)
    wide_col = lax.all_gather(column_share, "row", axis=1, tiled=True)
    piece_rows = tile_cols // col_count
    split_block = wide_col.reshape(col_count, piece_rows, wide_col.shape[1])
    arrived = lax.all_to_all(split_block, "col", split_axis=0, concat_axis=0, tiled=True)
    needed = lax.dynamic_slice_in_dim(arrived, row_index * block_ratio, block_ratio, 0)
    whole_pieces = lax.all_gather(needed, "col", axis=1, tiled=True)
    wide_row = whole_pieces.reshape(block_ratio * tile_cols, wide_col.shape[1])
    energy_rows = pair_energy(
        lax.dynamic_slice_in_dim(occ_index, row_index * tile_rows, tile_rows),
        lax.dynamic_slice_in_dim(vir_index, row_index * tile_rows, tile_rows),
        occ_energy,
        vir_energy,
    )
    energy_cols = pair_energy(
        lax.dynamic_slice_in_dim(occ_index, col_index * tile_cols, tile_cols),
        lax.dynamic_slice_in_dim(vir_index, col_index * tile_cols, tile_cols),
        occ_energy,
        vir_energy,
    )
    outer_sum = lax.dot_general(
        wide_row,
        wide_col,
        (((1,), (1,)), ((), ())),
        precision=lax.Precision.HIGHEST,
        preferred_element_type=jnp.float32,
    )
    return -outer_sum / (energy_rows[:, None] + energy_cols[None, :])


def solution(mesh):
    return jax.shard_map(
        local,
        mesh=mesh,
        in_specs=(P("row", "col"), P("row", "col"), P(), P(), P(), P()),
        out_specs=P("row", "col"),
        check_vma=False,
    )
```

profile of v0, /device:TPU:5, one launch (start us, length us, event | category | flops | bytes accessed | tf_op | source)
XLA Modules:
  0.0 122.6 jit_solution(16636859885570150338)
XLA Ops:
  6.5 0.0 copy-start
  6.5 0.0 all-gather.3.cloned.1.call-start
  6.5 0.7 all-gather.3.cloned.1.call-update
  7.3 0.0 reduce-scatter.2.cloned.1.call-start
  7.3 27.0 %all-gather.3.cloned.1.call-done = f32[1024,256]{0,1:T(8,128)} async-done(((f32[1024,32]{0,1:T(8,128)}), f32[1024,256]{0,1:T(8,128)}) %all-gather.3.cloned.1.call-update) | async-done | bytes 1048592 | tf_op jit(solution)/shard_map/all_gather | solution.py:26
  34.3 0.0 copy-done
  34.3 4.2 %convolution_add_fusion = f32[512,256]{0,1:T(8,128)} fusion(f32[1024,512]{1,0:T(8,128)S(1)} %copy-done, f32[1024,256]{0,1:T(8,128)} %all-gather.3.cloned.1.call-done, s32[]{:T(128)S(6)} %select_n.48, f32[]{:T(128)S(6)} %select_n.46), kind=kOutput, calls=%fused_computation.5 | convolution fusion | flops 1610874880 | bytes 4194312 | tf_op jit(solution)/shard_map/dot_general | solution.py:27
  38.5 0.0 copy-start.2
  38.5 0.0 copy-start.1
  38.5 0.0 reduce-scatter.2.cloned.1.call-update
  38.5 19.4 %reduce-scatter.2.cloned.1.call-done = f32[512,64]{0,1:T(8,128)} async-done(((f32[512,256]{0,1:T(8,128)}), f32[512,64]{0,1:T(8,128)}) %reduce-scatter.2.cloned.1.call-update) | async-done | bytes 131088 | tf_op jit(solution)/shard_map/reduce_scatter | solution.py:42
  57.9 13.4 %all_gather.10 = f32[512,256]{0,1:T(8,128)S(1)} all-gather(f32[512,64]{0,1:T(8,128)} %reduce-scatter.2.cloned.1.call-done), channel_id=1, replica_groups=mesh['row'=4,'col'=8] {'row'}, dimensions={1}, use_global_device_ids=true | all-gather | bytes 655360 | tf_op jit(solution)/shard_map/all_gather | solution.py:43
  71.4 1.0 copy.8
  72.3 9.1 %all-to-all-start = ((f32[8,64,256]{2,1,0:T(8,128)}), f32[8,64,256]{2,1,0:T(8,128)S(1)}, u32[]{:S(2)}, u32[]{:S(2)}) async-start(f32[8,64,256]{2,1,0:T(8,128)} %bitcast), calls=%async_computation.1 | async-start | bytes 1048576 | tf_op jit(solution)/shard_map/all_to_all | solution.py:46
  81.5 0.0 all-gather.5.cloned.1.call-start
  81.5 6.0 %all-to-all-done = f32[8,64,256]{2,1,0:T(8,128)S(1)} async-done(((f32[8,64,256]{2,1,0:T(8,128)}), f32[8,64,256]{2,1,0:T(8,128)S(1)}, u32[]{:S(2)}, u32[]{:S(2)}) %all-to-all-start) | async-done | bytes 524320 | tf_op jit(solution)/shard_map/all_to_all | solution.py:46
  87.4 0.7 constant_dynamic-slice_fusion
  88.1 0.0 all-gather.5.cloned.1.call-update
  88.1 0.8 dynamic_slice.23
  88.9 0.8 dynamic_slice.22
  89.6 0.7 dynamic_slice.21
  90.3 0.7 dynamic_slice.20
  91.0 0.0 copy-done.2
  91.0 0.1 select_reduce_fusion.3
  91.1 0.0 copy-done.1
  91.1 0.7 select_reduce_fusion.1
  91.8 0.1 select_reduce_fusion.2
  91.9 1.2 select_reduce_fusion
  93.1 18.4 %all-gather.5.cloned.1.call-done = f32[2,512,256]{2,1,0:T(8,128)} async-done(((f32[2,64,256]{2,1,0:T(8,128)}), f32[2,512,256]{2,1,0:T(8,128)}) %all-gather.5.cloned.1.call-update) | async-done | bytes 1048592 | tf_op jit(solution)/shard_map/all_gather | solution.py:48
  111.5 4.5 %add_divide_fusion = f32[1024,512]{1,0:T(8,128)} fusion(f32[1024,256]{1,0:T(8,128)} %bitcast.6, f32[512,256]{0,1:T(8,128)S(1)} %all_gather.10, f32[512]{0:T(512)S(1)} %sub.20, f32[1024]{0:T(1024)S(1)} %sub.19), kind=kOutput, calls=%fused_computation.4 | convolution fusion | flops 1612185600 | bytes 3676160 | tf_op jit(solution)/shard_map/dot_general | solution.py:62
  (2 shorter events, 0.0 us)
Async XLA Ops:
  6.5 27.8 %copy-start = (f32[1024,512]{1,0:T(8,128)S(1)}, f32[1024,512]{1,0:T(8,128)}, u32[]{:S(2)}) copy-start(f32[1024,512]{1,0:T(8,128)} %param.6) | copy-start | bytes 6291460
  6.5 27.8 %all-gather.3.cloned.1.call-start = ((), (), s32[]{:S(2)}) async-start(), calls=%async_computation.2 | async-start | bytes 1179648 | tf_op jit(solution)/shard_map/all_gather | solution.py:26
  7.3 50.7 %reduce-scatter.2.cloned.1.call-start = ((), (), s32[]{:S(2)}) async-start(), calls=%async_computation.3 | async-start | bytes 655360 | tf_op jit(solution)/shard_map/reduce_scatter | solution.py:42
  38.5 52.5 %copy-start.2 = (f32[64]{0:T(128)S(1)}, f32[64]{0:T(128)}, u32[]{:S(2)}) copy-start(f32[64]{0:T(128)} %param.10) | copy-start | bytes 772
  38.5 52.6 %copy-start.1 = (f32[2048]{0:T(1024)S(1)}, f32[2048]{0:T(1024)}, u32[]{:S(2)}) copy-start(f32[2048]{0:T(1024)} %param.11) | copy-start | bytes 24580
  72.3 15.1 %all-to-all-start = ((f32[8,64,256]{2,1,0:T(8,128)}), f32[8,64,256]{2,1,0:T(8,128)S(1)}, u32[]{:S(2)}, u32[]{:S(2)}) async-start(f32[8,64,256]{2,1,0:T(8,128)} %bitcast), calls=%async_computation.1 | async-start | bytes 1048576 | tf_op jit(solution)/shard_map/all_to_all | solution.py:46
  81.5 30.1 %all-gather.5.cloned.1.call-start = ((), (), s32[]{:S(2)}) async-start(), calls=%async_computation.4 | async-start | bytes 1179648 | tf_op jit(solution)/shard_map/all_gather | solution.py:48
Sparse Core Ops, SparseCore 0:
  9.2 25.0 all-gather.2
  38.6 19.2 reduce-scatter.1
  88.2 23.2 all-gather.4
where the time goes:
time: 124 us; the launch traced here: 123 us
  waiting for transfers between devices  71.6 us (58%)
  blocking collectives  13.4 us (11%)
  between operations  13.2 us (11%)
  starting transfers between devices  9.15 us (7%)
  matrix products  8.69 us (7%)
  local copies, waits for them, and re-layouts  4.57 us (4%)
  other arithmetic  2.08 us (2%)
    all_gather x1, waiting for transfers between devices, local(): column_piece = lax.all_gather(factors, 'col', axis=1, tiled=True)  27 us
    reduce_scatter x1, waiting for transfers between devices, local(): lax.psum_scatter(partial_sum, 'row', scatter_dimension=1, tiled=True)  19.4 us
    all_gather x1, waiting for transfers between devices, local(): whole_pieces = lax.all_gather(needed, 'col', axis=1, tiled=True)  18.4 us
    all_gather x1, blocking collectives, local(): wide_col = lax.all_gather(column_share, 'row', axis=1, tiled=True)  13.4 us
    all_to_all x1, starting transfers between devices, local(): lax.all_to_all(split_block, 'col', split_axis=0, concat_axis=0, tiled=True)  9.11 us
    all_to_all x1, waiting for transfers between devices, local(): lax.all_to_all(split_block, 'col', split_axis=0, concat_axis=0, tiled=True)  5.96 us
    dot_general x1, matrix products, local(): lax.dot_general(wide_row, wide_col, (((1,), (1,)), ((), ())), precision=l...  4.54 us
    dot_general x1, matrix products, local(): lax.dot_general(amplitudes, column_piece, (((0,), (0,)), ((), ())), preci...  4.15 us
  transfers between devices with their start and end apart: 4, of which 4 were waited for; matrix products, arithmetic and copies ran while one was open for 4% of the time, Pallas kernels for 0%

commit v1 on v0

v1 whole, which is shorter than its diff:
```python
import functools

import jax
import jax.numpy as jnp
from jax import lax
from jax.experimental import pallas as pl
from jax.experimental.pallas import tpu as pltpu
from jax.sharding import PartitionSpec as P

AXES = ("row", "col")
MIB = 1 << 20


def split(x):
    high = x.astype(jnp.bfloat16)
    low = (x - high.astype(jnp.float32)).astype(jnp.bfloat16)
    return high, low


def params(*arrays):
    held = sum(a.size * a.dtype.itemsize for a in arrays)
    return pltpu.CompilerParams(vmem_limit_bytes=2 * held + 4 * MIB)


def whole_specs(count):
    return [pl.BlockSpec(memory_space=pltpu.VMEM)] * count


def shape_of(shape, dtype=jnp.float32):
    return jax.ShapeDtypeStruct(shape, dtype)


def prepare_kernel(place, own_ref, sibling_ref, high_ref, low_ref):
    half = sibling_ref.shape[0]
    wide = own_ref.shape[1]
    core = place[0]
    own = own_ref[pl.ds(pl.multiple_of(core * half, half), half), :].T
    high, low = split(own)
    here = pl.ds(pl.multiple_of(core * wide, wide), wide)
    high_ref[here, :] = high
    low_ref[here, :] = low
    high, low = split(sibling_ref[...].T)
    there = pl.ds(pl.multiple_of((1 - core) * wide, wide), wide)
    high_ref[there, :] = high
    low_ref[there, :] = low


def prepare(core, own, sibling):
    half, wide = sibling.shape
    out = shape_of((2 * wide, half), jnp.bfloat16)
    return pl.pallas_call(
        prepare_kernel,
        out_shape=(out, out),
        in_specs=[pl.BlockSpec(memory_space=pltpu.SMEM)] + whole_specs(2),
        out_specs=whole_specs(2),
        compiler_params=params(own, sibling, out, out),
        cost_estimate=pl.CostEstimate(flops=0, bytes_accessed=own.size * 12, transcendentals=0),
        name="prepare",
    )(core.reshape(1), own, sibling)


def contract_kernel(own_ref, sibling_ref, high_ref, low_ref, out_ref):
    factors = jnp.concatenate([own_ref[...], sibling_ref[...]], axis=0)
    rows = factors.shape[0]
    high, low = split(factors)
    both = jnp.concatenate([high, low], axis=0)
    first = jnp.dot(both, high_ref[...], preferred_element_type=jnp.float32)
    second = jnp.dot(high, low_ref[...], preferred_element_type=jnp.float32)
    out_ref[...] = first[:rows] + (first[rows:] + second)


def contract(own, sibling, high, low):
    out = shape_of((2 * own.shape[0], high.shape[1]))
    return pl.pallas_call(
        contract_kernel,
        out_shape=out,
        in_specs=whole_specs(4),
        out_specs=whole_specs(1)[0],
        compiler_params=params(own, sibling, high, low, out),
        cost_estimate=pl.CostEstimate(
            flops=6 * out.size * high.shape[0], bytes_accessed=high.size * 4, transcendentals=0
        ),
        name="contract",
    )(own, sibling, high, low)


def pick(table, index):
    rows, lanes = table.shape
    length = index.shape[1]
    at_lane = lax.broadcasted_iota(jnp.int32, (lanes, length), 0) == index % lanes
    picked = jnp.dot(
        table,
        at_lane.astype(jnp.float32),
        precision=lax.Precision.HIGHEST,
        preferred_element_type=jnp.float32,
    )
    at_row = lax.broadcasted_iota(jnp.int32, (rows, length), 0) == index // lanes
    return jnp.sum(jnp.where(at_row, picked, 0.0), axis=0, keepdims=True)


def energy_kernel(place, occ_ref, vir_ref, occ_table, vir_table, rows_ref, cols_ref):
    for number, out_ref in enumerate((rows_ref, cols_ref)):
        length = out_ref.shape[1]
        here = pl.ds(pl.multiple_of(place[number] * length, length), length)
        out_ref[...] = pick(vir_table[...], vir_ref[:, here]) - pick(occ_table[...], occ_ref[:, here])


def as_table(energies):
    lanes = 128
    padded = jnp.pad(energies, (0, -energies.shape[0] % lanes))
    return padded.reshape(-1, lanes)


def pair_energies(place, occ_index, vir_index, occ_energy, vir_energy, rows, cols):
    occ_index, vir_index = occ_index[None, :], vir_index[None, :]
    occ_table, vir_table = as_table(occ_energy), as_table(vir_energy)
    return pl.pallas_call(
        energy_kernel,
        out_shape=(shape_of((1, rows)), shape_of((1, cols))),
        in_specs=[pl.BlockSpec(memory_space=pltpu.SMEM)] + whole_specs(4),
        out_specs=whole_specs(2),
        compiler_params=pltpu.CompilerParams(vmem_limit_bytes=8 * MIB),
        cost_estimate=pl.CostEstimate(flops=0, bytes_accessed=MIB, transcendentals=0),
        name="energies",
    )(place, occ_index, vir_index, occ_table, vir_table)


def outer_kernel(slots, place, rows_energy, cols_energy, *refs):
    own, other, columns = refs[:slots], refs[slots : 2 * slots], refs[2 * slots : 3 * slots]
    out_ref, high_ref, low_ref = refs[3 * slots :]
    step, steps = pl.program_id(0), pl.num_programs(0)
    depth, wide = columns[0].shape
    tall = out_ref.shape[0]

    @pl.when(step == 0)
    def _():
        for slot in range(slots):
            high, low = split(columns[slot][...])
            high_ref[pl.ds(slot * depth, depth), :] = high
            low_ref[pl.ds(slot * depth, depth), :] = low

    def finish(left, number):
        left = left.T
        high, low = split(left)
        total = jnp.dot(low, high_ref[...], preferred_element_type=jnp.float32)
        total += jnp.dot(high, low_ref[...], preferred_element_type=jnp.float32)
        total += jnp.dot(high, high_ref[...], preferred_element_type=jnp.float32)
        at = pl.ds(pl.multiple_of(number * tall, tall), tall)
        row = jnp.broadcast_to(rows_energy[:, at], (128, tall)).T
        denominator = jnp.concatenate([row] * (wide // 128), axis=1) + cols_energy[...]
        out_ref[...] = -total / denominator

    per_half = steps // 2
    inner = step % per_half
    here = pl.ds(pl.multiple_of(inner * tall, tall), tall)
    core = place[0]

    @pl.when(step < per_half)
    def _():
        finish(jnp.concatenate([ref[:, here] for ref in own], axis=0), core * per_half + inner)

    @pl.when(step >= per_half)
    def _():
        half = depth // 2
        parts = []
        for ref in other:
            parts += [ref[half:, here], ref[:half, here]]
        finish(jnp.concatenate(parts, axis=0), (1 - core) * per_half + inner)


def outer(core, rows_energy, cols_energy, own, other, columns):
    slots = len(own)
    depth, wide = columns[0].shape
    half = own[0].shape[1]
    tall = min(256, half)
    per_half = half // tall

    def place_of(step, place):
        number = jnp.where(step < per_half, place[0], 1 - place[0]) * per_half + step % per_half
        return number, 0

    arrays = [*own, *other, *columns]
    out = shape_of((2 * half, wide))
    parts = pltpu.VMEM((slots * depth, wide), jnp.bfloat16)
    return pl.pallas_call(
        functools.partial(outer_kernel, slots),
        out_shape=out,
        grid_spec=pltpu.PrefetchScalarGridSpec(
            num_scalar_prefetch=1,
            grid=(2 * per_half,),
            in_specs=whole_specs(2 + len(arrays)),
            out_specs=pl.BlockSpec((tall, wide), place_of),
            scratch_shapes=[parts, parts],
        ),
        compiler_params=pltpu.CompilerParams(
            vmem_limit_bytes=sum(a.size * 4 for a in arrays) + 10 * tall * wide * 4 + 8 * MIB
        ),
        cost_estimate=pl.CostEstimate(
            flops=6 * out.size * slots * depth, bytes_accessed=out.size * 4, transcendentals=0
        ),
        name="outer",
    )(core.reshape(1), rows_energy, cols_energy, *arrays)


def local(rows, cols, amplitudes, factors, occ_index, vir_index, occ_energy, vir_energy):
    cores = cols // rows
    chips = [(z, j, s) for z in range(rows) for j in range(rows) for s in range(cores)]

    def number(z, j, s):
        return z * cols + j * cores + s

    def move(x, to):
        return lax.ppermute(x, AXES, [(number(*at), number(*to(*at))) for at in chips])

    def swap(x):
        return move(x, lambda z, j, s: (z, j, 1 - s))

    def transposed(x, t):
        return move(x, lambda z, j, s: (j ^ z ^ t, z, s))

    def across(x, t):
        return move(x, lambda z, j, s: (z, z ^ j ^ t, s))

    slots = range(rows)
    col_index = lax.axis_index("col")
    row_index = lax.axis_index("row")
    core = col_index % cores
    tall, wide = amplitudes.shape
    half = tall // cores
    pieces = factors.T

    received = [transposed(pieces, t) for t in slots]
    for_sibling = lax.dynamic_slice_in_dim(amplitudes, (1 - core) * half, half, 0)
    high, low = prepare(core, amplitudes, swap(for_sibling))
    place = jnp.stack([row_index, col_index]).astype(jnp.int32)
    rows_energy, cols_energy = pair_energies(
        place, occ_index, vir_index, occ_energy, vir_energy, tall, wide
    )
    both = jnp.concatenate([pieces, swap(pieces)], axis=0)
    total = lax.dynamic_slice_in_dim(both, core * half, half, 1)
    for t in slots:
        partial = contract(received[t], swap(received[t]), high, low)
        total = total + across(partial, t)
    columns = [transposed(total, t) for t in slots]
    own = [across(total, t) for t in slots]
    other = [swap(x) for x in own]
    return outer(core, rows_energy, cols_energy, own, other, columns)


def solution(mesh):
    rows, cols = mesh.shape["row"], mesh.shape["col"]
    return jax.shard_map(
        functools.partial(local, rows, cols),
        mesh=mesh,
        in_specs=(P("row", "col"), P("row", "col"), P(), P(), P(), P()),
        out_specs=P("row", "col"),
        check_vma=False,
    )
```

time: 124 us -> 80.4 us (0.65)
  waiting for transfers between devices: 71.6 us -> 13.8 us
  starting transfers between devices: 9.15 us -> 56.7 us
  blocking collectives: 13.4 us -> 0 us
  between operations: 13.2 us -> 0.37 us
  matrix products: 8.69 us -> 0 us
  Pallas kernels: 0 us -> 6.96 us
  local copies, waits for them, and re-layouts: 4.57 us -> 1.48 us
  other arithmetic: 2.08 us -> 0.14 us
    ppermute x0 -> x26, starting transfers between devices: none -> 56.7 us  [move(): lax.ppermute(x, AXES, [(number(*at), number(*to(*at))) for at in chips])]
    all_gather x2 -> x0, waiting for transfers between devices: 45.4 us -> none  [the longest x1 27 us: local(): column_piece = lax.all_gather(factors, 'col', axis=1, tiled=True)]
    reduce_scatter x1 -> x0, waiting for transfers between devices: 19.4 us -> none  [local(): lax.psum_scatter(partial_sum, 'row', scatter_dimension=1, tiled=True)]
    ppermute x0 -> x26, waiting for transfers between devices: none -> 13.8 us  [move(): lax.ppermute(x, AXES, [(number(*at), number(*to(*at))) for at in chips])]
    all_gather x1 -> x0, blocking collectives: 13.4 us -> none  [local(): wide_col = lax.all_gather(column_share, 'row', axis=1, tiled=True)]
    all_to_all x1 -> x0, starting transfers between devices: 9.11 us -> none  [local(): lax.all_to_all(split_block, 'col', split_axis=0, concat_axis=0, tiled=True)]
    dot_general x2 -> x0, matrix products: 8.69 us -> none  [the longest x1 4.54 us: local(): lax.dot_general(wide_row, wide_col, (((1,), (1,)), ((), ())), precision=l...]
    pallas_call x0 -> x7, Pallas kernels: none -> 6.96 us  [the longest x1 3.03 us: outer(): pl.pallas_call(functools.partial(outer_kernel, slots), out_shape=out, gri...]
  transfers between devices with their start and end apart: 4 -> 26, of which waited for: 4 -> 5; matrix products, arithmetic and copies ran while one was open for 4% -> 0% of each run, Pallas kernels for 0% -> 5%
where the time goes in v1:
time: 80.4 us; the launch traced here: 79.4 us
  starting transfers between devices  56.7 us (71%)
  waiting for transfers between devices  13.8 us (17%)
  Pallas kernels  6.96 us (9%)
  local copies, waits for them, and re-layouts  1.48 us (2%)
    ppermute x26, starting transfers between devices, move(): lax.ppermute(x, AXES, [(number(*at), number(*to(*at))) for at in chips])  56.7 us
    ppermute x26, waiting for transfers between devices, move(): lax.ppermute(x, AXES, [(number(*at), number(*to(*at))) for at in chips])  13.8 us
    pallas_call x1, Pallas kernels, outer(): pl.pallas_call(functools.partial(outer_kernel, slots), out_shape=out, gri...  3.03 us
    pallas_call x4, Pallas kernels, contract(): pl.pallas_call(contract_kernel, out_shape=out, in_specs=whole_specs(4), o...  1.79 us
  transfers between devices with their start and end apart: 26, of which 5 were waited for; matrix products, arithmetic and copies ran while one was open for 0% of the time, Pallas kernels for 5%

profile of v1, /device:TPU:5, one launch (start us, length us, event | category | flops | bytes accessed | tf_op | source)
XLA Modules:
  0.0 79.4 jit_solution(9971262647816751699)
XLA Ops:
  0.0 1.4 %constant_dynamic-slice_fusion = f32[512,512]{1,0:T(8,128)S(1)} fusion(f32[1024,512]{1,0:T(8,128)} %own_ref.1, s32[]{:T(128)S(6)} %select_n.15), kind=kLoop, calls=%fused_computation.7 | loop fusion | bytes 2097156 | tf_op jit(solution)/shard_map/dynamic_slice | solution.py:233
  1.4 0.7 collective-permute-start.3
  2.2 4.2 %collective-permute-start.1 = (f32[32,1024]{1,0:T(8,128)}, f32[32,1024]{1,0:T(8,128)S(1)}, u32[]{:S(2)}, u32[]{:S(2)}) collective-permute-start(f32[32,1024]{1,0:T(8,128)} %bitcast.12), channel_id=1, source_target_pairs={{0,0},{1,1},{2,8},{3,9},{4,16},{5,17},{6,24},{7,25},{8,10},{9,11},... | collective-permute-start | bytes 393224 | tf_op jit(solution)/shard_map/ppermute | solution.py:213
  6.3 5.1 %collective-permute-start.5 = (f32[32,1024]{1,0:T(8,128)}, f32[32,1024]{1,0:T(8,128)S(1)}, u32[]{:S(2)}, u32[]{:S(2)}) collective-permute-start(f32[32,1024]{1,0:T(8,128)} %bitcast.13), channel_id=1, source_target_pairs={{0,8},{1,9},{2,0},{3,1},{4,24},{5,25},{6,16},{7,17},{8,2},{9,3},{1... | collective-permute-start | bytes 393224 | tf_op jit(solution)/shard_map/ppermute | solution.py:213
  11.4 1.9 %collective-permute-start.8 = (f32[32,1024]{1,0:T(8,128)}, f32[32,1024]{1,0:T(8,128)S(1)}, u32[]{:S(2)}, u32[]{:S(2)}) collective-permute-start(f32[32,1024]{1,0:T(8,128)} %bitcast.14), channel_id=1, source_target_pairs={{0,16},{1,17},{2,24},{3,25},{4,0},{5,1},{6,8},{7,9},{8,26},{9,27},... | collective-permute-start | bytes 393224 | tf_op jit(solution)/shard_map/ppermute | solution.py:213
  13.4 2.2 %collective-permute-start.11 = (f32[32,1024]{1,0:T(8,128)}, f32[32,1024]{1,0:T(8,128)S(1)}, u32[]{:S(2)}, u32[]{:S(2)}) collective-permute-start(f32[32,1024]{1,0:T(8,128)} %bitcast.15), channel_id=1, source_target_pairs={{0,24},{1,25},{2,16},{3,17},{4,8},{5,9},{6,0},{7,1},{8,18},{9,19},... | collective-permute-start | bytes 393224 | tf_op jit(solution)/shard_map/ppermute | solution.py:213
  15.6 0.0 collective-permute-done.1.own_ref
  15.6 1.1 %collective-permute-start.2 = (f32[32,1024]{1,0:T(8,128)S(1)}, f32[32,1024]{1,0:T(8,128)S(1)}, u32[]{:S(2)}, u32[]{:S(2)}) collective-permute-start(f32[32,1024]{1,0:T(8,128)S(1)} %collective-permute-done.1.own_ref), channel_id=1, source_target_pairs={{0,1},{1,0},{2,3},{3,2},{4,5},{5,4},{6,7},{7,6},{8,9},{9,8},{10,11... | collective-permute-start | bytes 393224 | tf_op jit(solution)/shard_map/ppermute | solution.py:213
  16.7 3.0 %collective-permute-done.5.own_ref = f32[32,1024]{1,0:T(8,128)S(1)} collective-permute-done((f32[32,1024]{1,0:T(8,128)}, f32[32,1024]{1,0:T(8,128)S(1)}, u32[]{:S(2)}, u32[]{:S(2)}) %collective-permute-start.5) | collective-permute-done | bytes 131104 | tf_op jit(solution)/shard_map/ppermute | solution.py:213
  19.8 1.0 %collective-permute-start.6 = (f32[32,1024]{1,0:T(8,128)S(1)}, f32[32,1024]{1,0:T(8,128)S(1)}, u32[]{:S(2)}, u32[]{:S(2)}) collective-permute-start(f32[32,1024]{1,0:T(8,128)S(1)} %collective-permute-done.5.own_ref), channel_id=1, source_target_pairs={{0,1},{1,0},{2,3},{3,2},{4,5},{5,4},{6,7},{7,6},{8,9},{9,8},{10,11... | collective-permute-start | bytes 393224 | tf_op jit(solution)/shard_map/ppermute | solution.py:213
  20.7 5.5 %collective-permute-done.8.own_ref = f32[32,1024]{1,0:T(8,128)S(1)} collective-permute-done((f32[32,1024]{1,0:T(8,128)}, f32[32,1024]{1,0:T(8,128)S(1)}, u32[]{:S(2)}, u32[]{:S(2)}) %collective-permute-start.8) | collective-permute-done | bytes 131104 | tf_op jit(solution)/shard_map/ppermute | solution.py:213
  26.3 0.6 collective-permute-start.9
  26.9 2.2 %collective-permute-done.11.own_ref = f32[32,1024]{1,0:T(8,128)S(1)} collective-permute-done((f32[32,1024]{1,0:T(8,128)}, f32[32,1024]{1,0:T(8,128)S(1)}, u32[]{:S(2)}, u32[]{:S(2)}) %collective-permute-start.11) | collective-permute-done | bytes 131104 | tf_op jit(solution)/shard_map/ppermute | solution.py:213
  29.1 0.5 collective-permute-start.12
  29.6 0.0 collective-permute-done.3.sibling_ref
  29.6 0.0 collective-permute-start
  29.6 0.6 prepare.1
  30.2 0.0 collective-permute-done.2.sibling_ref
  30.2 0.4 contract.4
  30.7 0.7 collective-permute-start.4
  31.4 0.0 collective-permute-done.6.sibling_ref
  31.4 0.5 contract.5
  31.8 0.0 copy-start.4
  31.8 2.1 %collective-permute-start.7 = (f32[64,512]{1,0:T(8,128)S(1)}, f32[64,512]{1,0:T(8,128)S(1)}, u32[]{:S(2)}, u32[]{:S(2)}) collective-permute-start(f32[64,512]{1,0:T(8,128)S(1)} %contract.5), channel_id=1, source_target_pairs={{0,2},{1,3},{2,0},{3,1},{4,6},{5,7},{6,4},{7,5},{8,8},{9,9},{10,10... | collective-permute-start | bytes 393224 | tf_op jit(solution)/shard_map/ppermute | solution.py:213
  33.9 0.0 collective-permute-done.9.sibling_ref
  33.9 0.5 contract.6
  34.4 0.0 copy-start.5
  34.4 0.0 copy-start.1
  34.4 0.0 copy-start.2
  34.4 0.0 copy-start.3
  34.4 2.1 %collective-permute-start.10 = (f32[64,512]{1,0:T(8,128)S(1)}, f32[64,512]{1,0:T(8,128)S(1)}, u32[]{:S(2)}, u32[]{:S(2)}) collective-permute-start(f32[64,512]{1,0:T(8,128)S(1)} %contract.6), channel_id=1, source_target_pairs={{0,4},{1,5},{2,6},{3,7},{4,0},{5,1},{6,2},{7,3},{8,14},{9,15},{10,... | collective-permute-start | bytes 393224 | tf_op jit(solution)/shard_map/ppermute | solution.py:213
  36.5 0.0 collective-permute-done.12.sibling_ref
  36.5 0.4 contract.7
  36.9 4.5 %collective-permute-start.13 = (f32[64,512]{1,0:T(8,128)S(1)}, f32[64,512]{1,0:T(8,128)S(1)}, u32[]{:S(2)}, u32[]{:S(2)}) collective-permute-start(f32[64,512]{1,0:T(8,128)S(1)} %contract.7), channel_id=1, source_target_pairs={{0,6},{1,7},{2,4},{3,5},{4,2},{5,3},{6,0},{7,1},{8,12},{9,13},{10,... | collective-permute-start | bytes 393224 | tf_op jit(solution)/shard_map/ppermute | solution.py:213
  41.5 0.0 collective-permute-done
  41.5 0.0 collective-permute-done.4
  41.5 0.0 collective-permute-done.7
  41.5 0.0 collective-permute-done.10
  41.5 2.7 %collective-permute-done.13 = f32[64,512]{1,0:T(8,128)S(1)} collective-permute-done((f32[64,512]{1,0:T(8,128)S(1)}, f32[64,512]{1,0:T(8,128)S(1)}, u32[]{:S(2)}, u32[]{:S(2)}) %collective-permute-start.13) | collective-permute-done | bytes 131104 | tf_op jit(solution)/shard_map/ppermute | solution.py:213
  44.2 0.1 fusion.4
  44.3 0.7 collective-permute-start.14
  45.0 3.1 %collective-permute-start.15 = (f32[64,512]{1,0:T(8,128)S(1)}, f32[64,512]{1,0:T(8,128)S(1)}, u32[]{:S(2)}, u32[]{:S(2)}) collective-permute-start(f32[64,512]{1,0:T(8,128)S(1)} %fusion.4), channel_id=1, source_target_pairs={{0,2},{1,3},{2,0},{3,1},{4,6},{5,7},{6,4},{7,5},{8,8},{9,9},{10,10... | collective-permute-start | bytes 393224 | tf_op jit(solution)/shard_map/ppermute | solution.py:213
  48.1 2.9 %collective-permute-start.16 = (f32[64,512]{1,0:T(8,128)S(1)}, f32[64,512]{1,0:T(8,128)S(1)}, u32[]{:S(2)}, u32[]{:S(2)}) collective-permute-start(f32[64,512]{1,0:T(8,128)S(1)} %fusion.4), channel_id=1, source_target_pairs={{0,4},{1,5},{2,6},{3,7},{4,0},{5,1},{6,2},{7,3},{8,14},{9,15},{10,... | collective-permute-start | bytes 393224 | tf_op jit(solution)/shard_map/ppermute | solution.py:213
  51.0 2.4 %collective-permute-start.17 = (f32[64,512]{1,0:T(8,128)S(1)}, f32[64,512]{1,0:T(8,128)S(1)}, u32[]{:S(2)}, u32[]{:S(2)}) collective-permute-start(f32[64,512]{1,0:T(8,128)S(1)} %fusion.4), channel_id=1, source_target_pairs={{0,6},{1,7},{2,4},{3,5},{4,2},{5,3},{6,0},{7,1},{8,12},{9,13},{10,... | collective-permute-start | bytes 393224 | tf_op jit(solution)/shard_map/ppermute | solution.py:213
  53.4 1.9 %collective-permute-start.22 = (f32[64,512]{1,0:T(8,128)S(1)}, f32[64,512]{1,0:T(8,128)S(1)}, u32[]{:S(2)}, u32[]{:S(2)}) collective-permute-start(f32[64,512]{1,0:T(8,128)S(1)} %fusion.4), channel_id=1, source_target_pairs={{0,0},{1,1},{2,8},{3,9},{4,16},{5,17},{6,24},{7,25},{8,10},{9,11},... | collective-permute-start | bytes 393224 | tf_op jit(solution)/shard_map/ppermute | solution.py:213
  55.3 0.0 collective-permute-done.14.refs_0_
  55.3 1.9 %collective-permute-start.23 = (f32[64,512]{1,0:T(8,128)S(1)}, f32[64,512]{1,0:T(8,128)S(1)}, u32[]{:S(2)}, u32[]{:S(2)}) collective-permute-start(f32[64,512]{1,0:T(8,128)S(1)} %fusion.4), channel_id=1, source_target_pairs={{0,8},{1,9},{2,0},{3,1},{4,24},{5,25},{6,16},{7,17},{8,2},{9,3},{1... | collective-permute-start | bytes 393224 | tf_op jit(solution)/shard_map/ppermute | solution.py:213
  57.3 0.0 collective-permute-done.15.refs_1_
  57.3 4.9 %collective-permute-start.24 = (f32[64,512]{1,0:T(8,128)S(1)}, f32[64,512]{1,0:T(8,128)S(1)}, u32[]{:S(2)}, u32[]{:S(2)}) collective-permute-start(f32[64,512]{1,0:T(8,128)S(1)} %fusion.4), channel_id=1, source_target_pairs={{0,16},{1,17},{2,24},{3,25},{4,0},{5,1},{6,8},{7,9},{8,26},{9,27},... | collective-permute-start | bytes 393224 | tf_op jit(solution)/shard_map/ppermute | solution.py:213
  62.2 0.0 collective-permute-done.16.refs_2_
  62.2 4.5 %collective-permute-start.25 = (f32[64,512]{1,0:T(8,128)S(1)}, f32[64,512]{1,0:T(8,128)S(1)}, u32[]{:S(2)}, u32[]{:S(2)}) collective-permute-start(f32[64,512]{1,0:T(8,128)S(1)} %fusion.4), channel_id=1, source_target_pairs={{0,24},{1,25},{2,16},{3,17},{4,8},{5,9},{6,0},{7,1},{8,18},{9,19},... | collective-permute-start | bytes 393224 | tf_op jit(solution)/shard_map/ppermute | solution.py:213
  66.7 0.0 collective-permute-done.17.refs_3_
  66.7 3.7 %collective-permute-start.18 = (f32[64,512]{1,0:T(8,128)S(1)}, f32[64,512]{1,0:T(8,128)S(1)}, u32[]{:S(2)}, u32[]{:S(2)}) collective-permute-start(f32[64,512]{1,0:T(8,128)S(1)} %collective-permute-done.14.refs_0_), channel_id=1, source_target_pairs={{0,1},{1,0},{2,3},{3,2},{4,5},{5,4},{6,7},{7,6},{8,9},{9,8},{10,11... | collective-permute-start | bytes 393224 | tf_op jit(solution)/shard_map/ppermute | solution.py:213
  70.4 0.1 collective-permute-start.19
  70.5 0.2 collective-permute-done.23.refs_9_
  70.7 1.2 %collective-permute-start.20 = (f32[64,512]{1,0:T(8,128)S(1)}, f32[64,512]{1,0:T(8,128)S(1)}, u32[]{:S(2)}, u32[]{:S(2)}) collective-permute-start(f32[64,512]{1,0:T(8,128)S(1)} %collective-permute-done.16.refs_2_), channel_id=1, source_target_pairs={{0,1},{1,0},{2,3},{3,2},{4,5},{5,4},{6,7},{7,6},{8,9},{9,8},{10,11... | collective-permute-start | bytes 393224 | tf_op jit(solution)/shard_map/ppermute | solution.py:213
  71.9 2.8 %collective-permute-start.21 = (f32[64,512]{1,0:T(8,128)S(1)}, f32[64,512]{1,0:T(8,128)S(1)}, u32[]{:S(2)}, u32[]{:S(2)}) collective-permute-start(f32[64,512]{1,0:T(8,128)S(1)} %collective-permute-done.17.refs_3_), channel_id=1, source_target_pairs={{0,1},{1,0},{2,3},{3,2},{4,5},{5,4},{6,7},{7,6},{8,9},{9,8},{10,11... | collective-permute-start | bytes 393224 | tf_op jit(solution)/shard_map/ppermute | solution.py:213
  74.8 0.1 pad_add_fusion.place
  74.8 1.5 %energies.1 = (f32[1,1024]{1,0:T(1,128)S(1)}, f32[1,512]{1,0:T(1,128)S(1)}) custom-call(s32[2]{0:T(128)S(1)} %pad_add_fusion.place, s32[1,4096]{1,0:T(1,128)S(1)} %bitcast.9, s32[1,4096]{1,0:T(1,128)S(1)} %bitcast.10, f32[1,128]{1,0:T(1,128)S(1)} %pad_bitcast_fusion.occ_table, f32[16,128]{1,0:T(8,128)S(1)} %bitcast.11), custom_call_target="tpu_custom_call" | custom-call | bytes 1048576 | tf_op jit(solution)/shard_map/energies/pallas_call | solution.py:117
  76.4 0.0 collective-permute-done.25.refs_11_
  76.4 0.0 collective-permute-done.18.refs_4_
  76.4 0.0 collective-permute-done.20.refs_6_
  76.4 0.0 collective-permute-done.21.refs_7_
  76.4 3.0 %outer.1 = f32[1024,512]{1,0:T(8,128)} custom-call(s32[1]{0:T(128)} %bitcast.place, f32[1,1024]{1,0:T(1,128)S(1)} %get-tuple-element.9.rows_energy, f32[1,512]{1,0:T(1,128)S(1)} %get-tuple-element.10.cols_energy, f32[64,512]{1,0:T(8,128)S(1)} %collective-permute-done.14.refs_0_, f32[64,512]{1,0:T(8,128)S(1)} %collective-permute-done.15.refs_1_, ...), custom_call_target="tpu_custom_call" | custom-call | flops 805306368 | bytes 2097152 | tf_op jit(solution)/shard_map/outer/pallas_call | solution.py:185
  (11 shorter events, 0.0 us)
Async XLA Ops:
  0.0 29.6 %copy-start = (f32[1024,512]{1,0:T(8,128)S(1)}, f32[1024,512]{1,0:T(8,128)}, u32[]{:S(2)}) copy-start(f32[1024,512]{1,0:T(8,128)} %own_ref.1) | copy-start | bytes 6291460
  1.4 28.1 %collective-permute-start.3 = (f32[512,512]{1,0:T(8,128)S(1)}, f32[512,512]{1,0:T(8,128)S(1)}, u32[]{:S(2)}, u32[]{:S(2)}) collective-permute-start(f32[512,512]{1,0:T(8,128)S(1)} %constant_dynamic-slice_fusion), channel_id=1, source_target_pairs={{0,1},{1,0},{2,3},{3,2},{4,5},{5,4},{6,7},{7,6},{8,9},{9,8},{10,11... | collective-permute-start | bytes 3145736 | tf_op jit(solution)/shard_map/ppermute | solution.py:213
  2.2 13.4 %collective-permute-start.1 = (f32[32,1024]{1,0:T(8,128)}, f32[32,1024]{1,0:T(8,128)S(1)}, u32[]{:S(2)}, u32[]{:S(2)}) collective-permute-start(f32[32,1024]{1,0:T(8,128)} %bitcast.12), channel_id=1, source_target_pairs={{0,0},{1,1},{2,8},{3,9},{4,16},{5,17},{6,24},{7,25},{8,10},{9,11},... | collective-permute-start | bytes 393224 | tf_op jit(solution)/shard_map/ppermute | solution.py:213
  6.3 13.4 %collective-permute-start.5 = (f32[32,1024]{1,0:T(8,128)}, f32[32,1024]{1,0:T(8,128)S(1)}, u32[]{:S(2)}, u32[]{:S(2)}) collective-permute-start(f32[32,1024]{1,0:T(8,128)} %bitcast.13), channel_id=1, source_target_pairs={{0,8},{1,9},{2,0},{3,1},{4,24},{5,25},{6,16},{7,17},{8,2},{9,3},{1... | collective-permute-start | bytes 393224 | tf_op jit(solution)/shard_map/ppermute | solution.py:213
  11.4 14.8 %collective-permute-start.8 = (f32[32,1024]{1,0:T(8,128)}, f32[32,1024]{1,0:T(8,128)S(1)}, u32[]{:S(2)}, u32[]{:S(2)}) collective-permute-start(f32[32,1024]{1,0:T(8,128)} %bitcast.14), channel_id=1, source_target_pairs={{0,16},{1,17},{2,24},{3,25},{4,0},{5,1},{6,8},{7,9},{8,26},{9,27},... | collective-permute-start | bytes 393224 | tf_op jit(solution)/shard_map/ppermute | solution.py:213
  13.4 15.7 %collective-permute-start.11 = (f32[32,1024]{1,0:T(8,128)}, f32[32,1024]{1,0:T(8,128)S(1)}, u32[]{:S(2)}, u32[]{:S(2)}) collective-permute-start(f32[32,1024]{1,0:T(8,128)} %bitcast.15), channel_id=1, source_target_pairs={{0,24},{1,25},{2,16},{3,17},{4,8},{5,9},{6,0},{7,1},{8,18},{9,19},... | collective-permute-start | bytes 393224 | tf_op jit(solution)/shard_map/ppermute | solution.py:213
  15.6 14.6 %collective-permute-start.2 = (f32[32,1024]{1,0:T(8,128)S(1)}, f32[32,1024]{1,0:T(8,128)S(1)}, u32[]{:S(2)}, u32[]{:S(2)}) collective-permute-start(f32[32,1024]{1,0:T(8,128)S(1)} %collective-permute-done.1.own_ref), channel_id=1, source_target_pairs={{0,1},{1,0},{2,3},{3,2},{4,5},{5,4},{6,7},{7,6},{8,9},{9,8},{10,11... | collective-permute-start | bytes 393224 | tf_op jit(solution)/shard_map/ppermute | solution.py:213
  19.8 11.6 %collective-permute-start.6 = (f32[32,1024]{1,0:T(8,128)S(1)}, f32[32,1024]{1,0:T(8,128)S(1)}, u32[]{:S(2)}, u32[]{:S(2)}) collective-permute-start(f32[32,1024]{1,0:T(8,128)S(1)} %collective-permute-done.5.own_ref), channel_id=1, source_target_pairs={{0,1},{1,0},{2,3},{3,2},{4,5},{5,4},{6,7},{7,6},{8,9},{9,8},{10,11... | collective-permute-start | bytes 393224 | tf_op jit(solution)/shard_map/ppermute | solution.py:213
  26.3 7.6 %collective-permute-start.9 = (f32[32,1024]{1,0:T(8,128)S(1)}, f32[32,1024]{1,0:T(8,128)S(1)}, u32[]{:S(2)}, u32[]{:S(2)}) collective-permute-start(f32[32,1024]{1,0:T(8,128)S(1)} %collective-permute-done.8.own_ref), channel_id=1, source_target_pairs={{0,1},{1,0},{2,3},{3,2},{4,5},{5,4},{6,7},{7,6},{8,9},{9,8},{10,11... | collective-permute-start | bytes 393224 | tf_op jit(solution)/shard_map/ppermute | solution.py:213
  29.1 7.4 %collective-permute-start.12 = (f32[32,1024]{1,0:T(8,128)S(1)}, f32[32,1024]{1,0:T(8,128)S(1)}, u32[]{:S(2)}, u32[]{:S(2)}) collective-permute-start(f32[32,1024]{1,0:T(8,128)S(1)} %collective-permute-done.11.own_ref), channel_id=1, source_target_pairs={{0,1},{1,0},{2,3},{3,2},{4,5},{5,4},{6,7},{7,6},{8,9},{9,8},{10,11... | collective-permute-start | bytes 393224 | tf_op jit(solution)/shard_map/ppermute | solution.py:213
  29.6 11.9 %collective-permute-start = (f32[32,1024]{1,0:T(8,128)}, f32[32,1024]{1,0:T(8,128)S(1)}, u32[]{:S(2)}, u32[]{:S(2)}) collective-permute-start(f32[32,1024]{1,0:T(8,128)} %bitcast.16), channel_id=1, source_target_pairs={{0,1},{1,0},{2,3},{3,2},{4,5},{5,4},{6,7},{7,6},{8,9},{9,8},{10,11... | collective-permute-start | bytes 393224 | tf_op jit(solution)/shard_map/ppermute | solution.py:213
  30.7 10.8 %collective-permute-start.4 = (f32[64,512]{1,0:T(8,128)S(1)}, f32[64,512]{1,0:T(8,128)S(1)}, u32[]{:S(2)}, u32[]{:S(2)}) collective-permute-start(f32[64,512]{1,0:T(8,128)S(1)} %contract.4), channel_id=1, source_target_pairs={{0,0},{1,1},{2,2},{3,3},{4,4},{5,5},{6,6},{7,7},{8,10},{9,11},{10,... | collective-permute-start | bytes 393224 | tf_op jit(solution)/shard_map/ppermute | solution.py:213
  31.8 12.4 %copy-start.4 = (f32[1024,32]{0,1:T(8,128)S(1)}, f32[1024,32]{0,1:T(8,128)}, u32[]{:S(2)}) copy-start(f32[1024,32]{0,1:T(8,128)} %param.7) | copy-start | bytes 393220
  31.8 9.7 %collective-permute-start.7 = (f32[64,512]{1,0:T(8,128)S(1)}, f32[64,512]{1,0:T(8,128)S(1)}, u32[]{:S(2)}, u32[]{:S(2)}) collective-permute-start(f32[64,512]{1,0:T(8,128)S(1)} %contract.5), channel_id=1, source_target_pairs={{0,2},{1,3},{2,0},{3,1},{4,6},{5,7},{6,4},{7,5},{8,8},{9,9},{10,10... | collective-permute-start | bytes 393224 | tf_op jit(solution)/shard_map/ppermute | solution.py:213
  34.4 40.4 %copy-start.5 = (f32[64]{0:T(128)S(1)}, f32[64]{0:T(128)}, u32[]{:S(2)}) copy-start(f32[64]{0:T(128)} %param.10) | copy-start | bytes 772
  34.4 40.5 %copy-start.1 = (s32[4096]{0:T(1024)S(1)}, s32[4096]{0:T(1024)}, u32[]{:S(2)}) copy-start(s32[4096]{0:T(1024)} %param.8) | copy-start | bytes 49156
  34.4 40.4 %copy-start.2 = (s32[4096]{0:T(1024)S(1)}, s32[4096]{0:T(1024)}, u32[]{:S(2)}) copy-start(s32[4096]{0:T(1024)} %param.9) | copy-start | bytes 49156
  34.4 40.4 %copy-start.3 = (f32[2048]{0:T(1024)S(1)}, f32[2048]{0:T(1024)}, u32[]{:S(2)}) copy-start(f32[2048]{0:T(1024)} %param.11) | copy-start | bytes 24580
  34.4 7.1 %collective-permute-start.10 = (f32[64,512]{1,0:T(8,128)S(1)}, f32[64,512]{1,0:T(8,128)S(1)}, u32[]{:S(2)}, u32[]{:S(2)}) collective-permute-start(f32[64,512]{1,0:T(8,128)S(1)} %contract.6), channel_id=1, source_target_pairs={{0,4},{1,5},{2,6},{3,7},{4,0},{5,1},{6,2},{7,3},{8,14},{9,15},{10,... | collective-permute-start | bytes 393224 | tf_op jit(solution)/shard_map/ppermute | solution.py:213
  36.9 7.3 %collective-permute-start.13 = (f32[64,512]{1,0:T(8,128)S(1)}, f32[64,512]{1,0:T(8,128)S(1)}, u32[]{:S(2)}, u32[]{:S(2)}) collective-permute-start(f32[64,512]{1,0:T(8,128)S(1)} %contract.7), channel_id=1, source_target_pairs={{0,6},{1,7},{2,4},{3,5},{4,2},{5,3},{6,0},{7,1},{8,12},{9,13},{10,... | collective-permute-start | bytes 393224 | tf_op jit(solution)/shard_map/ppermute | solution.py:213
  44.3 11.0 %collective-permute-start.14 = (f32[64,512]{1,0:T(8,128)S(1)}, f32[64,512]{1,0:T(8,128)S(1)}, u32[]{:S(2)}, u32[]{:S(2)}) collective-permute-start(f32[64,512]{1,0:T(8,128)S(1)} %fusion.4), channel_id=1, source_target_pairs={{0,0},{1,1},{2,2},{3,3},{4,4},{5,5},{6,6},{7,7},{8,10},{9,11},{10,... | collective-permute-start | bytes 393224 | tf_op jit(solution)/shard_map/ppermute | solution.py:213
  45.0 12.3 %collective-permute-start.15 = (f32[64,512]{1,0:T(8,128)S(1)}, f32[64,512]{1,0:T(8,128)S(1)}, u32[]{:S(2)}, u32[]{:S(2)}) collective-permute-start(f32[64,512]{1,0:T(8,128)S(1)} %fusion.4), channel_id=1, source_target_pairs={{0,2},{1,3},{2,0},{3,1},{4,6},{5,7},{6,4},{7,5},{8,8},{9,9},{10,10... | collective-permute-start | bytes 393224 | tf_op jit(solution)/shard_map/ppermute | solution.py:213
  48.1 14.1 %collective-permute-start.16 = (f32[64,512]{1,0:T(8,128)S(1)}, f32[64,512]{1,0:T(8,128)S(1)}, u32[]{:S(2)}, u32[]{:S(2)}) collective-permute-start(f32[64,512]{1,0:T(8,128)S(1)} %fusion.4), channel_id=1, source_target_pairs={{0,4},{1,5},{2,6},{3,7},{4,0},{5,1},{6,2},{7,3},{8,14},{9,15},{10,... | collective-permute-start | bytes 393224 | tf_op jit(solution)/shard_map/ppermute | solution.py:213
  51.0 15.7 %collective-permute-start.17 = (f32[64,512]{1,0:T(8,128)S(1)}, f32[64,512]{1,0:T(8,128)S(1)}, u32[]{:S(2)}, u32[]{:S(2)}) collective-permute-start(f32[64,512]{1,0:T(8,128)S(1)} %fusion.4), channel_id=1, source_target_pairs={{0,6},{1,7},{2,4},{3,5},{4,2},{5,3},{6,0},{7,1},{8,12},{9,13},{10,... | collective-permute-start | bytes 393224 | tf_op jit(solution)/shard_map/ppermute | solution.py:213
  53.4 17.0 %collective-permute-start.22 = (f32[64,512]{1,0:T(8,128)S(1)}, f32[64,512]{1,0:T(8,128)S(1)}, u32[]{:S(2)}, u32[]{:S(2)}) collective-permute-start(f32[64,512]{1,0:T(8,128)S(1)} %fusion.4), channel_id=1, source_target_pairs={{0,0},{1,1},{2,8},{3,9},{4,16},{5,17},{6,24},{7,25},{8,10},{9,11},... | collective-permute-start | bytes 393224 | tf_op jit(solution)/shard_map/ppermute | solution.py:213
  55.3 15.4 %collective-permute-start.23 = (f32[64,512]{1,0:T(8,128)S(1)}, f32[64,512]{1,0:T(8,128)S(1)}, u32[]{:S(2)}, u32[]{:S(2)}) collective-permute-start(f32[64,512]{1,0:T(8,128)S(1)} %fusion.4), channel_id=1, source_target_pairs={{0,8},{1,9},{2,0},{3,1},{4,24},{5,25},{6,16},{7,17},{8,2},{9,3},{1... | collective-permute-start | bytes 393224 | tf_op jit(solution)/shard_map/ppermute | solution.py:213
  57.3 14.7 %collective-permute-start.24 = (f32[64,512]{1,0:T(8,128)S(1)}, f32[64,512]{1,0:T(8,128)S(1)}, u32[]{:S(2)}, u32[]{:S(2)}) collective-permute-start(f32[64,512]{1,0:T(8,128)S(1)} %fusion.4), channel_id=1, source_target_pairs={{0,16},{1,17},{2,24},{3,25},{4,0},{5,1},{6,8},{7,9},{8,26},{9,27},... | collective-permute-start | bytes 393224 | tf_op jit(solution)/shard_map/ppermute | solution.py:213
  62.2 14.2 %collective-permute-start.25 = (f32[64,512]{1,0:T(8,128)S(1)}, f32[64,512]{1,0:T(8,128)S(1)}, u32[]{:S(2)}, u32[]{:S(2)}) collective-permute-start(f32[64,512]{1,0:T(8,128)S(1)} %fusion.4), channel_id=1, source_target_pairs={{0,24},{1,25},{2,16},{3,17},{4,8},{5,9},{6,0},{7,1},{8,18},{9,19},... | collective-permute-start | bytes 393224 | tf_op jit(solution)/shard_map/ppermute | solution.py:213
  66.7 9.6 %collective-permute-start.18 = (f32[64,512]{1,0:T(8,128)S(1)}, f32[64,512]{1,0:T(8,128)S(1)}, u32[]{:S(2)}, u32[]{:S(2)}) collective-permute-start(f32[64,512]{1,0:T(8,128)S(1)} %collective-permute-done.14.refs_0_), channel_id=1, source_target_pairs={{0,1},{1,0},{2,3},{3,2},{4,5},{5,4},{6,7},{7,6},{8,9},{9,8},{10,11... | collective-permute-start | bytes 393224 | tf_op jit(solution)/shard_map/ppermute | solution.py:213
  70.4 6.0 %collective-permute-start.19 = (f32[64,512]{1,0:T(8,128)S(1)}, f32[64,512]{1,0:T(8,128)S(1)}, u32[]{:S(2)}, u32[]{:S(2)}) collective-permute-start(f32[64,512]{1,0:T(8,128)S(1)} %collective-permute-done.15.refs_1_), channel_id=1, source_target_pairs={{0,1},{1,0},{2,3},{3,2},{4,5},{5,4},{6,7},{7,6},{8,9},{9,8},{10,11... | collective-permute-start | bytes 393224 | tf_op jit(solution)/shard_map/ppermute | solution.py:213
  70.7 5.7 %collective-permute-start.20 = (f32[64,512]{1,0:T(8,128)S(1)}, f32[64,512]{1,0:T(8,128)S(1)}, u32[]{:S(2)}, u32[]{:S(2)}) collective-permute-start(f32[64,512]{1,0:T(8,128)S(1)} %collective-permute-done.16.refs_2_), channel_id=1, source_target_pairs={{0,1},{1,0},{2,3},{3,2},{4,5},{5,4},{6,7},{7,6},{8,9},{9,8},{10,11... | collective-permute-start | bytes 393224 | tf_op jit(solution)/shard_map/ppermute | solution.py:213
  71.9 4.5 %collective-permute-start.21 = (f32[64,512]{1,0:T(8,128)S(1)}, f32[64,512]{1,0:T(8,128)S(1)}, u32[]{:S(2)}, u32[]{:S(2)}) collective-permute-start(f32[64,512]{1,0:T(8,128)S(1)} %collective-permute-done.17.refs_3_), channel_id=1, source_target_pairs={{0,1},{1,0},{2,3},{3,2},{4,5},{5,4},{6,7},{7,6},{8,9},{9,8},{10,11... | collective-permute-start | bytes 393224 | tf_op jit(solution)/shard_map/ppermute | solution.py:213

commit v2 on v1

v2 whole, which is shorter than its diff:
```python
import functools

import jax
import jax.numpy as jnp
from jax import lax
from jax.experimental import pallas as pl
from jax.experimental.pallas import tpu as pltpu
from jax.sharding import PartitionSpec as P

AXES = ("row", "col")
MIB = 1 << 20


def split(x):
    high = x.astype(jnp.bfloat16)
    low = (x - high.astype(jnp.float32)).astype(jnp.bfloat16)
    return high, low


def params(*arrays):
    held = sum(a.size * a.dtype.itemsize for a in arrays)
    return pltpu.CompilerParams(vmem_limit_bytes=2 * held + 4 * MIB)


def whole_specs(count):
    return [pl.BlockSpec(memory_space=pltpu.VMEM)] * count


def shape_of(shape, dtype=jnp.float32):
    return jax.ShapeDtypeStruct(shape, dtype)


def prepare_kernel(place, own_ref, sibling_ref, high_ref, low_ref):
    wide = own_ref.shape[1]
    core = place[0]
    for number, ref in ((core, own_ref), (1 - core, sibling_ref)):
        high, low = split(ref[...].T)
        here = pl.ds(pl.multiple_of(number * wide, wide), wide)
        high_ref[here, :] = high
        low_ref[here, :] = low


def prepare(core, own, sibling):
    tall, wide = own.shape
    out = shape_of((2 * wide, tall), jnp.bfloat16)
    return pl.pallas_call(
        prepare_kernel,
        out_shape=(out, out),
        in_specs=[pl.BlockSpec(memory_space=pltpu.SMEM)] + whole_specs(2),
        out_specs=whole_specs(2),
        compiler_params=params(own, sibling, out, out),
        cost_estimate=pl.CostEstimate(flops=0, bytes_accessed=own.size * 16, transcendentals=0),
        name="prepare",
    )(core.reshape(1), own, sibling)


def contract_kernel(factors_ref, high_ref, low_ref, out_ref):
    rows = factors_ref.shape[0]
    high, low = split(factors_ref[...])
    both = jnp.concatenate([high, low], axis=0)
    first = jnp.dot(both, high_ref[...], preferred_element_type=jnp.float32)
    second = jnp.dot(high, low_ref[...], preferred_element_type=jnp.float32)
    out_ref[...] = first[:rows] + (first[rows:] + second)


def contract(factors, high, low):
    out = shape_of((factors.shape[0], high.shape[1]))
    return pl.pallas_call(
        contract_kernel,
        out_shape=out,
        in_specs=whole_specs(3),
        out_specs=whole_specs(1)[0],
        compiler_params=params(factors, high, low, out),
        cost_estimate=pl.CostEstimate(
            flops=6 * out.size * high.shape[0], bytes_accessed=high.size * 4, transcendentals=0
        ),
        name="contract",
    )(factors, high, low)


def pick(table, index):
    rows, lanes = table.shape
    length = index.shape[1]
    at_lane = lax.broadcasted_iota(jnp.int32, (lanes, length), 0) == index % lanes
    picked = jnp.dot(
        table,
        at_lane.astype(jnp.float32),
        precision=lax.Precision.HIGHEST,
        preferred_element_type=jnp.float32,
    )
    at_row = lax.broadcasted_iota(jnp.int32, (rows, length), 0) == index // lanes
    return jnp.sum(jnp.where(at_row, picked, 0.0), axis=0, keepdims=True)


def energy_kernel(place, occ_ref, vir_ref, occ_table, vir_table, rows_ref, cols_ref):
    for number, out_ref in enumerate((rows_ref, cols_ref)):
        length = out_ref.shape[1]
        here = pl.ds(pl.multiple_of(place[number] * length, length), length)
        out_ref[...] = pick(vir_table[...], vir_ref[:, here]) - pick(occ_table[...], occ_ref[:, here])


def as_table(energies):
    lanes = 128
    padded = jnp.pad(energies, (0, -energies.shape[0] % lanes))
    return padded.reshape(-1, lanes)


def pair_energies(place, occ_index, vir_index, occ_energy, vir_energy, rows, cols):
    occ_index, vir_index = occ_index[None, :], vir_index[None, :]
    occ_table, vir_table = as_table(occ_energy), as_table(vir_energy)
    return pl.pallas_call(
        energy_kernel,
        out_shape=(shape_of((1, rows)), shape_of((1, cols))),
        in_specs=[pl.BlockSpec(memory_space=pltpu.SMEM)] + whole_specs(4),
        out_specs=whole_specs(2),
        compiler_params=pltpu.CompilerParams(vmem_limit_bytes=8 * MIB),
        cost_estimate=pl.CostEstimate(flops=0, bytes_accessed=MIB, transcendentals=0),
        name="energies",
    )(place, occ_index, vir_index, occ_table, vir_table)


def outer_kernel(slots, place, rows_energy, cols_energy, *refs):
    left, right = refs[:slots], refs[slots : 2 * slots]
    out_ref, left_ref, high_ref, low_ref = refs[2 * slots :]
    step = pl.program_id(0)
    depth = left[0].shape[0]
    tall, wide = out_ref.shape

    @pl.when(step == 0)
    def _():
        mine = pl.ds(pl.multiple_of(place[0] * wide, wide), wide)
        for slot in range(slots):
            left_ref[pl.ds(pl.multiple_of(place[1 + slot] * depth, depth), depth), :] = left[slot][...]
            high, low = split(right[slot][:, mine])
            here = pl.ds(pl.multiple_of(place[1 + slots + slot] * depth, depth), depth)
            high_ref[here, :] = high
            low_ref[here, :] = low

    here = pl.ds(pl.multiple_of(step * tall, tall), tall)
    high, low = split(left_ref[:, here].T)
    total = jnp.dot(low, high_ref[...], preferred_element_type=jnp.float32)
    total += jnp.dot(high, low_ref[...], preferred_element_type=jnp.float32)
    total += jnp.dot(high, high_ref[...], preferred_element_type=jnp.float32)
    row = jnp.broadcast_to(rows_energy[:, here], (128, tall)).T
    denominator = jnp.concatenate([row] * (wide // 128), axis=1) + cols_energy[...]
    out_ref[...] = -total / denominator


def outer(place, rows_energy, cols_energy, left, right):
    slots = len(left)
    depth, total = left[0].shape
    wide = cols_energy.shape[1]
    tall = min(256, total)
    arrays = [*left, *right]
    out = shape_of((total, wide))
    parts = pltpu.VMEM((slots * depth, wide), jnp.bfloat16)
    return pl.pallas_call(
        functools.partial(outer_kernel, slots),
        out_shape=out,
        grid_spec=pltpu.PrefetchScalarGridSpec(
            num_scalar_prefetch=1,
            grid=(total // tall,),
            in_specs=whole_specs(2 + len(arrays)),
            out_specs=pl.BlockSpec((tall, wide), lambda step, place: (step, 0)),
            scratch_shapes=[pltpu.VMEM((slots * depth, total), jnp.float32), parts, parts],
        ),
        compiler_params=pltpu.CompilerParams(
            vmem_limit_bytes=sum(a.size * 4 for a in arrays) * 2 + 10 * tall * wide * 4 + 8 * MIB
        ),
        cost_estimate=pl.CostEstimate(
            flops=6 * out.size * slots * depth, bytes_accessed=out.size * 4, transcendentals=0
        ),
        name="outer",
    )(place, rows_energy, cols_energy, *arrays)


def local(rows, cols, amplitudes, factors, occ_index, vir_index, occ_energy, vir_energy):
    cores = 2
    share = rows // cores
    chips = [(z, j, s) for z in range(rows) for j in range(rows) for s in range(cores)]

    def number(z, j, s):
        return z * cols + j * cores + s

    def move(x, to):
        return lax.ppermute(x, AXES, [(number(*at), number(*to(*at))) for at in chips])

    def swap(x):
        return move(x, lambda z, j, s: (z, j, 1 - s))

    def transposed(x, i):
        return move(x, lambda z, j, s: (j ^ z ^ (s * share + i), z, s))

    def reduced(x, i):
        return move(x, lambda z, j, s: (z, z ^ j ^ (s * share + i), s))

    def across(x, i):
        return move(x, lambda z, j, s: (z, j ^ (s * share + i), s))

    turns = range(share)
    row_index = lax.axis_index("row").astype(jnp.int32)
    col_index = lax.axis_index("col").astype(jnp.int32)
    core, chip = col_index % cores, col_index // cores
    tall, wide = amplitudes.shape

    def share_of(x):
        other = swap(x)
        return jnp.where(
            core == 0, jnp.concatenate([x, other], axis=0), jnp.concatenate([other, x], axis=0)
        )

    pieces = share_of(factors.T)
    received = [transposed(pieces, i) for i in turns]
    high, low = prepare(core, amplitudes, swap(amplitudes))
    rows_energy, cols_energy = pair_energies(
        jnp.stack([row_index, col_index]), occ_index, vir_index, occ_energy, vir_energy, tall, wide
    )
    high, low, rows_energy, cols_energy = lax.optimization_barrier(
        (high, low, rows_energy, cols_energy)
    )
    arrived = [reduced(contract(received[i], high, low), i) for i in turns]
    total = functools.reduce(jnp.add, arrived)
    dressed = pieces + (total + swap(total))
    columns = [transposed(dressed, i) for i in turns]
    own = [across(dressed, i) for i in turns]
    columns += [swap(x) for x in columns]
    own += [swap(x) for x in own]
    turn = jnp.concatenate([core * share + jnp.arange(share), (1 - core) * share + jnp.arange(share)])
    place = jnp.concatenate([core[None], chip ^ turn, row_index ^ chip ^ turn]).astype(jnp.int32)
    return outer(place, rows_energy, cols_energy, own, columns)


def solution(mesh):
    rows, cols = mesh.shape["row"], mesh.shape["col"]
    return jax.shard_map(
        functools.partial(local, rows, cols),
        mesh=mesh,
        in_specs=(P("row", "col"), P("row", "col"), P(), P(), P(), P()),
        out_specs=P("row", "col"),
        check_vma=False,
    )
```

time: 80.4 us -> 64.2 us (0.80)
  starting transfers between devices: 56.7 us -> 26.2 us
  waiting for transfers between devices: 13.8 us -> 23.7 us
  local copies, waits for them, and re-layouts: 1.48 us -> 4.38 us
  other arithmetic: 0.14 us -> 1.33 us
  Pallas kernels: 6.96 us -> 7.9 us
    ppermute x26 -> x15, starting transfers between devices: 56.7 us -> 26.2 us  [move(): lax.ppermute(x, AXES, [(number(*at), number(*to(*at))) for at in chips])]
    ppermute x26 -> x15, waiting for transfers between devices: 13.8 us -> 23.7 us  [move(): lax.ppermute(x, AXES, [(number(*at), number(*to(*at))) for at in chips])]
    unnamed x12 -> x8, local copies, waits for them, and re-layouts: 0.04 us -> 3.72 us
    dynamic_slice x1 -> x0, local copies, waits for them, and re-layouts: 1.44 us -> none  [local(): lax.dynamic_slice_in_dim(amplitudes, (1 - core) * half, half, 0)]
    select_n x0 -> x1, other arithmetic: none -> 1 us  [share_of(): jnp.where(core == 0, jnp.concatenate([x, other], axis=0), jnp.concatenate...]
    pallas_call x4 -> x2, Pallas kernels: 1.79 us -> 1.55 us  [contract(): pl.pallas_call(contract_kernel, out_shape=out, in_specs=whole_specs(3), o...]
  transfers between devices with their start and end apart: 26 -> 15, of which waited for: 5 -> 8; matrix products, arithmetic and copies ran while one was open for 0% -> 3% of each run, Pallas kernels for 5% -> 7%
where the time goes in v2:
time: 64.2 us; the launch traced here: 63.7 us
  starting transfers between devices  26.2 us (41%)
  waiting for transfers between devices  23.7 us (37%)
  Pallas kernels  7.9 us (12%)
  local copies, waits for them, and re-layouts  4.38 us (7%)
  other arithmetic  1.33 us (2%)
    ppermute x15, starting transfers between devices, move(): lax.ppermute(x, AXES, [(number(*at), number(*to(*at))) for at in chips])  26.2 us
    ppermute x15, waiting for transfers between devices, move(): lax.ppermute(x, AXES, [(number(*at), number(*to(*at))) for at in chips])  23.7 us
    unnamed x8, local copies, waits for them, and re-layouts  3.72 us
    pallas_call x1, Pallas kernels, outer(): pl.pallas_call(functools.partial(outer_kernel, slots), out_shape=out, gri...  3.55 us
    pallas_call x2, Pallas kernels, contract(): pl.pallas_call(contract_kernel, out_shape=out, in_specs=whole_specs(3), o...  1.55 us
    pallas_call x1, Pallas kernels, pair_energies(): pl.pallas_call(energy_kernel, out_shape=(shape_of((1, rows)), shape_of((1...  1.53 us
  transfers between devices with their start and end apart: 15, of which 8 were waited for; matrix products, arithmetic and copies ran while one was open for 3% of the time, Pallas kernels for 7%

profile of v2, /device:TPU:5, one launch (start us, length us, event | category | flops | bytes accessed | tf_op | source)
XLA Modules:
  0.0 63.7 jit_solution(7589249332106353604)
XLA Ops:
  0.0 0.7 %collective-permute-start = (f32[1024,512]{1,0:T(8,128)}, f32[1024,512]{1,0:T(8,128)S(1)}, u32[]{:S(2)}, u32[]{:S(2)}) collective-permute-start(f32[1024,512]{1,0:T(8,128)} %own_ref.1), channel_id=1, source_target_pairs={{0,1},{1,0},{2,3},{3,2},{4,5},{5,4},{6,7},{7,6},{8,9},{9,8},{10,11... | collective-permute-start | bytes 6291464 | tf_op jit(solution)/shard_map/ppermute | solution.py:186
  0.7 0.0 collective-permute-start.1
  0.7 4.2 %collective-permute-done.1 = f32[32,1024]{1,0:T(8,128)S(1)} collective-permute-done((f32[32,1024]{1,0:T(8,128)}, f32[32,1024]{1,0:T(8,128)S(1)}, u32[]{:S(2)}, u32[]{:S(2)}) %collective-permute-start.1) | collective-permute-done | bytes 131104 | tf_op jit(solution)/shard_map/ppermute | solution.py:186
  4.9 1.0 %maximum_select_fusion = f32[64,1024]{1,0:T(8,128)S(1)} fusion(f32[32,1024]{1,0:T(8,128)S(1)} %collective-permute-done.1, f32[32,1024]{1,0:T(8,128)} %bitcast.13, pred[]{:T(512)S(6)} %eq.5), kind=kLoop, calls=%fused_computation | loop fusion | flops 196608 | bytes 524289 | tf_op jit(solution)/shard_map/jit(_where)/select_n | solution.py:208
  5.9 1.9 %collective-permute-start.2 = (f32[64,1024]{1,0:T(8,128)S(1)}, f32[64,1024]{1,0:T(8,128)S(1)}, u32[]{:S(2)}, u32[]{:S(2)}) collective-permute-start(f32[64,1024]{1,0:T(8,128)S(1)} %maximum_select_fusion), channel_id=1, source_target_pairs={{0,0},{1,17},{2,8},{3,25},{4,16},{5,1},{6,24},{7,9},{8,10},{9,27},... | collective-permute-start | bytes 786440 | tf_op jit(solution)/shard_map/ppermute | solution.py:186
  7.8 6.4 %collective-permute-start.4 = (f32[64,1024]{1,0:T(8,128)S(1)}, f32[64,1024]{1,0:T(8,128)S(1)}, u32[]{:S(2)}, u32[]{:S(2)}) collective-permute-start(f32[64,1024]{1,0:T(8,128)S(1)} %maximum_select_fusion), channel_id=1, source_target_pairs={{0,8},{1,25},{2,0},{3,17},{4,24},{5,9},{6,16},{7,1},{8,2},{9,19},{... | collective-permute-start | bytes 786440 | tf_op jit(solution)/shard_map/ppermute | solution.py:186
  14.2 0.7 %pad_bitcast_fusion.occ_table = f32[1,128]{1,0:T(1,128)S(1)} fusion(f32[64]{0:T(128)} %param.10), kind=kLoop, calls=%fused_computation.5 | loop fusion | bytes 768 | tf_op jit(solution)/shard_map/reshape | solution.py:105
  14.8 0.1 pad_add_fusion.2.place
  14.9 0.0 copy-start.1
  14.9 0.7 %copy-done.1 = s32[4096]{0:T(1024)S(1)} copy-done((s32[4096]{0:T(1024)S(1)}, s32[4096]{0:T(1024)}, u32[]{:S(2)}) %copy-start.1) | copy-done | bytes 16408
  15.6 0.0 copy-start.2
  15.6 0.7 %copy-done.2 = s32[4096]{0:T(1024)S(1)} copy-done((s32[4096]{0:T(1024)S(1)}, s32[4096]{0:T(1024)}, u32[]{:S(2)}) %copy-start.2) | copy-done | bytes 16408
  16.4 0.0 copy-start.3
  16.4 0.7 %copy-done.3 = f32[2048]{0:T(1024)S(1)} copy-done((f32[2048]{0:T(1024)S(1)}, f32[2048]{0:T(1024)}, u32[]{:S(2)}) %copy-start.3) | copy-done | bytes 8216
  17.1 1.5 %energies.1 = (f32[1,1024]{1,0:T(1,128)S(1)}, f32[1,512]{1,0:T(1,128)S(1)}) custom-call(s32[2]{0:T(128)S(1)} %pad_add_fusion.2.place, s32[1,4096]{1,0:T(1,128)S(1)} %bitcast.9, s32[1,4096]{1,0:T(1,128)S(1)} %bitcast.10, f32[1,128]{1,0:T(1,128)S(1)} %pad_bitcast_fusion.occ_table, f32[16,128]{1,0:T(8,128)S(1)} %bitcast.11), custom_call_target="tpu_custom_call" | custom-call | bytes 1048576 | tf_op jit(solution)/shard_map/energies/pallas_call | solution.py:111
  18.6 0.0 collective-permute-done.sibling_ref
  18.6 0.0 copy-start
  18.6 1.6 %copy-done = f32[1024,512]{1,0:T(8,128)S(1)} copy-done((f32[1024,512]{1,0:T(8,128)S(1)}, f32[1024,512]{1,0:T(8,128)}, u32[]{:S(2)}) %copy-start) | copy-done | bytes 2097176
  20.2 1.3 %prepare.1 = (bf16[1024,1024]{1,0:T(8,128)(2,1)S(1)}, bf16[1024,1024]{1,0:T(8,128)(2,1)S(1)}) custom-call(s32[1]{0:T(128)} %bitcast.place, f32[1024,512]{1,0:T(8,128)S(1)} %copy-done, f32[1024,512]{1,0:T(8,128)S(1)} %collective-permute-done.sibling_ref), custom_call_target="tpu_custom_call" | custom-call | bytes 8388608 | tf_op jit(solution)/shard_map/prepare/pallas_call | solution.py:46
  21.5 0.0 collective-permute-done.2.factors_ref
  21.5 0.8 %contract.2 = f32[64,1024]{1,0:T(8,128)S(1)} custom-call(f32[64,1024]{1,0:T(8,128)S(1)} %collective-permute-done.2.factors_ref, bf16[1024,1024]{1,0:T(8,128)(2,1)S(1)} %get-tuple-element.19.high_ref, bf16[1024,1024]{1,0:T(8,128)(2,1)S(1)} %get-tuple-element.20.low_ref), custom_call_target="tpu_custom_call" | custom-call | flops 402653184 | bytes 4194304 | tf_op jit(solution)/shard_map/contract/pallas_call | solution.py:68
  22.3 2.9 %collective-permute-start.3 = (f32[64,1024]{1,0:T(8,128)S(1)}, f32[64,1024]{1,0:T(8,128)S(1)}, u32[]{:S(2)}, u32[]{:S(2)}) collective-permute-start(f32[64,1024]{1,0:T(8,128)S(1)} %contract.2), channel_id=1, source_target_pairs={{0,0},{1,5},{2,2},{3,7},{4,4},{5,1},{6,6},{7,3},{8,10},{9,15},{10,... | collective-permute-start | bytes 786440 | tf_op jit(solution)/shard_map/ppermute | solution.py:186
  25.2 0.0 collective-permute-done.4.factors_ref
  25.2 0.8 %contract.3 = f32[64,1024]{1,0:T(8,128)S(1)} custom-call(f32[64,1024]{1,0:T(8,128)S(1)} %collective-permute-done.4.factors_ref, bf16[1024,1024]{1,0:T(8,128)(2,1)S(1)} %get-tuple-element.19.high_ref, bf16[1024,1024]{1,0:T(8,128)(2,1)S(1)} %get-tuple-element.20.low_ref), custom_call_target="tpu_custom_call" | custom-call | flops 402653184 | bytes 4194304 | tf_op jit(solution)/shard_map/contract/pallas_call | solution.py:68
  26.0 1.9 %collective-permute-start.5 = (f32[64,1024]{1,0:T(8,128)S(1)}, f32[64,1024]{1,0:T(8,128)S(1)}, u32[]{:S(2)}, u32[]{:S(2)}) collective-permute-start(f32[64,1024]{1,0:T(8,128)S(1)} %contract.3), channel_id=1, source_target_pairs={{0,2},{1,7},{2,0},{3,5},{4,6},{5,3},{6,4},{7,1},{8,8},{9,13},{10,1... | collective-permute-start | bytes 786440 | tf_op jit(solution)/shard_map/ppermute | solution.py:186
  27.9 1.5 %collective-permute-done.3 = f32[64,1024]{1,0:T(8,128)S(1)} collective-permute-done((f32[64,1024]{1,0:T(8,128)S(1)}, f32[64,1024]{1,0:T(8,128)S(1)}, u32[]{:S(2)}, u32[]{:S(2)}) %collective-permute-start.3) | collective-permute-done | bytes 262176 | tf_op jit(solution)/shard_map/ppermute | solution.py:186
  29.4 4.6 %collective-permute-done.5 = f32[64,1024]{1,0:T(8,128)S(1)} collective-permute-done((f32[64,1024]{1,0:T(8,128)S(1)}, f32[64,1024]{1,0:T(8,128)S(1)}, u32[]{:S(2)}, u32[]{:S(2)}) %collective-permute-start.5) | collective-permute-done | bytes 262176 | tf_op jit(solution)/shard_map/ppermute | solution.py:186
  34.0 2.7 %collective-permute-start.6 = (f32[64,1024]{1,0:T(8,128)S(1)}, f32[64,1024]{1,0:T(8,128)S(1)}, u32[]{:S(2)}, u32[]{:S(2)}) collective-permute-start(f32[64,1024]{1,0:T(8,128)S(1)} %add.33), channel_id=1, source_target_pairs={{0,1},{1,0},{2,3},{3,2},{4,5},{5,4},{6,7},{7,6},{8,9},{9,8},{10,11... | collective-permute-start | bytes 786440 | tf_op jit(solution)/shard_map/ppermute | solution.py:186
  36.7 1.2 %collective-permute-done.6 = f32[64,1024]{1,0:T(8,128)S(1)} collective-permute-done((f32[64,1024]{1,0:T(8,128)S(1)}, f32[64,1024]{1,0:T(8,128)S(1)}, u32[]{:S(2)}, u32[]{:S(2)}) %collective-permute-start.6) | collective-permute-done | bytes 262176 | tf_op jit(solution)/shard_map/ppermute | solution.py:186
  37.9 0.1 add_add_fusion
  38.0 2.8 %collective-permute-start.7 = (f32[64,1024]{1,0:T(8,128)S(1)}, f32[64,1024]{1,0:T(8,128)S(1)}, u32[]{:S(2)}, u32[]{:S(2)}) collective-permute-start(f32[64,1024]{1,0:T(8,128)S(1)} %add_add_fusion), channel_id=1, source_target_pairs={{0,0},{1,5},{2,2},{3,7},{4,4},{5,1},{6,6},{7,3},{8,8},{9,13},{10,1... | collective-permute-start | bytes 786440 | tf_op jit(solution)/shard_map/ppermute | solution.py:186
  40.8 0.1 collective-permute-start.8
  40.9 2.8 %collective-permute-start.11 = (f32[64,1024]{1,0:T(8,128)S(1)}, f32[64,1024]{1,0:T(8,128)S(1)}, u32[]{:S(2)}, u32[]{:S(2)}) collective-permute-start(f32[64,1024]{1,0:T(8,128)S(1)} %add_add_fusion), channel_id=1, source_target_pairs={{0,0},{1,17},{2,8},{3,25},{4,16},{5,1},{6,24},{7,9},{8,10},{9,27},... | collective-permute-start | bytes 786440 | tf_op jit(solution)/shard_map/ppermute | solution.py:186
  43.7 3.9 %collective-permute-start.12 = (f32[64,1024]{1,0:T(8,128)S(1)}, f32[64,1024]{1,0:T(8,128)S(1)}, u32[]{:S(2)}, u32[]{:S(2)}) collective-permute-start(f32[64,1024]{1,0:T(8,128)S(1)} %add_add_fusion), channel_id=1, source_target_pairs={{0,8},{1,25},{2,0},{3,17},{4,24},{5,9},{6,16},{7,1},{8,2},{9,19},{... | collective-permute-start | bytes 786440 | tf_op jit(solution)/shard_map/ppermute | solution.py:186
  47.6 0.0 collective-permute-done.7.refs_0_
  47.6 0.1 collective-permute-start.9
  47.7 2.3 %collective-permute-done.8.refs_1_ = f32[64,1024]{1,0:T(8,128)S(1)} collective-permute-done((f32[64,1024]{1,0:T(8,128)S(1)}, f32[64,1024]{1,0:T(8,128)S(1)}, u32[]{:S(2)}, u32[]{:S(2)}) %collective-permute-start.8) | collective-permute-done | bytes 262176 | tf_op jit(solution)/shard_map/ppermute | solution.py:186
  50.0 0.0 collective-permute-start.10
  50.0 4.2 %collective-permute-done.11.refs_4_ = f32[64,1024]{1,0:T(8,128)S(1)} collective-permute-done((f32[64,1024]{1,0:T(8,128)S(1)}, f32[64,1024]{1,0:T(8,128)S(1)}, u32[]{:S(2)}, u32[]{:S(2)}) %collective-permute-start.11) | collective-permute-done | bytes 262176 | tf_op jit(solution)/shard_map/ppermute | solution.py:186
  54.2 0.0 collective-permute-start.13
  54.2 4.4 %collective-permute-done.12.refs_5_ = f32[64,1024]{1,0:T(8,128)S(1)} collective-permute-done((f32[64,1024]{1,0:T(8,128)S(1)}, f32[64,1024]{1,0:T(8,128)S(1)}, u32[]{:S(2)}, u32[]{:S(2)}) %collective-permute-start.12) | collective-permute-done | bytes 262176 | tf_op jit(solution)/shard_map/ppermute | solution.py:186
  58.6 0.0 collective-permute-start.14
  58.6 0.1 broadcast_xor_fusion.1
  58.7 0.1 pad_add_fusion.1.place
  58.8 0.0 collective-permute-done.9.refs_2_
  58.8 0.0 collective-permute-done.10.refs_3_
  58.8 0.0 collective-permute-done.13.refs_6_
  58.8 1.4 %collective-permute-done.14.refs_7_ = f32[64,1024]{1,0:T(8,128)S(1)} collective-permute-done((f32[64,1024]{1,0:T(8,128)S(1)}, f32[64,1024]{1,0:T(8,128)S(1)}, u32[]{:S(2)}, u32[]{:S(2)}) %collective-permute-start.14) | collective-permute-done | bytes 262176 | tf_op jit(solution)/shard_map/ppermute | solution.py:186
  60.1 3.5 %outer.1 = f32[1024,512]{1,0:T(8,128)} custom-call(s32[9]{0:T(128)S(1)} %pad_add_fusion.1.place, f32[1,1024]{1,0:T(1,128)S(1)} %get-tuple-element.17.rows_energy, f32[1,512]{1,0:T(1,128)S(1)} %get-tuple-element.18.cols_energy, f32[64,1024]{1,0:T(8,128)S(1)} %collective-permute-done.7.refs_0_, f32[64,1024]{1,0:T(8,128)S(1)} %collective-permute-done.8.refs_1_, ...), custom_call_target="tpu_custom_call" | custom-call | flops 805306368 | bytes 2097152 | tf_op jit(solution)/shard_map/outer/pallas_call | solution.py:157
  (3 shorter events, 0.0 us)
Async XLA Ops:
  0.0 18.6 %collective-permute-start = (f32[1024,512]{1,0:T(8,128)}, f32[1024,512]{1,0:T(8,128)S(1)}, u32[]{:S(2)}, u32[]{:S(2)}) collective-permute-start(f32[1024,512]{1,0:T(8,128)} %own_ref.1), channel_id=1, source_target_pairs={{0,1},{1,0},{2,3},{3,2},{4,5},{5,4},{6,7},{7,6},{8,9},{9,8},{10,11... | collective-permute-start | bytes 6291464 | tf_op jit(solution)/shard_map/ppermute | solution.py:186
  0.7 4.2 %collective-permute-start.1 = (f32[32,1024]{1,0:T(8,128)}, f32[32,1024]{1,0:T(8,128)S(1)}, u32[]{:S(2)}, u32[]{:S(2)}) collective-permute-start(f32[32,1024]{1,0:T(8,128)} %bitcast.12), channel_id=1, source_target_pairs={{0,1},{1,0},{2,3},{3,2},{4,5},{5,4},{6,7},{7,6},{8,9},{9,8},{10,11... | collective-permute-start | bytes 393224 | tf_op jit(solution)/shard_map/ppermute | solution.py:186
  5.9 15.6 %collective-permute-start.2 = (f32[64,1024]{1,0:T(8,128)S(1)}, f32[64,1024]{1,0:T(8,128)S(1)}, u32[]{:S(2)}, u32[]{:S(2)}) collective-permute-start(f32[64,1024]{1,0:T(8,128)S(1)} %maximum_select_fusion), channel_id=1, source_target_pairs={{0,0},{1,17},{2,8},{3,25},{4,16},{5,1},{6,24},{7,9},{8,10},{9,27},... | collective-permute-start | bytes 786440 | tf_op jit(solution)/shard_map/ppermute | solution.py:186
  7.8 17.4 %collective-permute-start.4 = (f32[64,1024]{1,0:T(8,128)S(1)}, f32[64,1024]{1,0:T(8,128)S(1)}, u32[]{:S(2)}, u32[]{:S(2)}) collective-permute-start(f32[64,1024]{1,0:T(8,128)S(1)} %maximum_select_fusion), channel_id=1, source_target_pairs={{0,8},{1,25},{2,0},{3,17},{4,24},{5,9},{6,16},{7,1},{8,2},{9,19},{... | collective-permute-start | bytes 786440 | tf_op jit(solution)/shard_map/ppermute | solution.py:186
  14.9 0.7 %copy-start.1 = (s32[4096]{0:T(1024)S(1)}, s32[4096]{0:T(1024)}, u32[]{:S(2)}) copy-start(s32[4096]{0:T(1024)} %param.8) | copy-start | bytes 49156
  15.6 0.7 %copy-start.2 = (s32[4096]{0:T(1024)S(1)}, s32[4096]{0:T(1024)}, u32[]{:S(2)}) copy-start(s32[4096]{0:T(1024)} %param.9) | copy-start | bytes 49156
  16.4 0.7 %copy-start.3 = (f32[2048]{0:T(1024)S(1)}, f32[2048]{0:T(1024)}, u32[]{:S(2)}) copy-start(f32[2048]{0:T(1024)} %param.11) | copy-start | bytes 24580
  18.6 1.6 %copy-start = (f32[1024,512]{1,0:T(8,128)S(1)}, f32[1024,512]{1,0:T(8,128)}, u32[]{:S(2)}) copy-start(f32[1024,512]{1,0:T(8,128)} %own_ref.1) | copy-start | bytes 6291460
  22.3 7.1 %collective-permute-start.3 = (f32[64,1024]{1,0:T(8,128)S(1)}, f32[64,1024]{1,0:T(8,128)S(1)}, u32[]{:S(2)}, u32[]{:S(2)}) collective-permute-start(f32[64,1024]{1,0:T(8,128)S(1)} %contract.2), channel_id=1, source_target_pairs={{0,0},{1,5},{2,2},{3,7},{4,4},{5,1},{6,6},{7,3},{8,10},{9,15},{10,... | collective-permute-start | bytes 786440 | tf_op jit(solution)/shard_map/ppermute | solution.py:186
  26.0 8.0 %collective-permute-start.5 = (f32[64,1024]{1,0:T(8,128)S(1)}, f32[64,1024]{1,0:T(8,128)S(1)}, u32[]{:S(2)}, u32[]{:S(2)}) collective-permute-start(f32[64,1024]{1,0:T(8,128)S(1)} %contract.3), channel_id=1, source_target_pairs={{0,2},{1,7},{2,0},{3,5},{4,6},{5,3},{6,4},{7,1},{8,8},{9,13},{10,1... | collective-permute-start | bytes 786440 | tf_op jit(solution)/shard_map/ppermute | solution.py:186
  34.0 3.9 %collective-permute-start.6 = (f32[64,1024]{1,0:T(8,128)S(1)}, f32[64,1024]{1,0:T(8,128)S(1)}, u32[]{:S(2)}, u32[]{:S(2)}) collective-permute-start(f32[64,1024]{1,0:T(8,128)S(1)} %add.33), channel_id=1, source_target_pairs={{0,1},{1,0},{2,3},{3,2},{4,5},{5,4},{6,7},{7,6},{8,9},{9,8},{10,11... | collective-permute-start | bytes 786440 | tf_op jit(solution)/shard_map/ppermute | solution.py:186
  38.0 9.7 %collective-permute-start.7 = (f32[64,1024]{1,0:T(8,128)S(1)}, f32[64,1024]{1,0:T(8,128)S(1)}, u32[]{:S(2)}, u32[]{:S(2)}) collective-permute-start(f32[64,1024]{1,0:T(8,128)S(1)} %add_add_fusion), channel_id=1, source_target_pairs={{0,0},{1,5},{2,2},{3,7},{4,4},{5,1},{6,6},{7,3},{8,8},{9,13},{10,1... | collective-permute-start | bytes 786440 | tf_op jit(solution)/shard_map/ppermute | solution.py:186
  40.8 9.2 %collective-permute-start.8 = (f32[64,1024]{1,0:T(8,128)S(1)}, f32[64,1024]{1,0:T(8,128)S(1)}, u32[]{:S(2)}, u32[]{:S(2)}) collective-permute-start(f32[64,1024]{1,0:T(8,128)S(1)} %add_add_fusion), channel_id=1, source_target_pairs={{0,2},{1,7},{2,0},{3,5},{4,6},{5,3},{6,4},{7,1},{8,10},{9,15},{10,... | collective-permute-start | bytes 786440 | tf_op jit(solution)/shard_map/ppermute | solution.py:186
  40.9 13.3 %collective-permute-start.11 = (f32[64,1024]{1,0:T(8,128)S(1)}, f32[64,1024]{1,0:T(8,128)S(1)}, u32[]{:S(2)}, u32[]{:S(2)}) collective-permute-start(f32[64,1024]{1,0:T(8,128)S(1)} %add_add_fusion), channel_id=1, source_target_pairs={{0,0},{1,17},{2,8},{3,25},{4,16},{5,1},{6,24},{7,9},{8,10},{9,27},... | collective-permute-start | bytes 786440 | tf_op jit(solution)/shard_map/ppermute | solution.py:186
  43.7 14.9 %collective-permute-start.12 = (f32[64,1024]{1,0:T(8,128)S(1)}, f32[64,1024]{1,0:T(8,128)S(1)}, u32[]{:S(2)}, u32[]{:S(2)}) collective-permute-start(f32[64,1024]{1,0:T(8,128)S(1)} %add_add_fusion), channel_id=1, source_target_pairs={{0,8},{1,25},{2,0},{3,17},{4,24},{5,9},{6,16},{7,1},{8,2},{9,19},{... | collective-permute-start | bytes 786440 | tf_op jit(solution)/shard_map/ppermute | solution.py:186
  47.6 11.1 %collective-permute-start.9 = (f32[64,1024]{1,0:T(8,128)S(1)}, f32[64,1024]{1,0:T(8,128)S(1)}, u32[]{:S(2)}, u32[]{:S(2)}) collective-permute-start(f32[64,1024]{1,0:T(8,128)S(1)} %collective-permute-done.7.refs_0_), channel_id=1, source_target_pairs={{0,1},{1,0},{2,3},{3,2},{4,5},{5,4},{6,7},{7,6},{8,9},{9,8},{10,11... | collective-permute-start | bytes 786440 | tf_op jit(solution)/shard_map/ppermute | solution.py:186
  50.0 8.8 %collective-permute-start.10 = (f32[64,1024]{1,0:T(8,128)S(1)}, f32[64,1024]{1,0:T(8,128)S(1)}, u32[]{:S(2)}, u32[]{:S(2)}) collective-permute-start(f32[64,1024]{1,0:T(8,128)S(1)} %collective-permute-done.8.refs_1_), channel_id=1, source_target_pairs={{0,1},{1,0},{2,3},{3,2},{4,5},{5,4},{6,7},{7,6},{8,9},{9,8},{10,11... | collective-permute-start | bytes 786440 | tf_op jit(solution)/shard_map/ppermute | solution.py:186
  54.2 4.6 %collective-permute-start.13 = (f32[64,1024]{1,0:T(8,128)S(1)}, f32[64,1024]{1,0:T(8,128)S(1)}, u32[]{:S(2)}, u32[]{:S(2)}) collective-permute-start(f32[64,1024]{1,0:T(8,128)S(1)} %collective-permute-done.11.refs_4_), channel_id=1, source_target_pairs={{0,1},{1,0},{2,3},{3,2},{4,5},{5,4},{6,7},{7,6},{8,9},{9,8},{10,11... | collective-permute-start | bytes 786440 | tf_op jit(solution)/shard_map/ppermute | solution.py:186
  58.6 1.5 %collective-permute-start.14 = (f32[64,1024]{1,0:T(8,128)S(1)}, f32[64,1024]{1,0:T(8,128)S(1)}, u32[]{:S(2)}, u32[]{:S(2)}) collective-permute-start(f32[64,1024]{1,0:T(8,128)S(1)} %collective-permute-done.12.refs_5_), channel_id=1, source_target_pairs={{0,1},{1,0},{2,3},{3,2},{4,5},{5,4},{6,7},{7,6},{8,9},{9,8},{10,11... | collective-permute-start | bytes 786440 | tf_op jit(solution)/shard_map/ppermute | solution.py:186

commit v3 on v2

--- a/solution.py
+++ b/solution.py
@@ -119,25 +119,51 @@
     )(place, occ_index, vir_index, occ_table, vir_table)
 
 
-def outer_kernel(slots, place, rows_energy, cols_energy, *refs):
-    left, right = refs[:slots], refs[slots : 2 * slots]
-    out_ref, left_ref, high_ref, low_ref = refs[2 * slots :]
+def left_kernel(slots, *refs):
+    high_ref, low_ref = refs[slots:]
+    depth = refs[0].shape[0]
+    step = 128 // depth
+    for slot in range(0, slots, step):
+        block = jnp.concatenate([refs[slot + k][...] for k in range(step)], axis=0).T
+        high, low = split(block)
+        here = pl.ds(slot * depth, step * depth)
+        high_ref[:, here] = high
+        low_ref[:, here] = low
+
+
+def left_parts(left):
+    slots = len(left)
+    depth, total = left[0].shape
+    out = shape_of((total, slots * depth), jnp.bfloat16)
+    return pl.pallas_call(
+        functools.partial(left_kernel, slots),
+        out_shape=(out, out),
+        in_specs=whole_specs(slots),
+        out_specs=whole_specs(2),
+        compiler_params=params(*left, out, out),
+        cost_estimate=pl.CostEstimate(flops=0, bytes_accessed=out.size * 8, transcendentals=0),
+        name="left_parts",
+    )(*left)
+
+
+def outer_kernel(slots, place, rows_energy, cols_energy, left_high, left_low, *refs):
+    right = refs[:slots]
+    out_ref, high_ref, low_ref = refs[slots:]
     step = pl.program_id(0)
-    depth = left[0].shape[0]
+    depth = right[0].shape[0]
     tall, wide = out_ref.shape
 
     @pl.when(step == 0)
     def _():
         mine = pl.ds(pl.multiple_of(place[0] * wide, wide), wide)
         for slot in range(slots):
-            left_ref[pl.ds(pl.multiple_of(place[1 + slot] * depth, depth), depth), :] = left[slot][...]
             high, low = split(right[slot][:, mine])
-            here = pl.ds(pl.multiple_of(place[1 + slots + slot] * depth, depth), depth)
+            here = pl.ds(pl.multiple_of(place[1 + slot] * depth, depth), depth)
             high_ref[here, :] = high
             low_ref[here, :] = low
 
     here = pl.ds(pl.multiple_of(step * tall, tall), tall)
-    high, low = split(left_ref[:, here].T)
+    high, low = left_high[here, :], left_low[here, :]
     total = jnp.dot(low, high_ref[...], preferred_element_type=jnp.float32)
     total += jnp.dot(high, low_ref[...], preferred_element_type=jnp.float32)
     total += jnp.dot(high, high_ref[...], preferred_element_type=jnp.float32)
@@ -146,12 +172,12 @@
     out_ref[...] = -total / denominator
 
 
-def outer(place, rows_energy, cols_energy, left, right):
-    slots = len(left)
-    depth, total = left[0].shape
+def outer(place, rows_energy, cols_energy, left_high, left_low, right):
+    slots = len(right)
+    depth, total = right[0].shape
     wide = cols_energy.shape[1]
     tall = min(256, total)
-    arrays = [*left, *right]
+    arrays = [left_high, left_low, *right]
     out = shape_of((total, wide))
     parts = pltpu.VMEM((slots * depth, wide), jnp.bfloat16)
     return pl.pallas_call(
@@ -162,10 +188,10 @@
             grid=(total // tall,),
             in_specs=whole_specs(2 + len(arrays)),
             out_specs=pl.BlockSpec((tall, wide), lambda step, place: (step, 0)),
-            scratch_shapes=[pltpu.VMEM((slots * depth, total), jnp.float32), parts, parts],
+            scratch_shapes=[parts, parts],
         ),
         compiler_params=pltpu.CompilerParams(
-            vmem_limit_bytes=sum(a.size * 4 for a in arrays) * 2 + 10 * tall * wide * 4 + 8 * MIB
+            vmem_limit_bytes=sum(a.size * 4 for a in arrays) + 10 * tall * wide * 4 + 8 * MIB
         ),
         cost_estimate=pl.CostEstimate(
             flops=6 * out.size * slots * depth, bytes_accessed=out.size * 4, transcendentals=0
@@ -182,6 +208,10 @@
     def number(z, j, s):
         return z * cols + j * cores + s
 
+    def turn(i, s):
+        i = share - 1 - i
+        return i if s == 0 else rows - 1 - i
+
     def move(x, to):
         return lax.ppermute(x, AXES, [(number(*at), number(*to(*at))) for at in chips])
 
@@ -189,18 +219,18 @@
         return move(x, lambda z, j, s: (z, j, 1 - s))
 
     def transposed(x, i):
-        return move(x, lambda z, j, s: (j ^ z ^ (s * share + i), z, s))
+        return move(x, lambda z, j, s: (j ^ z ^ turn(i, s), z, s))
 
     def reduced(x, i):
-        return move(x, lambda z, j, s: (z, z ^ j ^ (s * share + i), s))
+        return move(x, lambda z, j, s: (z, z ^ j ^ turn(i, s), s))
 
     def across(x, i):
-        return move(x, lambda z, j, s: (z, j ^ (s * share + i), s))
+        return move(x, lambda z, j, s: (z, j ^ turn(i, s), s))
 
     turns = range(share)
     row_index = lax.axis_index("row").astype(jnp.int32)
     col_index = lax.axis_index("col").astype(jnp.int32)
-    core, chip = col_index % cores, col_index // cores
+    core = col_index % cores
     tall, wide = amplitudes.shape
 
     def share_of(x):
@@ -211,7 +241,8 @@
 
     pieces = share_of(factors.T)
     received = [transposed(pieces, i) for i in turns]
-    high, low = prepare(core, amplitudes, swap(amplitudes))
+    tied, pieces = lax.optimization_barrier((amplitudes, pieces))
+    high, low = prepare(core, amplitudes, swap(tied))
     rows_energy, cols_energy = pair_energies(
         jnp.stack([row_index, col_index]), occ_index, vir_index, occ_energy, vir_energy, tall, wide
     )
@@ -221,13 +252,20 @@
     arrived = [reduced(contract(received[i], high, low), i) for i in turns]
     total = functools.reduce(jnp.add, arrived)
     dressed = pieces + (total + swap(total))
-    columns = [transposed(dressed, i) for i in turns]
-    own = [across(dressed, i) for i in turns]
-    columns += [swap(x) for x in columns]
-    own += [swap(x) for x in own]
-    turn = jnp.concatenate([core * share + jnp.arange(share), (1 - core) * share + jnp.arange(share)])
-    place = jnp.concatenate([core[None], chip ^ turn, row_index ^ chip ^ turn]).astype(jnp.int32)
-    return outer(place, rows_energy, cols_energy, own, columns)
+    left = [across(dressed, i) for i in turns]
+    left += [swap(x) for x in left]
+    right = [transposed(dressed, i) for i in turns]
+    right += [swap(x) for x in right]
+    first = share - 1 - jnp.arange(share, dtype=jnp.int32)
+    first = jnp.where(core == 0, first, rows - 1 - first)
+    order = jnp.concatenate([first, rows - 1 - first])
+    wanted = row_index ^ order
+    at = jnp.sum(
+        jnp.where(wanted[:, None] == order[None, :], jnp.arange(rows, dtype=jnp.int32)[None, :], 0), axis=1
+    )
+    place = jnp.concatenate([core[None], at]).astype(jnp.int32)
+    left_high, left_low = left_parts(left)
+    return outer(place, rows_energy, cols_energy, left_high, left_low, right)
 
 
 def solution(mesh):

time: 64.2 us -> 60.2 us (0.938)
  waiting for transfers between devices: 23.7 us -> 16.9 us
  starting transfers between devices: 26.2 us -> 28.7 us
    ppermute x15, waiting for transfers between devices: 23.7 us -> 16.9 us  [move(): lax.ppermute(x, AXES, [(number(*at), number(*to(*at))) for at in chips])]
    ppermute x15, starting transfers between devices: 26.2 us -> 28.7 us  [move(): lax.ppermute(x, AXES, [(number(*at), number(*to(*at))) for at in chips])]
  transfers between devices with their start and end apart: 15 -> 15, of which waited for: 8 -> 7; matrix products, arithmetic and copies ran while one was open for 3% -> 2% of each run, Pallas kernels for 7% -> 8%
where the time goes in v3:
time: 60.2 us; the launch traced here: 59.7 us
  starting transfers between devices  28.7 us (48%)
  waiting for transfers between devices  16.9 us (28%)
  Pallas kernels  8.04 us (13%)
  local copies, waits for them, and re-layouts  4.38 us (7%)
  other arithmetic  1.5 us (2%)
    ppermute x15, starting transfers between devices, move(): lax.ppermute(x, AXES, [(number(*at), number(*to(*at))) for at in chips])  28.7 us
    ppermute x15, waiting for transfers between devices, move(): lax.ppermute(x, AXES, [(number(*at), number(*to(*at))) for at in chips])  16.9 us
    unnamed x8, local copies, waits for them, and re-layouts  3.72 us
    pallas_call x1, Pallas kernels, outer(): pl.pallas_call(functools.partial(outer_kernel, slots), out_shape=out, gri...  3.35 us
    pallas_call x2, Pallas kernels, contract(): pl.pallas_call(contract_kernel, out_shape=out, in_specs=whole_specs(3), o...  1.54 us
    pallas_call x1, Pallas kernels, pair_energies(): pl.pallas_call(energy_kernel, out_shape=(shape_of((1, rows)), shape_of((1...  1.53 us
    pallas_call x1, Pallas kernels, prepare(): pl.pallas_call(prepare_kernel, out_shape=(out, out), in_specs=[pl.BlockSp...  1.28 us
  transfers between devices with their start and end apart: 15, of which 7 were waited for; matrix products, arithmetic and copies ran while one was open for 2% of the time, Pallas kernels for 8%

profile of v3, /device:TPU:5, one launch (start us, length us, event | category | flops | bytes accessed | tf_op | source)
XLA Modules:
  0.0 59.7 jit_solution(16524731604092807698)
XLA Ops:
  0.0 0.7 %collective-permute-start = (f32[32,1024]{1,0:T(8,128)}, f32[32,1024]{1,0:T(8,128)S(1)}, u32[]{:S(2)}, u32[]{:S(2)}) collective-permute-start(f32[32,1024]{1,0:T(8,128)} %bitcast.12), channel_id=1, source_target_pairs={{0,1},{1,0},{2,3},{3,2},{4,5},{5,4},{6,7},{7,6},{8,9},{9,8},{10,11... | collective-permute-start | bytes 393224 | tf_op jit(solution)/shard_map/ppermute | solution.py:216
  0.7 1.2 %collective-permute-done = f32[32,1024]{1,0:T(8,128)S(1)} collective-permute-done((f32[32,1024]{1,0:T(8,128)}, f32[32,1024]{1,0:T(8,128)S(1)}, u32[]{:S(2)}, u32[]{:S(2)}) %collective-permute-start) | collective-permute-done | bytes 131104 | tf_op jit(solution)/shard_map/ppermute | solution.py:216
  1.9 1.0 %maximum_select_fusion = f32[64,1024]{1,0:T(8,128)S(1)} fusion(f32[32,1024]{1,0:T(8,128)S(1)} %collective-permute-done, f32[32,1024]{1,0:T(8,128)} %bitcast.13, pred[]{:T(512)S(6)} %eq.10), kind=kLoop, calls=%fused_computation | loop fusion | flops 196608 | bytes 524289 | tf_op jit(solution)/shard_map/jit(_where)/select_n | solution.py:238
  2.9 0.4 collective-permute-start.1
  3.3 3.1 %collective-permute-start.4 = (f32[64,1024]{1,0:T(8,128)S(1)}, f32[64,1024]{1,0:T(8,128)S(1)}, u32[]{:S(2)}, u32[]{:S(2)}) collective-permute-start(f32[64,1024]{1,0:T(8,128)S(1)} %maximum_select_fusion), channel_id=1, source_target_pairs={{0,0},{1,25},{2,8},{3,17},{4,16},{5,9},{6,24},{7,1},{8,10},{9,19},... | collective-permute-start | bytes 786440 | tf_op jit(solution)/shard_map/ppermute | solution.py:216
  6.5 4.2 %collective-permute-start.2 = (f32[64,1024]{1,0:T(8,128)S(1)}, f32[64,1024]{1,0:T(8,128)S(1)}, u32[]{:S(2)}, u32[]{:S(2)}) collective-permute-start(f32[64,1024]{1,0:T(8,128)S(1)} %maximum_select_fusion), channel_id=1, source_target_pairs={{0,8},{1,17},{2,0},{3,25},{4,24},{5,1},{6,16},{7,9},{8,2},{9,27},{... | collective-permute-start | bytes 786440 | tf_op jit(solution)/shard_map/ppermute | solution.py:216
  10.7 0.7 %pad_bitcast_fusion.occ_table = f32[1,128]{1,0:T(1,128)S(1)} fusion(f32[64]{0:T(128)} %param.10), kind=kLoop, calls=%fused_computation.7 | loop fusion | bytes 768 | tf_op jit(solution)/shard_map/reshape | solution.py:105
  11.3 0.1 pad_add_fusion.2.place
  11.4 0.0 copy-start.1
  11.4 0.7 %copy-done.1 = s32[4096]{0:T(1024)S(1)} copy-done((s32[4096]{0:T(1024)S(1)}, s32[4096]{0:T(1024)}, u32[]{:S(2)}) %copy-start.1) | copy-done | bytes 16408
  12.1 0.0 copy-start.2
  12.1 0.7 %copy-done.2 = s32[4096]{0:T(1024)S(1)} copy-done((s32[4096]{0:T(1024)S(1)}, s32[4096]{0:T(1024)}, u32[]{:S(2)}) %copy-start.2) | copy-done | bytes 16408
  12.9 0.0 copy-start.3
  12.9 0.7 %copy-done.3 = f32[2048]{0:T(1024)S(1)} copy-done((f32[2048]{0:T(1024)S(1)}, f32[2048]{0:T(1024)}, u32[]{:S(2)}) %copy-start.3) | copy-done | bytes 8216
  13.6 1.5 %energies.1 = (f32[1,1024]{1,0:T(1,128)S(1)}, f32[1,512]{1,0:T(1,128)S(1)}) custom-call(s32[2]{0:T(128)S(1)} %pad_add_fusion.2.place, s32[1,4096]{1,0:T(1,128)S(1)} %bitcast.9, s32[1,4096]{1,0:T(1,128)S(1)} %bitcast.10, f32[1,128]{1,0:T(1,128)S(1)} %pad_bitcast_fusion.occ_table, f32[16,128]{1,0:T(8,128)S(1)} %bitcast.11), custom_call_target="tpu_custom_call" | custom-call | bytes 1048576 | tf_op jit(solution)/shard_map/energies/pallas_call | solution.py:111
  15.1 0.0 collective-permute-done.1.sibling_ref
  15.1 0.0 copy-start
  15.1 1.6 %copy-done = f32[1024,512]{1,0:T(8,128)S(1)} copy-done((f32[1024,512]{1,0:T(8,128)S(1)}, f32[1024,512]{1,0:T(8,128)}, u32[]{:S(2)}) %copy-start) | copy-done | bytes 2097176
  16.7 1.3 %prepare.1 = (bf16[1024,1024]{1,0:T(8,128)(2,1)S(1)}, bf16[1024,1024]{1,0:T(8,128)(2,1)S(1)}) custom-call(s32[1]{0:T(128)} %bitcast.place, f32[1024,512]{1,0:T(8,128)S(1)} %copy-done, f32[1024,512]{1,0:T(8,128)S(1)} %collective-permute-done.1.sibling_ref), custom_call_target="tpu_custom_call" | custom-call | bytes 8388608 | tf_op jit(solution)/shard_map/prepare/pallas_call | solution.py:46
  18.0 0.0 collective-permute-done.4.factors_ref
  18.0 0.8 %contract.3 = f32[64,1024]{1,0:T(8,128)S(1)} custom-call(f32[64,1024]{1,0:T(8,128)S(1)} %collective-permute-done.4.factors_ref, bf16[1024,1024]{1,0:T(8,128)(2,1)S(1)} %get-tuple-element.25.high_ref, bf16[1024,1024]{1,0:T(8,128)(2,1)S(1)} %get-tuple-element.26.low_ref), custom_call_target="tpu_custom_call" | custom-call | flops 402653184 | bytes 4194304 | tf_op jit(solution)/shard_map/contract/pallas_call | solution.py:68
  18.8 4.6 %collective-permute-start.5 = (f32[64,1024]{1,0:T(8,128)S(1)}, f32[64,1024]{1,0:T(8,128)S(1)}, u32[]{:S(2)}, u32[]{:S(2)}) collective-permute-start(f32[64,1024]{1,0:T(8,128)S(1)} %contract.3), channel_id=1, source_target_pairs={{0,0},{1,7},{2,2},{3,5},{4,4},{5,3},{6,6},{7,1},{8,10},{9,13},{10,... | collective-permute-start | bytes 786440 | tf_op jit(solution)/shard_map/ppermute | solution.py:216
  23.4 0.0 collective-permute-done.2.factors_ref
  23.4 0.8 %contract.2 = f32[64,1024]{1,0:T(8,128)S(1)} custom-call(f32[64,1024]{1,0:T(8,128)S(1)} %collective-permute-done.2.factors_ref, bf16[1024,1024]{1,0:T(8,128)(2,1)S(1)} %get-tuple-element.25.high_ref, bf16[1024,1024]{1,0:T(8,128)(2,1)S(1)} %get-tuple-element.26.low_ref), custom_call_target="tpu_custom_call" | custom-call | flops 402653184 | bytes 4194304 | tf_op jit(solution)/shard_map/contract/pallas_call | solution.py:68
  24.2 1.9 %collective-permute-start.3 = (f32[64,1024]{1,0:T(8,128)S(1)}, f32[64,1024]{1,0:T(8,128)S(1)}, u32[]{:S(2)}, u32[]{:S(2)}) collective-permute-start(f32[64,1024]{1,0:T(8,128)S(1)} %contract.2), channel_id=1, source_target_pairs={{0,2},{1,5},{2,0},{3,7},{4,6},{5,1},{6,4},{7,3},{8,8},{9,15},{10,1... | collective-permute-start | bytes 786440 | tf_op jit(solution)/shard_map/ppermute | solution.py:216
  26.1 3.6 %collective-permute-done.5 = f32[64,1024]{1,0:T(8,128)S(1)} collective-permute-done((f32[64,1024]{1,0:T(8,128)S(1)}, f32[64,1024]{1,0:T(8,128)S(1)}, u32[]{:S(2)}, u32[]{:S(2)}) %collective-permute-start.5) | collective-permute-done | bytes 262176 | tf_op jit(solution)/shard_map/ppermute | solution.py:216
  29.7 2.2 %collective-permute-done.3 = f32[64,1024]{1,0:T(8,128)S(1)} collective-permute-done((f32[64,1024]{1,0:T(8,128)S(1)}, f32[64,1024]{1,0:T(8,128)S(1)}, u32[]{:S(2)}, u32[]{:S(2)}) %collective-permute-start.3) | collective-permute-done | bytes 262176 | tf_op jit(solution)/shard_map/ppermute | solution.py:216
  31.9 0.1 collective-permute-start.6
  32.0 1.5 %collective-permute-done.6 = f32[64,1024]{1,0:T(8,128)S(1)} collective-permute-done((f32[64,1024]{1,0:T(8,128)S(1)}, f32[64,1024]{1,0:T(8,128)S(1)}, u32[]{:S(2)}, u32[]{:S(2)}) %collective-permute-start.6) | collective-permute-done | bytes 262176 | tf_op jit(solution)/shard_map/ppermute | solution.py:216
  33.6 2.4 %collective-permute-start.8 = (f32[64,1024]{1,0:T(8,128)S(1)}, f32[64,1024]{1,0:T(8,128)S(1)}, u32[]{:S(2)}, u32[]{:S(2)}) collective-permute-start(f32[64,1024]{1,0:T(8,128)S(1)} %add_add_fusion), channel_id=1, source_target_pairs={{0,0},{1,7},{2,2},{3,5},{4,4},{5,3},{6,6},{7,1},{8,8},{9,15},{10,1... | collective-permute-start | bytes 786440 | tf_op jit(solution)/shard_map/ppermute | solution.py:216
  36.0 0.6 %collective-permute-start.7 = (f32[64,1024]{1,0:T(8,128)S(1)}, f32[64,1024]{1,0:T(8,128)S(1)}, u32[]{:S(2)}, u32[]{:S(2)}) collective-permute-start(f32[64,1024]{1,0:T(8,128)S(1)} %add_add_fusion), channel_id=1, source_target_pairs={{0,2},{1,5},{2,0},{3,7},{4,6},{5,1},{6,4},{7,3},{8,10},{9,13},{10,... | collective-permute-start | bytes 786440 | tf_op jit(solution)/shard_map/ppermute | solution.py:216
  36.7 2.8 %collective-permute-start.11 = (f32[64,1024]{1,0:T(8,128)S(1)}, f32[64,1024]{1,0:T(8,128)S(1)}, u32[]{:S(2)}, u32[]{:S(2)}) collective-permute-start(f32[64,1024]{1,0:T(8,128)S(1)} %add_add_fusion), channel_id=1, source_target_pairs={{0,8},{1,17},{2,0},{3,25},{4,24},{5,1},{6,16},{7,9},{8,2},{9,27},{... | collective-permute-start | bytes 786440 | tf_op jit(solution)/shard_map/ppermute | solution.py:216
  39.5 7.2 %collective-permute-start.12 = (f32[64,1024]{1,0:T(8,128)S(1)}, f32[64,1024]{1,0:T(8,128)S(1)}, u32[]{:S(2)}, u32[]{:S(2)}) collective-permute-start(f32[64,1024]{1,0:T(8,128)S(1)} %add_add_fusion), channel_id=1, source_target_pairs={{0,0},{1,25},{2,8},{3,17},{4,16},{5,9},{6,24},{7,1},{8,10},{9,19},... | collective-permute-start | bytes 786440 | tf_op jit(solution)/shard_map/ppermute | solution.py:216
  46.7 0.0 collective-permute-done.8.refs_1_
  46.7 0.1 collective-permute-start.10
  46.8 0.0 collective-permute-done.7.refs_0_
  46.8 0.5 collective-permute-start.9
  47.3 4.6 %collective-permute-done.11.refs_0_ = f32[64,1024]{1,0:T(8,128)S(1)} collective-permute-done((f32[64,1024]{1,0:T(8,128)S(1)}, f32[64,1024]{1,0:T(8,128)S(1)}, u32[]{:S(2)}, u32[]{:S(2)}) %collective-permute-start.11) | collective-permute-done | bytes 262176 | tf_op jit(solution)/shard_map/ppermute | solution.py:216
  51.8 0.0 collective-permute-start.13
  51.8 2.9 %collective-permute-done.12.refs_1_ = f32[64,1024]{1,0:T(8,128)S(1)} collective-permute-done((f32[64,1024]{1,0:T(8,128)S(1)}, f32[64,1024]{1,0:T(8,128)S(1)}, u32[]{:S(2)}, u32[]{:S(2)}) %collective-permute-start.12) | collective-permute-done | bytes 262176 | tf_op jit(solution)/shard_map/ppermute | solution.py:216
  54.8 0.0 collective-permute-start.14
  54.8 0.1 broadcast_xor_fusion
  54.8 0.2 select_reduce_fusion
  55.0 0.1 pad_add_fusion.1.place
  55.1 0.0 collective-permute-done.10.refs_3_
  55.1 0.0 collective-permute-done.9.refs_2_
  55.1 0.3 left_parts.1
  55.5 0.0 collective-permute-done.13.refs_2_
  55.5 0.8 %collective-permute-done.14.refs_3_ = f32[64,1024]{1,0:T(8,128)S(1)} collective-permute-done((f32[64,1024]{1,0:T(8,128)S(1)}, f32[64,1024]{1,0:T(8,128)S(1)}, u32[]{:S(2)}, u32[]{:S(2)}) %collective-permute-start.14) | collective-permute-done | bytes 262176 | tf_op jit(solution)/shard_map/ppermute | solution.py:216
  56.3 3.4 %outer.1 = f32[1024,512]{1,0:T(8,128)} custom-call(s32[5]{0:T(128)S(1)} %pad_add_fusion.1.place, f32[1,1024]{1,0:T(1,128)S(1)} %get-tuple-element.22.rows_energy, f32[1,512]{1,0:T(1,128)S(1)} %get-tuple-element.23.cols_energy, bf16[1024,256]{1,0:T(8,128)(2,1)S(1)} %get-tuple-element.27.left_high, bf16[1024,256]{1,0:T(8,128)(2,1)S(1)} %get-tuple-element.28.left_low, ...), custom_call_target="tpu_custom_call" | custom-call | flops 805306368 | bytes 2097152 | tf_op jit(solution)/shard_map/outer/pallas_call | solution.py:183
  (3 shorter events, 0.1 us)
Async XLA Ops:
  0.0 1.9 %collective-permute-start = (f32[32,1024]{1,0:T(8,128)}, f32[32,1024]{1,0:T(8,128)S(1)}, u32[]{:S(2)}, u32[]{:S(2)}) collective-permute-start(f32[32,1024]{1,0:T(8,128)} %bitcast.12), channel_id=1, source_target_pairs={{0,1},{1,0},{2,3},{3,2},{4,5},{5,4},{6,7},{7,6},{8,9},{9,8},{10,11... | collective-permute-start | bytes 393224 | tf_op jit(solution)/shard_map/ppermute | solution.py:216
  2.9 12.2 %collective-permute-start.1 = (f32[1024,512]{1,0:T(8,128)}, f32[1024,512]{1,0:T(8,128)S(1)}, u32[]{:S(2)}, u32[]{:S(2)}) collective-permute-start(f32[1024,512]{1,0:T(8,128)} %own_ref.1), channel_id=1, source_target_pairs={{0,1},{1,0},{2,3},{3,2},{4,5},{5,4},{6,7},{7,6},{8,9},{9,8},{10,11... | collective-permute-start | bytes 6291464 | tf_op jit(solution)/shard_map/ppermute | solution.py:216
  3.3 14.7 %collective-permute-start.4 = (f32[64,1024]{1,0:T(8,128)S(1)}, f32[64,1024]{1,0:T(8,128)S(1)}, u32[]{:S(2)}, u32[]{:S(2)}) collective-permute-start(f32[64,1024]{1,0:T(8,128)S(1)} %maximum_select_fusion), channel_id=1, source_target_pairs={{0,0},{1,25},{2,8},{3,17},{4,16},{5,9},{6,24},{7,1},{8,10},{9,19},... | collective-permute-start | bytes 786440 | tf_op jit(solution)/shard_map/ppermute | solution.py:216
  6.5 16.9 %collective-permute-start.2 = (f32[64,1024]{1,0:T(8,128)S(1)}, f32[64,1024]{1,0:T(8,128)S(1)}, u32[]{:S(2)}, u32[]{:S(2)}) collective-permute-start(f32[64,1024]{1,0:T(8,128)S(1)} %maximum_select_fusion), channel_id=1, source_target_pairs={{0,8},{1,17},{2,0},{3,25},{4,24},{5,1},{6,16},{7,9},{8,2},{9,27},{... | collective-permute-start | bytes 786440 | tf_op jit(solution)/shard_map/ppermute | solution.py:216
  11.4 0.7 %copy-start.1 = (s32[4096]{0:T(1024)S(1)}, s32[4096]{0:T(1024)}, u32[]{:S(2)}) copy-start(s32[4096]{0:T(1024)} %param.8) | copy-start | bytes 49156
  12.1 0.7 %copy-start.2 = (s32[4096]{0:T(1024)S(1)}, s32[4096]{0:T(1024)}, u32[]{:S(2)}) copy-start(s32[4096]{0:T(1024)} %param.9) | copy-start | bytes 49156
  12.9 0.7 %copy-start.3 = (f32[2048]{0:T(1024)S(1)}, f32[2048]{0:T(1024)}, u32[]{:S(2)}) copy-start(f32[2048]{0:T(1024)} %param.11) | copy-start | bytes 24580
  15.1 1.6 %copy-start = (f32[1024,512]{1,0:T(8,128)S(1)}, f32[1024,512]{1,0:T(8,128)}, u32[]{:S(2)}) copy-start(f32[1024,512]{1,0:T(8,128)} %own_ref.1) | copy-start | bytes 6291460
  18.8 10.9 %collective-permute-start.5 = (f32[64,1024]{1,0:T(8,128)S(1)}, f32[64,1024]{1,0:T(8,128)S(1)}, u32[]{:S(2)}, u32[]{:S(2)}) collective-permute-start(f32[64,1024]{1,0:T(8,128)S(1)} %contract.3), channel_id=1, source_target_pairs={{0,0},{1,7},{2,2},{3,5},{4,4},{5,3},{6,6},{7,1},{8,10},{9,13},{10,... | collective-permute-start | bytes 786440 | tf_op jit(solution)/shard_map/ppermute | solution.py:216
  24.2 7.7 %collective-permute-start.3 = (f32[64,1024]{1,0:T(8,128)S(1)}, f32[64,1024]{1,0:T(8,128)S(1)}, u32[]{:S(2)}, u32[]{:S(2)}) collective-permute-start(f32[64,1024]{1,0:T(8,128)S(1)} %contract.2), channel_id=1, source_target_pairs={{0,2},{1,5},{2,0},{3,7},{4,6},{5,1},{6,4},{7,3},{8,8},{9,15},{10,1... | collective-permute-start | bytes 786440 | tf_op jit(solution)/shard_map/ppermute | solution.py:216
  31.9 1.6 %collective-permute-start.6 = (f32[64,1024]{1,0:T(8,128)S(1)}, f32[64,1024]{1,0:T(8,128)S(1)}, u32[]{:S(2)}, u32[]{:S(2)}) collective-permute-start(f32[64,1024]{1,0:T(8,128)S(1)} %add.16), channel_id=1, source_target_pairs={{0,1},{1,0},{2,3},{3,2},{4,5},{5,4},{6,7},{7,6},{8,9},{9,8},{10,11... | collective-permute-start | bytes 786440 | tf_op jit(solution)/shard_map/ppermute | solution.py:216
  33.6 13.1 %collective-permute-start.8 = (f32[64,1024]{1,0:T(8,128)S(1)}, f32[64,1024]{1,0:T(8,128)S(1)}, u32[]{:S(2)}, u32[]{:S(2)}) collective-permute-start(f32[64,1024]{1,0:T(8,128)S(1)} %add_add_fusion), channel_id=1, source_target_pairs={{0,0},{1,7},{2,2},{3,5},{4,4},{5,3},{6,6},{7,1},{8,8},{9,15},{10,1... | collective-permute-start | bytes 786440 | tf_op jit(solution)/shard_map/ppermute | solution.py:216
  36.0 10.7 %collective-permute-start.7 = (f32[64,1024]{1,0:T(8,128)S(1)}, f32[64,1024]{1,0:T(8,128)S(1)}, u32[]{:S(2)}, u32[]{:S(2)}) collective-permute-start(f32[64,1024]{1,0:T(8,128)S(1)} %add_add_fusion), channel_id=1, source_target_pairs={{0,2},{1,5},{2,0},{3,7},{4,6},{5,1},{6,4},{7,3},{8,10},{9,13},{10,... | collective-permute-start | bytes 786440 | tf_op jit(solution)/shard_map/ppermute | solution.py:216
  36.7 15.1 %collective-permute-start.11 = (f32[64,1024]{1,0:T(8,128)S(1)}, f32[64,1024]{1,0:T(8,128)S(1)}, u32[]{:S(2)}, u32[]{:S(2)}) collective-permute-start(f32[64,1024]{1,0:T(8,128)S(1)} %add_add_fusion), channel_id=1, source_target_pairs={{0,8},{1,17},{2,0},{3,25},{4,24},{5,1},{6,16},{7,9},{8,2},{9,27},{... | collective-permute-start | bytes 786440 | tf_op jit(solution)/shard_map/ppermute | solution.py:216
  39.5 15.3 %collective-permute-start.12 = (f32[64,1024]{1,0:T(8,128)S(1)}, f32[64,1024]{1,0:T(8,128)S(1)}, u32[]{:S(2)}, u32[]{:S(2)}) collective-permute-start(f32[64,1024]{1,0:T(8,128)S(1)} %add_add_fusion), channel_id=1, source_target_pairs={{0,0},{1,25},{2,8},{3,17},{4,16},{5,9},{6,24},{7,1},{8,10},{9,19},... | collective-permute-start | bytes 786440 | tf_op jit(solution)/shard_map/ppermute | solution.py:216
  46.7 8.4 %collective-permute-start.10 = (f32[64,1024]{1,0:T(8,128)S(1)}, f32[64,1024]{1,0:T(8,128)S(1)}, u32[]{:S(2)}, u32[]{:S(2)}) collective-permute-start(f32[64,1024]{1,0:T(8,128)S(1)} %collective-permute-done.8.refs_1_), channel_id=1, source_target_pairs={{0,1},{1,0},{2,3},{3,2},{4,5},{5,4},{6,7},{7,6},{8,9},{9,8},{10,11... | collective-permute-start | bytes 786440 | tf_op jit(solution)/shard_map/ppermute | solution.py:216
  46.8 8.4 %collective-permute-start.9 = (f32[64,1024]{1,0:T(8,128)S(1)}, f32[64,1024]{1,0:T(8,128)S(1)}, u32[]{:S(2)}, u32[]{:S(2)}) collective-permute-start(f32[64,1024]{1,0:T(8,128)S(1)} %collective-permute-done.7.refs_0_), channel_id=1, source_target_pairs={{0,1},{1,0},{2,3},{3,2},{4,5},{5,4},{6,7},{7,6},{8,9},{9,8},{10,11... | collective-permute-start | bytes 786440 | tf_op jit(solution)/shard_map/ppermute | solution.py:216
  51.8 3.6 %collective-permute-start.13 = (f32[64,1024]{1,0:T(8,128)S(1)}, f32[64,1024]{1,0:T(8,128)S(1)}, u32[]{:S(2)}, u32[]{:S(2)}) collective-permute-start(f32[64,1024]{1,0:T(8,128)S(1)} %collective-permute-done.11.refs_0_), channel_id=1, source_target_pairs={{0,1},{1,0},{2,3},{3,2},{4,5},{5,4},{6,7},{7,6},{8,9},{9,8},{10,11... | collective-permute-start | bytes 786440 | tf_op jit(solution)/shard_map/ppermute | solution.py:216
  54.8 1.5 %collective-permute-start.14 = (f32[64,1024]{1,0:T(8,128)S(1)}, f32[64,1024]{1,0:T(8,128)S(1)}, u32[]{:S(2)}, u32[]{:S(2)}) collective-permute-start(f32[64,1024]{1,0:T(8,128)S(1)} %collective-permute-done.12.refs_1_), channel_id=1, source_target_pairs={{0,1},{1,0},{2,3},{3,2},{4,5},{5,4},{6,7},{7,6},{8,9},{9,8},{10,11... | collective-permute-start | bytes 786440 | tf_op jit(solution)/shard_map/ppermute | solution.py:216

commit v4 on v3

v4 whole, which is shorter than its diff:
```python
import functools

import jax
import jax.numpy as jnp
from jax import lax
from jax.experimental import pallas as pl
from jax.experimental.pallas import tpu as pltpu
from jax.sharding import PartitionSpec as P

AXES = ("row", "col")
MIB = 1 << 20


def split(x):
    high = x.astype(jnp.bfloat16)
    low = (x - high.astype(jnp.float32)).astype(jnp.bfloat16)
    return high, low


def params(*arrays):
    held = sum(a.size * a.dtype.itemsize for a in arrays)
    return pltpu.CompilerParams(vmem_limit_bytes=2 * held + 4 * MIB)


def whole_specs(count):
    return [pl.BlockSpec(memory_space=pltpu.VMEM)] * count


def shape_of(shape, dtype=jnp.float32):
    return jax.ShapeDtypeStruct(shape, dtype)


def prepare_kernel(block_ref, high_ref, low_ref):
    high_ref[...], low_ref[...] = split(block_ref[...].T)


def prepare(block):
    tall, wide = block.shape
    step = min(256, tall)
    out = shape_of((wide, tall), jnp.bfloat16)
    out_spec = pl.BlockSpec((wide, step), lambda i: (0, i))
    return pl.pallas_call(
        prepare_kernel,
        out_shape=(out, out),
        grid=(tall // step,),
        in_specs=[pl.BlockSpec((step, wide), lambda i: (i, 0))],
        out_specs=[out_spec, out_spec],
        compiler_params=pltpu.CompilerParams(vmem_limit_bytes=step * wide * 32 + 4 * MIB),
        cost_estimate=pl.CostEstimate(flops=0, bytes_accessed=block.size * 8, transcendentals=0),
        name="prepare",
    )(block)


def contract_kernel(core, factors_ref, *refs):
    out_ref = refs[-1]
    rows = factors_ref.shape[0]
    parts = []
    for number, high_ref, low_ref in ((core[0], refs[0], refs[1]), (1 - core[0], refs[2], refs[3])):
        wide = high_ref.shape[0]
        high, low = split(factors_ref[:, pl.ds(pl.multiple_of(number * wide, wide), wide)])
        both = jnp.concatenate([high, low], axis=0)
        first = jnp.dot(both, high_ref[...], preferred_element_type=jnp.float32)
        second = jnp.dot(high, low_ref[...], preferred_element_type=jnp.float32)
        parts.append(first[:rows] + (first[rows:] + second))
    out_ref[...] = parts[0] + parts[1]


def contract(core, factors, own, sibling):
    wide, tall = own[0].shape
    out = shape_of((factors.shape[0], tall))
    arrays = [factors, *own, *sibling]
    return pl.pallas_call(
        contract_kernel,
        out_shape=out,
        in_specs=[pl.BlockSpec(memory_space=pltpu.SMEM)] + whole_specs(5),
        out_specs=whole_specs(1)[0],
        compiler_params=params(*arrays, out),
        cost_estimate=pl.CostEstimate(
            flops=12 * out.size * wide, bytes_accessed=own[0].size * 8, transcendentals=0
        ),
        name="contract",
    )(core.reshape(1), *arrays)


def pick(table, index):
    rows, lanes = table.shape
    length = index.shape[1]
    at_lane = lax.broadcasted_iota(jnp.int32, (lanes, length), 0) == index % lanes
    picked = jnp.dot(
        table,
        at_lane.astype(jnp.float32),
        precision=lax.Precision.HIGHEST,
        preferred_element_type=jnp.float32,
    )
    at_row = lax.broadcasted_iota(jnp.int32, (rows, length), 0) == index // lanes
    return jnp.sum(jnp.where(at_row, picked, 0.0), axis=0, keepdims=True)


def weight_kernel(place, occ_ref, vir_ref, occ_table, vir_table, out_ref):
    energies = []
    for number, length in enumerate(out_ref.shape):
        here = pl.ds(pl.multiple_of(place[number] * length, length), length)
        energies.append(pick(vir_table[...], vir_ref[:, here]) - pick(occ_table[...], occ_ref[:, here]))
    rows, cols = energies
    for start in range(0, out_ref.shape[0], 128):
        column = jnp.broadcast_to(rows[:, start : start + 128], (128, 128)).T
        wide = jnp.concatenate([column] * (out_ref.shape[1] // 128), axis=1)
        out_ref[pl.ds(start, 128), :] = -1.0 / (wide + cols)


def as_table(energies):
    lanes = 128
    padded = jnp.pad(energies, (0, -energies.shape[0] % lanes))
    return padded.reshape(-1, lanes)


def weights(place, occ_index, vir_index, occ_energy, vir_energy, rows, cols):
    occ_index, vir_index = occ_index[None, :], vir_index[None, :]
    occ_table, vir_table = as_table(occ_energy), as_table(vir_energy)
    out = shape_of((rows, cols))
    return pl.pallas_call(
        weight_kernel,
        out_shape=out,
        in_specs=[pl.BlockSpec(memory_space=pltpu.SMEM)] + whole_specs(4),
        out_specs=whole_specs(1)[0],
        compiler_params=pltpu.CompilerParams(vmem_limit_bytes=out.size * 4 + 8 * MIB),
        cost_estimate=pl.CostEstimate(flops=0, bytes_accessed=out.size * 4, transcendentals=0),
        name="weights",
    )(place, occ_index, vir_index, occ_table, vir_table)


def left_kernel(slots, *refs):
    high_ref, low_ref = refs[slots:]
    depth = refs[0].shape[0]
    step = 128 // depth
    for slot in range(0, slots, step):
        block = jnp.concatenate([refs[slot + k][...] for k in range(step)], axis=0).T
        high, low = split(block)
        here = pl.ds(slot * depth, step * depth)
        high_ref[:, here] = high
        low_ref[:, here] = low


def left_parts(left):
    slots = len(left)
    depth, total = left[0].shape
    out = shape_of((total, slots * depth), jnp.bfloat16)
    return pl.pallas_call(
        functools.partial(left_kernel, slots),
        out_shape=(out, out),
        in_specs=whole_specs(slots),
        out_specs=whole_specs(2),
        compiler_params=params(*left, out, out),
        cost_estimate=pl.CostEstimate(flops=0, bytes_accessed=out.size * 8, transcendentals=0),
        name="left_parts",
    )(*left)


CHUNKS = 4


def outer_kernel(slots, place, weights_ref, left_high, left_low, *refs):
    right = refs[:slots]
    out_ref, high_ref, low_ref, result_ref, sems = refs[slots:]
    depth = right[0].shape[0]
    total, wide = out_ref.shape
    mine = pl.ds(pl.multiple_of(place[0] * wide, wide), wide)
    for slot in range(slots):
        high, low = split(right[slot][:, mine])
        here = pl.ds(pl.multiple_of(place[1 + slot] * depth, depth), depth)
        high_ref[here, :] = high
        low_ref[here, :] = low
    tall = total // CHUNKS
    copies = []
    for chunk in range(CHUNKS):
        here = pl.ds(chunk * tall, tall)
        high, low = left_high[here, :], left_low[here, :]
        value = jnp.dot(low, high_ref[...], preferred_element_type=jnp.float32)
        value += jnp.dot(high, low_ref[...], preferred_element_type=jnp.float32)
        value += jnp.dot(high, high_ref[...], preferred_element_type=jnp.float32)
        result_ref[here, :] = value * weights_ref[here, :]
        copies.append(
            pltpu.make_async_copy(result_ref.at[here, :], out_ref.at[here, :], sems.at[chunk])
        )
        copies[-1].start()
    for copy in copies:
        copy.wait()


def outer(place, weights, left_high, left_low, right):
    slots = len(right)
    depth, total = right[0].shape
    wide = weights.shape[1]
    arrays = [weights, left_high, left_low, *right]
    out = shape_of((total, wide))
    parts = pltpu.VMEM((slots * depth, wide), jnp.bfloat16)
    return pl.pallas_call(
        functools.partial(outer_kernel, slots),
        out_shape=out,
        in_specs=[pl.BlockSpec(memory_space=pltpu.SMEM)] + whole_specs(len(arrays)),
        out_specs=pl.BlockSpec(memory_space=pl.ANY),
        scratch_shapes=[
            parts,
            parts,
            pltpu.VMEM((total, wide), jnp.float32),
            pltpu.SemaphoreType.DMA((CHUNKS,)),
        ],
        compiler_params=pltpu.CompilerParams(
            vmem_limit_bytes=sum(a.size * a.dtype.itemsize for a in arrays) + out.size * 8 + 8 * MIB
        ),
        cost_estimate=pl.CostEstimate(
            flops=6 * out.size * slots * depth, bytes_accessed=out.size * 4, transcendentals=0
        ),
        name="outer",
    )(place, *arrays)


def local(rows, cols, amplitudes, factors, occ_index, vir_index, occ_energy, vir_energy):
    cores = 2
    share = rows // cores
    chips = [(z, j, s) for z in range(rows) for j in range(rows) for s in range(cores)]

    def number(z, j, s):
        return z * cols + j * cores + s

    def turn(i, s):
        i = share - 1 - i
        return i if s == 0 else rows - 1 - i

    def move(x, to):
        return lax.ppermute(x, AXES, [(number(*at), number(*to(*at))) for at in chips])

    def swap(x):
        return move(x, lambda z, j, s: (z, j, 1 - s))

    def transposed(x, i):
        return move(x, lambda z, j, s: (j ^ z ^ turn(i, s), z, s))

    def reduced(x, i):
        return move(x, lambda z, j, s: (z, z ^ j ^ turn(i, s), s))

    def across(x, i):
        return move(x, lambda z, j, s: (z, j ^ turn(i, s), s))

    turns = range(share)
    row_index = lax.axis_index("row").astype(jnp.int32)
    col_index = lax.axis_index("col").astype(jnp.int32)
    core = col_index % cores
    tall, wide = amplitudes.shape

    def share_of(x):
        other = swap(x)
        return jnp.where(
            core == 0, jnp.concatenate([x, other], axis=0), jnp.concatenate([other, x], axis=0)
        )

    pieces = share_of(factors.T)
    received = [transposed(pieces, i) for i in turns]
    amplitudes, pieces = lax.optimization_barrier((amplitudes, pieces))
    blocks = prepare(amplitudes), prepare(swap(amplitudes))
    arrived = [reduced(contract(core, received[i], *blocks), i) for i in turns]
    total = functools.reduce(jnp.add, arrived)
    total = total + swap(total)
    total, occ_index, vir_index = lax.optimization_barrier((total, occ_index, vir_index))
    dressed = pieces + total
    factor = weights(
        jnp.stack([row_index, col_index]), occ_index, vir_index, occ_energy, vir_energy, tall, wide
    )
    right = [transposed(dressed, i) for i in turns]
    left = [across(dressed, i) for i in turns]
    right[0], left, factor = lax.optimization_barrier((right[0], left[::-1], factor))
    left = left[::-1]
    left += [swap(x) for x in left]
    right += [swap(x) for x in right]
    first = share - 1 - jnp.arange(share, dtype=jnp.int32)
    first = jnp.where(core == 0, first, rows - 1 - first)
    order = jnp.concatenate([first, rows - 1 - first])
    wanted = row_index ^ order
    at = jnp.sum(
        jnp.where(wanted[:, None] == order[None, :], jnp.arange(rows, dtype=jnp.int32)[None, :], 0), axis=1
    )
    place = jnp.concatenate([core[None], at]).astype(jnp.int32)
    left_high, left_low = left_parts(left)
    return outer(place, factor, left_high, left_low, right)


def solution(mesh):
    rows, cols = mesh.shape["row"], mesh.shape["col"]
    return jax.shard_map(
        functools.partial(local, rows, cols),
        mesh=mesh,
        in_specs=(P("row", "col"), P("row", "col"), P(), P(), P(), P()),
        out_specs=P("row", "col"),
        check_vma=False,
    )
```

time: 60.2 us -> 59.4 us (0.987)
  local copies, waits for them, and re-layouts: 4.38 us -> 1.62 us
  waiting for transfers between devices: 16.9 us -> 18.3 us
    unnamed x8 -> x10, local copies, waits for them, and re-layouts: 3.72 us -> 1.61 us
    ppermute x15, waiting for transfers between devices: 16.9 us -> 18.3 us  [move(): lax.ppermute(x, AXES, [(number(*at), number(*to(*at))) for at in chips])]
    reshape x1, local copies, waits for them, and re-layouts: 0.66 us -> 0.01 us  [as_table(): return padded.reshape(-1, lanes)]
    pallas_call x5 -> x6, Pallas kernels: 7.69 us -> 8.01 us  [the longest x1 2.44 us: outer(): pl.pallas_call(functools.partial(outer_kernel, slots), out_shape=out, in_...]
  transfers between devices with their start and end apart: 15 -> 15, of which waited for: 7 -> 9; matrix products, arithmetic and copies ran while one was open for 2% -> 1% of each run, Pallas kernels for 8% -> 10%
where the time goes in v4:
time: 59.4 us; the launch traced here: 59 us
  starting transfers between devices  28.9 us (49%)
  waiting for transfers between devices  18.3 us (31%)
  Pallas kernels  8.35 us (14%)
  local copies, waits for them, and re-layouts  1.62 us (3%)
  other arithmetic  1.53 us (3%)
    ppermute x15, starting transfers between devices, move(): lax.ppermute(x, AXES, [(number(*at), number(*to(*at))) for at in chips])  28.9 us
    ppermute x15, waiting for transfers between devices, move(): lax.ppermute(x, AXES, [(number(*at), number(*to(*at))) for at in chips])  18.3 us
    pallas_call x1, Pallas kernels, outer(): pl.pallas_call(functools.partial(outer_kernel, slots), out_shape=out, in_...  2.44 us
    pallas_call x2, Pallas kernels, prepare(): pl.pallas_call(prepare_kernel, out_shape=(out, out), grid=(tall // step,)...  2.2 us
    pallas_call x1, Pallas kernels, weights(): pl.pallas_call(weight_kernel, out_shape=out, in_specs=[pl.BlockSpec(memor...  1.81 us
    unnamed x10, local copies, waits for them, and re-layouts  1.61 us
    pallas_call x2, Pallas kernels, contract(): pl.pallas_call(contract_kernel, out_shape=out, in_specs=[pl.BlockSpec(mem...  1.56 us
  transfers between devices with their start and end apart: 15, of which 9 were waited for; matrix products, arithmetic and copies ran while one was open for 1% of the time, Pallas kernels for 10%

profile of v4, /device:TPU:5, one launch (start us, length us, event | category | flops | bytes accessed | tf_op | source)
XLA Modules:
  0.0 59.0 jit_solution(1021388031700367660)
XLA Ops:
  0.0 0.7 %collective-permute-start = (f32[32,1024]{1,0:T(8,128)}, f32[32,1024]{1,0:T(8,128)S(1)}, u32[]{:S(2)}, u32[]{:S(2)}) collective-permute-start(f32[32,1024]{1,0:T(8,128)} %bitcast.12), channel_id=1, source_target_pairs={{0,1},{1,0},{2,3},{3,2},{4,5},{5,4},{6,7},{7,6},{8,9},{9,8},{10,11... | collective-permute-start | bytes 393224 | tf_op jit(solution)/shard_map/ppermute | solution.py:231
  0.7 1.2 %collective-permute-done = f32[32,1024]{1,0:T(8,128)S(1)} collective-permute-done((f32[32,1024]{1,0:T(8,128)}, f32[32,1024]{1,0:T(8,128)S(1)}, u32[]{:S(2)}, u32[]{:S(2)}) %collective-permute-start) | collective-permute-done | bytes 131104 | tf_op jit(solution)/shard_map/ppermute | solution.py:231
  1.9 1.0 %maximum_select_fusion = f32[64,1024]{1,0:T(8,128)S(1)} fusion(f32[32,1024]{1,0:T(8,128)S(1)} %collective-permute-done, f32[32,1024]{1,0:T(8,128)} %bitcast.13, pred[]{:T(512)S(6)} %eq.10), kind=kLoop, calls=%fused_computation | loop fusion | flops 196608 | bytes 524289 | tf_op jit(solution)/shard_map/jit(_where)/select_n | solution.py:253
  2.9 0.4 collective-permute-start.2
  3.3 3.1 %collective-permute-start.4 = (f32[64,1024]{1,0:T(8,128)S(1)}, f32[64,1024]{1,0:T(8,128)S(1)}, u32[]{:S(2)}, u32[]{:S(2)}) collective-permute-start(f32[64,1024]{1,0:T(8,128)S(1)} %maximum_select_fusion), channel_id=1, source_target_pairs={{0,0},{1,25},{2,8},{3,17},{4,16},{5,9},{6,24},{7,1},{8,10},{9,19},... | collective-permute-start | bytes 786440 | tf_op jit(solution)/shard_map/ppermute | solution.py:231
  6.5 4.2 %collective-permute-start.1 = (f32[64,1024]{1,0:T(8,128)S(1)}, f32[64,1024]{1,0:T(8,128)S(1)}, u32[]{:S(2)}, u32[]{:S(2)}) collective-permute-start(f32[64,1024]{1,0:T(8,128)S(1)} %maximum_select_fusion), channel_id=1, source_target_pairs={{0,8},{1,17},{2,0},{3,25},{4,24},{5,1},{6,16},{7,9},{8,2},{9,27},{... | collective-permute-start | bytes 786440 | tf_op jit(solution)/shard_map/ppermute | solution.py:231
  10.7 0.0 copy-start
  10.7 1.6 %copy-done = f32[1024,512]{1,0:T(8,128)S(1)} copy-done((f32[1024,512]{1,0:T(8,128)S(1)}, f32[1024,512]{1,0:T(8,128)}, u32[]{:S(2)}) %copy-start) | copy-done | bytes 2097176
  12.3 1.1 %prepare.2 = (bf16[512,1024]{1,0:T(8,128)(2,1)S(1)}, bf16[512,1024]{1,0:T(8,128)(2,1)S(1)}) custom-call(f32[1024,512]{1,0:T(8,128)S(1)} %copy-done), custom_call_target="tpu_custom_call" | custom-call | bytes 4194304 | tf_op jit(solution)/shard_map/prepare/pallas_call | solution.py:42
  13.4 0.0 collective-permute-done.2.block_ref
  13.4 1.1 %prepare.3 = (bf16[512,1024]{1,0:T(8,128)(2,1)S(1)}, bf16[512,1024]{1,0:T(8,128)(2,1)S(1)}) custom-call(f32[1024,512]{1,0:T(8,128)S(1)} %collective-permute-done.2.block_ref), custom_call_target="tpu_custom_call" | custom-call | bytes 4194304 | tf_op jit(solution)/shard_map/prepare/pallas_call | solution.py:42
  14.5 1.2 %collective-permute-done.4.factors_ref = f32[64,1024]{1,0:T(8,128)S(1)} collective-permute-done((f32[64,1024]{1,0:T(8,128)S(1)}, f32[64,1024]{1,0:T(8,128)S(1)}, u32[]{:S(2)}, u32[]{:S(2)}) %collective-permute-start.4) | collective-permute-done | bytes 262176 | tf_op jit(solution)/shard_map/ppermute | solution.py:231
  15.6 0.8 %contract.3 = f32[64,1024]{1,0:T(8,128)S(1)} custom-call(s32[1]{0:T(128)} %bitcast.core, f32[64,1024]{1,0:T(8,128)S(1)} %collective-permute-done.4.factors_ref, bf16[512,1024]{1,0:T(8,128)(2,1)S(1)} %get-tuple-element.22.refs_0_, bf16[512,1024]{1,0:T(8,128)(2,1)S(1)} %get-tuple-element.23.refs_1_, bf16[512,1024]{1,0:T(8,128)(2,1)S(1)} %get-tuple-element.24.refs_2_, ...), custom_call_target="tpu_custom_call" | custom-call | flops 402653184 | bytes 4194304 | tf_op jit(solution)/shard_map/contract/pallas_call | solution.py:72
  16.4 3.5 %collective-permute-start.5 = (f32[64,1024]{1,0:T(8,128)S(1)}, f32[64,1024]{1,0:T(8,128)S(1)}, u32[]{:S(2)}, u32[]{:S(2)}) collective-permute-start(f32[64,1024]{1,0:T(8,128)S(1)} %contract.3), channel_id=1, source_target_pairs={{0,0},{1,7},{2,2},{3,5},{4,4},{5,3},{6,6},{7,1},{8,10},{9,13},{10,... | collective-permute-start | bytes 786440 | tf_op jit(solution)/shard_map/ppermute | solution.py:231
  19.9 1.1 %collective-permute-done.1.factors_ref = f32[64,1024]{1,0:T(8,128)S(1)} collective-permute-done((f32[64,1024]{1,0:T(8,128)S(1)}, f32[64,1024]{1,0:T(8,128)S(1)}, u32[]{:S(2)}, u32[]{:S(2)}) %collective-permute-start.1) | collective-permute-done | bytes 262176 | tf_op jit(solution)/shard_map/ppermute | solution.py:231
  21.0 0.8 %contract.2 = f32[64,1024]{1,0:T(8,128)S(1)} custom-call(s32[1]{0:T(128)} %bitcast.core, f32[64,1024]{1,0:T(8,128)S(1)} %collective-permute-done.1.factors_ref, bf16[512,1024]{1,0:T(8,128)(2,1)S(1)} %get-tuple-element.22.refs_0_, bf16[512,1024]{1,0:T(8,128)(2,1)S(1)} %get-tuple-element.23.refs_1_, bf16[512,1024]{1,0:T(8,128)(2,1)S(1)} %get-tuple-element.24.refs_2_, ...), custom_call_target="tpu_custom_call" | custom-call | flops 402653184 | bytes 4194304 | tf_op jit(solution)/shard_map/contract/pallas_call | solution.py:72
  21.8 0.0 copy-start.4
  21.8 0.0 copy-start.1
  21.9 0.0 copy-start.2
  21.9 0.0 copy-start.3
  21.9 2.1 %collective-permute-start.3 = (f32[64,1024]{1,0:T(8,128)S(1)}, f32[64,1024]{1,0:T(8,128)S(1)}, u32[]{:S(2)}, u32[]{:S(2)}) collective-permute-start(f32[64,1024]{1,0:T(8,128)S(1)} %contract.2), channel_id=1, source_target_pairs={{0,2},{1,5},{2,0},{3,7},{4,6},{5,1},{6,4},{7,3},{8,8},{9,15},{10,1... | collective-permute-start | bytes 786440 | tf_op jit(solution)/shard_map/ppermute | solution.py:231
  23.9 1.7 %collective-permute-done.5 = f32[64,1024]{1,0:T(8,128)S(1)} collective-permute-done((f32[64,1024]{1,0:T(8,128)S(1)}, f32[64,1024]{1,0:T(8,128)S(1)}, u32[]{:S(2)}, u32[]{:S(2)}) %collective-permute-start.5) | collective-permute-done | bytes 262176 | tf_op jit(solution)/shard_map/ppermute | solution.py:231
  25.6 3.8 %collective-permute-done.3 = f32[64,1024]{1,0:T(8,128)S(1)} collective-permute-done((f32[64,1024]{1,0:T(8,128)S(1)}, f32[64,1024]{1,0:T(8,128)S(1)}, u32[]{:S(2)}, u32[]{:S(2)}) %collective-permute-start.3) | collective-permute-done | bytes 262176 | tf_op jit(solution)/shard_map/ppermute | solution.py:231
  29.5 2.0 %collective-permute-start.6 = (f32[64,1024]{1,0:T(8,128)S(1)}, f32[64,1024]{1,0:T(8,128)S(1)}, u32[]{:S(2)}, u32[]{:S(2)}) collective-permute-start(f32[64,1024]{1,0:T(8,128)S(1)} %add.16), channel_id=1, source_target_pairs={{0,1},{1,0},{2,3},{3,2},{4,5},{5,4},{6,7},{7,6},{8,9},{9,8},{10,11... | collective-permute-start | bytes 786440 | tf_op jit(solution)/shard_map/ppermute | solution.py:231
  31.5 1.2 %collective-permute-done.6 = f32[64,1024]{1,0:T(8,128)S(1)} collective-permute-done((f32[64,1024]{1,0:T(8,128)S(1)}, f32[64,1024]{1,0:T(8,128)S(1)}, u32[]{:S(2)}, u32[]{:S(2)}) %collective-permute-start.6) | collective-permute-done | bytes 262176 | tf_op jit(solution)/shard_map/ppermute | solution.py:231
  32.7 1.9 %collective-permute-start.7 = (f32[64,1024]{1,0:T(8,128)S(1)}, f32[64,1024]{1,0:T(8,128)S(1)}, u32[]{:S(2)}, u32[]{:S(2)}) collective-permute-start(f32[64,1024]{1,0:T(8,128)S(1)} %add.18), channel_id=1, source_target_pairs={{0,8},{1,17},{2,0},{3,25},{4,24},{5,1},{6,16},{7,9},{8,2},{9,27},{... | collective-permute-start | bytes 786440 | tf_op jit(solution)/shard_map/ppermute | solution.py:231
  34.7 7.7 %collective-permute-start.8 = (f32[64,1024]{1,0:T(8,128)S(1)}, f32[64,1024]{1,0:T(8,128)S(1)}, u32[]{:S(2)}, u32[]{:S(2)}) collective-permute-start(f32[64,1024]{1,0:T(8,128)S(1)} %add.18), channel_id=1, source_target_pairs={{0,0},{1,7},{2,2},{3,5},{4,4},{5,3},{6,6},{7,1},{8,8},{9,15},{10,1... | collective-permute-start | bytes 786440 | tf_op jit(solution)/shard_map/ppermute | solution.py:231
  42.4 0.1 collective-permute-start.9
  42.5 2.5 %collective-permute-start.12 = (f32[64,1024]{1,0:T(8,128)S(1)}, f32[64,1024]{1,0:T(8,128)S(1)}, u32[]{:S(2)}, u32[]{:S(2)}) collective-permute-start(f32[64,1024]{1,0:T(8,128)S(1)} %add.18), channel_id=1, source_target_pairs={{0,0},{1,25},{2,8},{3,17},{4,16},{5,9},{6,24},{7,1},{8,10},{9,19},... | collective-permute-start | bytes 786440 | tf_op jit(solution)/shard_map/ppermute | solution.py:231
  44.9 0.0 copy-done.4
  45.0 0.1 pad_add_fusion.2.place
  45.0 0.0 copy-done.1
  45.0 0.0 copy-done.2
  45.0 0.0 copy-done.3
  45.1 1.8 %weights.1.weights_ref = f32[1024,512]{1,0:T(8,128)S(1)} custom-call(s32[2]{0:T(128)S(1)} %pad_add_fusion.2.place, s32[1,4096]{1,0:T(1,128)S(1)} %bitcast.9, s32[1,4096]{1,0:T(1,128)S(1)} %bitcast.10, f32[1,128]{1,0:T(1,128)S(1)} %pad_bitcast_fusion.occ_table, f32[16,128]{1,0:T(8,128)S(1)} %bitcast.11), custom_call_target="tpu_custom_call" | custom-call | bytes 2097152 | tf_op jit(solution)/shard_map/weights/pallas_call | solution.py:121
  46.9 0.0 collective-permute-done.7.refs_0_
  46.9 5.5 %collective-permute-done.8.refs_1_ = f32[64,1024]{1,0:T(8,128)S(1)} collective-permute-done((f32[64,1024]{1,0:T(8,128)S(1)}, f32[64,1024]{1,0:T(8,128)S(1)}, u32[]{:S(2)}, u32[]{:S(2)}) %collective-permute-start.8) | collective-permute-done | bytes 262176 | tf_op jit(solution)/shard_map/ppermute | solution.py:231
  52.4 0.0 collective-permute-done.9.refs_0_
  52.4 0.2 collective-permute-start.10
  52.6 0.3 collective-permute-start.11
  52.9 0.2 collective-permute-start.13
  53.1 1.9 %collective-permute-done.12.refs_1_ = f32[64,1024]{1,0:T(8,128)S(1)} collective-permute-done((f32[64,1024]{1,0:T(8,128)S(1)}, f32[64,1024]{1,0:T(8,128)S(1)}, u32[]{:S(2)}, u32[]{:S(2)}) %collective-permute-start.12) | collective-permute-done | bytes 262176 | tf_op jit(solution)/shard_map/ppermute | solution.py:231
  55.0 0.0 collective-permute-start.14
  55.0 0.1 broadcast_xor_fusion
  55.1 0.2 select_reduce_fusion
  55.3 0.1 pad_add_fusion.1.place
  55.3 0.0 collective-permute-done.10.refs_2_
  55.4 0.0 collective-permute-done.11.refs_3_
  55.4 0.3 left_parts.1
  55.7 0.0 collective-permute-done.13.refs_2_
  55.7 0.8 %collective-permute-done.14.refs_3_ = f32[64,1024]{1,0:T(8,128)S(1)} collective-permute-done((f32[64,1024]{1,0:T(8,128)S(1)}, f32[64,1024]{1,0:T(8,128)S(1)}, u32[]{:S(2)}, u32[]{:S(2)}) %collective-permute-start.14) | collective-permute-done | bytes 262176 | tf_op jit(solution)/shard_map/ppermute | solution.py:231
  56.5 2.4 %outer.1 = f32[1024,512]{1,0:T(8,128)} custom-call(s32[5]{0:T(128)S(1)} %pad_add_fusion.1.place, f32[1024,512]{1,0:T(8,128)S(1)} %weights.1.weights_ref, bf16[1024,256]{1,0:T(8,128)(2,1)S(1)} %get-tuple-element.32.left_high, bf16[1024,256]{1,0:T(8,128)(2,1)S(1)} %get-tuple-element.33.left_low, f32[64,1024]{1,0:T(8,128)S(1)} %collective-permute-done.7.refs_0_, ...), custom_call_target="tpu_custom_call" | custom-call | flops 805306368 | bytes 2097152 | tf_op jit(solution)/shard_map/outer/pallas_call | solution.py:197
  (5 shorter events, 0.1 us)
Async XLA Ops:
  0.0 1.9 %collective-permute-start = (f32[32,1024]{1,0:T(8,128)}, f32[32,1024]{1,0:T(8,128)S(1)}, u32[]{:S(2)}, u32[]{:S(2)}) collective-permute-start(f32[32,1024]{1,0:T(8,128)} %bitcast.12), channel_id=1, source_target_pairs={{0,1},{1,0},{2,3},{3,2},{4,5},{5,4},{6,7},{7,6},{8,9},{9,8},{10,11... | collective-permute-start | bytes 393224 | tf_op jit(solution)/shard_map/ppermute | solution.py:231
  2.9 10.5 %collective-permute-start.2 = (f32[1024,512]{1,0:T(8,128)}, f32[1024,512]{1,0:T(8,128)S(1)}, u32[]{:S(2)}, u32[]{:S(2)}) collective-permute-start(f32[1024,512]{1,0:T(8,128)} %block_ref), channel_id=1, source_target_pairs={{0,1},{1,0},{2,3},{3,2},{4,5},{5,4},{6,7},{7,6},{8,9},{9,8},{10,11... | collective-permute-start | bytes 6291464 | tf_op jit(solution)/shard_map/ppermute | solution.py:231
  3.3 12.3 %collective-permute-start.4 = (f32[64,1024]{1,0:T(8,128)S(1)}, f32[64,1024]{1,0:T(8,128)S(1)}, u32[]{:S(2)}, u32[]{:S(2)}) collective-permute-start(f32[64,1024]{1,0:T(8,128)S(1)} %maximum_select_fusion), channel_id=1, source_target_pairs={{0,0},{1,25},{2,8},{3,17},{4,16},{5,9},{6,24},{7,1},{8,10},{9,19},... | collective-permute-start | bytes 786440 | tf_op jit(solution)/shard_map/ppermute | solution.py:231
  6.5 14.6 %collective-permute-start.1 = (f32[64,1024]{1,0:T(8,128)S(1)}, f32[64,1024]{1,0:T(8,128)S(1)}, u32[]{:S(2)}, u32[]{:S(2)}) collective-permute-start(f32[64,1024]{1,0:T(8,128)S(1)} %maximum_select_fusion), channel_id=1, source_target_pairs={{0,8},{1,17},{2,0},{3,25},{4,24},{5,1},{6,16},{7,9},{8,2},{9,27},{... | collective-permute-start | bytes 786440 | tf_op jit(solution)/shard_map/ppermute | solution.py:231
  10.7 1.6 %copy-start = (f32[1024,512]{1,0:T(8,128)S(1)}, f32[1024,512]{1,0:T(8,128)}, u32[]{:S(2)}) copy-start(f32[1024,512]{1,0:T(8,128)} %block_ref) | copy-start | bytes 6291460
  16.4 9.2 %collective-permute-start.5 = (f32[64,1024]{1,0:T(8,128)S(1)}, f32[64,1024]{1,0:T(8,128)S(1)}, u32[]{:S(2)}, u32[]{:S(2)}) collective-permute-start(f32[64,1024]{1,0:T(8,128)S(1)} %contract.3), channel_id=1, source_target_pairs={{0,0},{1,7},{2,2},{3,5},{4,4},{5,3},{6,6},{7,1},{8,10},{9,13},{10,... | collective-permute-start | bytes 786440 | tf_op jit(solution)/shard_map/ppermute | solution.py:231
  21.8 23.1 %copy-start.4 = (f32[64]{0:T(128)S(1)}, f32[64]{0:T(128)}, u32[]{:S(2)}) copy-start(f32[64]{0:T(128)} %param.10) | copy-start | bytes 772
  21.8 23.2 %copy-start.1 = (s32[4096]{0:T(1024)S(1)}, s32[4096]{0:T(1024)}, u32[]{:S(2)}) copy-start(s32[4096]{0:T(1024)} %param.8) | copy-start | bytes 49156
  21.9 23.2 %copy-start.2 = (s32[4096]{0:T(1024)S(1)}, s32[4096]{0:T(1024)}, u32[]{:S(2)}) copy-start(s32[4096]{0:T(1024)} %param.9) | copy-start | bytes 49156
  21.9 23.2 %copy-start.3 = (f32[2048]{0:T(1024)S(1)}, f32[2048]{0:T(1024)}, u32[]{:S(2)}) copy-start(f32[2048]{0:T(1024)} %param.11) | copy-start | bytes 24580
  21.9 7.5 %collective-permute-start.3 = (f32[64,1024]{1,0:T(8,128)S(1)}, f32[64,1024]{1,0:T(8,128)S(1)}, u32[]{:S(2)}, u32[]{:S(2)}) collective-permute-start(f32[64,1024]{1,0:T(8,128)S(1)} %contract.2), channel_id=1, source_target_pairs={{0,2},{1,5},{2,0},{3,7},{4,6},{5,1},{6,4},{7,3},{8,8},{9,15},{10,1... | collective-permute-start | bytes 786440 | tf_op jit(solution)/shard_map/ppermute | solution.py:231
  29.5 3.2 %collective-permute-start.6 = (f32[64,1024]{1,0:T(8,128)S(1)}, f32[64,1024]{1,0:T(8,128)S(1)}, u32[]{:S(2)}, u32[]{:S(2)}) collective-permute-start(f32[64,1024]{1,0:T(8,128)S(1)} %add.16), channel_id=1, source_target_pairs={{0,1},{1,0},{2,3},{3,2},{4,5},{5,4},{6,7},{7,6},{8,9},{9,8},{10,11... | collective-permute-start | bytes 786440 | tf_op jit(solution)/shard_map/ppermute | solution.py:231
  32.7 14.1 %collective-permute-start.7 = (f32[64,1024]{1,0:T(8,128)S(1)}, f32[64,1024]{1,0:T(8,128)S(1)}, u32[]{:S(2)}, u32[]{:S(2)}) collective-permute-start(f32[64,1024]{1,0:T(8,128)S(1)} %add.18), channel_id=1, source_target_pairs={{0,8},{1,17},{2,0},{3,25},{4,24},{5,1},{6,16},{7,9},{8,2},{9,27},{... | collective-permute-start | bytes 786440 | tf_op jit(solution)/shard_map/ppermute | solution.py:231
  34.7 17.7 %collective-permute-start.8 = (f32[64,1024]{1,0:T(8,128)S(1)}, f32[64,1024]{1,0:T(8,128)S(1)}, u32[]{:S(2)}, u32[]{:S(2)}) collective-permute-start(f32[64,1024]{1,0:T(8,128)S(1)} %add.18), channel_id=1, source_target_pairs={{0,0},{1,7},{2,2},{3,5},{4,4},{5,3},{6,6},{7,1},{8,8},{9,15},{10,1... | collective-permute-start | bytes 786440 | tf_op jit(solution)/shard_map/ppermute | solution.py:231
  42.4 10.0 %collective-permute-start.9 = (f32[64,1024]{1,0:T(8,128)S(1)}, f32[64,1024]{1,0:T(8,128)S(1)}, u32[]{:S(2)}, u32[]{:S(2)}) collective-permute-start(f32[64,1024]{1,0:T(8,128)S(1)} %add.18), channel_id=1, source_target_pairs={{0,2},{1,5},{2,0},{3,7},{4,6},{5,1},{6,4},{7,3},{8,10},{9,13},{10,... | collective-permute-start | bytes 786440 | tf_op jit(solution)/shard_map/ppermute | solution.py:231
  42.5 12.6 %collective-permute-start.12 = (f32[64,1024]{1,0:T(8,128)S(1)}, f32[64,1024]{1,0:T(8,128)S(1)}, u32[]{:S(2)}, u32[]{:S(2)}) collective-permute-start(f32[64,1024]{1,0:T(8,128)S(1)} %add.18), channel_id=1, source_target_pairs={{0,0},{1,25},{2,8},{3,17},{4,16},{5,9},{6,24},{7,1},{8,10},{9,19},... | collective-permute-start | bytes 786440 | tf_op jit(solution)/shard_map/ppermute | solution.py:231
  52.4 3.0 %collective-permute-start.10 = (f32[64,1024]{1,0:T(8,128)S(1)}, f32[64,1024]{1,0:T(8,128)S(1)}, u32[]{:S(2)}, u32[]{:S(2)}) collective-permute-start(f32[64,1024]{1,0:T(8,128)S(1)} %collective-permute-done.9.refs_0_), channel_id=1, source_target_pairs={{0,1},{1,0},{2,3},{3,2},{4,5},{5,4},{6,7},{7,6},{8,9},{9,8},{10,11... | collective-permute-start | bytes 786440 | tf_op jit(solution)/shard_map/ppermute | solution.py:231
  52.6 2.8 %collective-permute-start.11 = (f32[64,1024]{1,0:T(8,128)S(1)}, f32[64,1024]{1,0:T(8,128)S(1)}, u32[]{:S(2)}, u32[]{:S(2)}) collective-permute-start(f32[64,1024]{1,0:T(8,128)S(1)} %collective-permute-done.8.refs_1_), channel_id=1, source_target_pairs={{0,1},{1,0},{2,3},{3,2},{4,5},{5,4},{6,7},{7,6},{8,9},{9,8},{10,11... | collective-permute-start | bytes 786440 | tf_op jit(solution)/shard_map/ppermute | solution.py:231
  52.9 2.8 %collective-permute-start.13 = (f32[64,1024]{1,0:T(8,128)S(1)}, f32[64,1024]{1,0:T(8,128)S(1)}, u32[]{:S(2)}, u32[]{:S(2)}) collective-permute-start(f32[64,1024]{1,0:T(8,128)S(1)} %collective-permute-done.7.refs_0_), channel_id=1, source_target_pairs={{0,1},{1,0},{2,3},{3,2},{4,5},{5,4},{6,7},{7,6},{8,9},{9,8},{10,11... | collective-permute-start | bytes 786440 | tf_op jit(solution)/shard_map/ppermute | solution.py:231
  55.0 1.5 %collective-permute-start.14 = (f32[64,1024]{1,0:T(8,128)S(1)}, f32[64,1024]{1,0:T(8,128)S(1)}, u32[]{:S(2)}, u32[]{:S(2)}) collective-permute-start(f32[64,1024]{1,0:T(8,128)S(1)} %collective-permute-done.12.refs_1_), channel_id=1, source_target_pairs={{0,1},{1,0},{2,3},{3,2},{4,5},{5,4},{6,7},{7,6},{8,9},{9,8},{10,11... | collective-permute-start | bytes 786440 | tf_op jit(solution)/shard_map/ppermute | solution.py:231

commit v5 on v4

--- a/solution.py
+++ b/solution.py
@@ -51,35 +51,64 @@
     )(block)
 
 
-def contract_kernel(core, factors_ref, *refs):
-    out_ref = refs[-1]
-    rows = factors_ref.shape[0]
-    parts = []
-    for number, high_ref, low_ref in ((core[0], refs[0], refs[1]), (1 - core[0], refs[2], refs[3])):
+def contract_kernel(slots, place, *refs):
+    factors, blocks = refs[:slots], refs[slots : slots + 4]
+    outs = refs[slots + 4 : 2 * slots + 4]
+    both_ref = refs[-1]
+    depth = factors[0].shape[0]
+    rows = slots * depth
+    for slot in range(slots):
+        high, low = split(factors[slot][...])
+        both_ref[pl.ds(pl.multiple_of(place[1 + slot] * depth, depth), depth), :] = high
+        both_ref[pl.ds(pl.multiple_of(rows + place[1 + slot] * depth, depth), depth), :] = low
+    total = None
+    for number, high_ref, low_ref in ((place[0], *blocks[:2]), (1 - place[0], *blocks[2:])):
         wide = high_ref.shape[0]
-        high, low = split(factors_ref[:, pl.ds(pl.multiple_of(number * wide, wide), wide)])
-        both = jnp.concatenate([high, low], axis=0)
-        first = jnp.dot(both, high_ref[...], preferred_element_type=jnp.float32)
-        second = jnp.dot(high, low_ref[...], preferred_element_type=jnp.float32)
-        parts.append(first[:rows] + (first[rows:] + second))
-    out_ref[...] = parts[0] + parts[1]
-
-
-def contract(core, factors, own, sibling):
-    wide, tall = own[0].shape
-    out = shape_of((factors.shape[0], tall))
-    arrays = [factors, *own, *sibling]
-    return pl.pallas_call(
-        contract_kernel,
-        out_shape=out,
-        in_specs=[pl.BlockSpec(memory_space=pltpu.SMEM)] + whole_specs(5),
-        out_specs=whole_specs(1)[0],
-        compiler_params=params(*arrays, out),
+        here = pl.ds(pl.multiple_of(number * wide, wide), wide)
+        first = jnp.dot(both_ref[:, here], high_ref[...], preferred_element_type=jnp.float32)
+        second = jnp.dot(both_ref[:rows, here], low_ref[...], preferred_element_type=jnp.float32)
+        part = first[:rows] + (first[rows:] + second)
+        total = part if total is None else total + part
+    for slot in range(slots):
+        outs[slot][...] = total[slot * depth : (slot + 1) * depth]
+
+
+def contract(place, factors, own, sibling):
+    slots = len(factors)
+    depth, length = factors[0].shape
+    tall = own[0].shape[1]
+    out = shape_of((depth, tall))
+    both = shape_of((2 * slots * depth, length), jnp.bfloat16)
+    arrays = [*factors, *own, *sibling]
+    return pl.pallas_call(
+        functools.partial(contract_kernel, slots),
+        out_shape=[out] * slots,
+        in_specs=[pl.BlockSpec(memory_space=pltpu.SMEM)] + whole_specs(len(arrays)),
+        out_specs=whole_specs(slots),
+        scratch_shapes=[pltpu.VMEM(both.shape, both.dtype)],
+        compiler_params=params(*arrays, both, *[out] * slots * 4),
         cost_estimate=pl.CostEstimate(
-            flops=12 * out.size * wide, bytes_accessed=own[0].size * 8, transcendentals=0
+            flops=6 * slots * out.size * length, bytes_accessed=own[0].size * 8, transcendentals=0
         ),
         name="contract",
-    )(core.reshape(1), *arrays)
+    )(place, *arrays)
+
+
+def fetch_kernel(x_ref, out_ref):
+    out_ref[...] = x_ref[...]
+
+
+def fetch(x):
+    return pl.pallas_call(
+        fetch_kernel,
+        out_shape=shape_of(x.shape),
+        grid=(1,),
+        in_specs=[pl.BlockSpec(x.shape, lambda i: (0, 0))],
+        out_specs=pl.BlockSpec(memory_space=pltpu.VMEM),
+        compiler_params=params(x, x),
+        cost_estimate=pl.CostEstimate(flops=0, bytes_accessed=x.size * 8, transcendentals=0),
+        name="fetch",
+    )(x)
 
 
 def pick(table, index):
@@ -156,7 +185,7 @@
     )(*left)
 
 
-CHUNKS = 4
+CHUNKS = 2
 
 
 def outer_kernel(slots, place, weights_ref, left_high, left_low, *refs):
@@ -170,17 +199,16 @@
         here = pl.ds(pl.multiple_of(place[1 + slot] * depth, depth), depth)
         high_ref[here, :] = high
         low_ref[here, :] = low
-    tall = total // CHUNKS
+    step = wide // CHUNKS
     copies = []
     for chunk in range(CHUNKS):
-        here = pl.ds(chunk * tall, tall)
-        high, low = left_high[here, :], left_low[here, :]
-        value = jnp.dot(low, high_ref[...], preferred_element_type=jnp.float32)
-        value += jnp.dot(high, low_ref[...], preferred_element_type=jnp.float32)
-        value += jnp.dot(high, high_ref[...], preferred_element_type=jnp.float32)
-        result_ref[here, :] = value * weights_ref[here, :]
+        here = pl.ds(chunk * step, step)
+        value = jnp.dot(left_low[...], high_ref[:, here], preferred_element_type=jnp.float32)
+        value += jnp.dot(left_high[...], low_ref[:, here], preferred_element_type=jnp.float32)
+        value += jnp.dot(left_high[...], high_ref[:, here], preferred_element_type=jnp.float32)
+        result_ref[:, here] = value * weights_ref[:, here]
         copies.append(
-            pltpu.make_async_copy(result_ref.at[here, :], out_ref.at[here, :], sems.at[chunk])
+            pltpu.make_async_copy(result_ref.at[:, here], out_ref.at[:, here], sems.at[chunk])
         )
         copies[-1].start()
     for copy in copies:
@@ -224,7 +252,6 @@
         return z * cols + j * cores + s
 
     def turn(i, s):
-        i = share - 1 - i
         return i if s == 0 else rows - 1 - i
 
     def move(x, to):
@@ -236,8 +263,12 @@
     def transposed(x, i):
         return move(x, lambda z, j, s: (j ^ z ^ turn(i, s), z, s))
 
-    def reduced(x, i):
-        return move(x, lambda z, j, s: (z, z ^ j ^ turn(i, s), s))
+    def reduced(x, k):
+        def to(z, j, s):
+            upper = z // share ^ s
+            return z, j ^ (upper * share + (share - 1 - k if upper else k)), s
+
+        return move(x, to)
 
     def across(x, i):
         return move(x, lambda z, j, s: (z, j ^ turn(i, s), s))
@@ -248,17 +279,24 @@
     core = col_index % cores
     tall, wide = amplitudes.shape
 
-    def share_of(x):
+    def share_of(x, mine):
         other = swap(x)
         return jnp.where(
-            core == 0, jnp.concatenate([x, other], axis=0), jnp.concatenate([other, x], axis=0)
+            core == 0, jnp.concatenate([mine, other], axis=0), jnp.concatenate([other, mine], axis=0)
         )
 
-    pieces = share_of(factors.T)
+    first = jnp.arange(share, dtype=jnp.int32)
+    mirror = share - 1 - first
+    low = row_index % share ^ jnp.where(core == 0, first, mirror)
+    low = jnp.where(row_index // share == core, low, share - 1 - low)
+    position = jnp.concatenate([core[None], low]).astype(jnp.int32)
+
+    pieces = share_of(factors.T, fetch(factors.T))
     received = [transposed(pieces, i) for i in turns]
     amplitudes, pieces = lax.optimization_barrier((amplitudes, pieces))
     blocks = prepare(amplitudes), prepare(swap(amplitudes))
-    arrived = [reduced(contract(core, received[i], *blocks), i) for i in turns]
+    partial = contract(position, received, *blocks)
+    arrived = [reduced(partial[k], k) for k in turns]
     total = functools.reduce(jnp.add, arrived)
     total = total + swap(total)
     total, occ_index, vir_index = lax.optimization_barrier((total, occ_index, vir_index))
@@ -268,11 +306,9 @@
     )
     right = [transposed(dressed, i) for i in turns]
     left = [across(dressed, i) for i in turns]
-    right[0], left, factor = lax.optimization_barrier((right[0], left[::-1], factor))
-    left = left[::-1]
+    right[0], left, factor = lax.optimization_barrier((right[0], left, factor))
     left += [swap(x) for x in left]
     right += [swap(x) for x in right]
-    first = share - 1 - jnp.arange(share, dtype=jnp.int32)
     first = jnp.where(core == 0, first, rows - 1 - first)
     order = jnp.concatenate([first, rows - 1 - first])
     wanted = row_index ^ order

time: 59.4 us -> 61.1 us (1.029)
  waiting for transfers between devices: 18.3 us -> 23.7 us
  starting transfers between devices: 28.9 us -> 24.4 us
  other arithmetic: 1.53 us -> 0.63 us
  local copies, waits for them, and re-layouts: 1.62 us -> 2.52 us
  Pallas kernels: 8.35 us -> 8.97 us
    ppermute x15, waiting for transfers between devices: 18.3 us -> 23.7 us  [move(): lax.ppermute(x, AXES, [(number(*at), number(*to(*at))) for at in chips])]
    ppermute x15, starting transfers between devices: 28.9 us -> 24.4 us  [move(): lax.ppermute(x, AXES, [(number(*at), number(*to(*at))) for at in chips])]
    select_n x1 -> x2, other arithmetic: 1 us -> 0.03 us  [the longest x1 0.02 us: share_of(): jnp.where(core == 0, jnp.concatenate([mine, other], axis=0), jnp.concaten...]
    unnamed x10 -> x12, local copies, waits for them, and re-layouts: 1.61 us -> 2.52 us
  transfers between devices with their start and end apart: 15 -> 15, of which waited for: 9 -> 11; matrix products, arithmetic and copies ran while one was open for 1% -> 1% of each run, Pallas kernels for 10% -> 7%
where the time goes in v5:
time: 61.1 us; the launch traced here: 60.5 us
  starting transfers between devices  24.4 us (40%)
  waiting for transfers between devices  23.7 us (39%)
  Pallas kernels  8.97 us (15%)
  local copies, waits for them, and re-layouts  2.52 us (4%)
  other arithmetic  0.63 us (1%)
    ppermute x15, starting transfers between devices, move(): lax.ppermute(x, AXES, [(number(*at), number(*to(*at))) for at in chips])  24.4 us
    ppermute x15, waiting for transfers between devices, move(): lax.ppermute(x, AXES, [(number(*at), number(*to(*at))) for at in chips])  23.7 us
    pallas_call x1, Pallas kernels, outer(): pl.pallas_call(functools.partial(outer_kernel, slots), out_shape=out, in_...  2.99 us
    unnamed x12, local copies, waits for them, and re-layouts  2.52 us
    pallas_call x2, Pallas kernels, prepare(): pl.pallas_call(prepare_kernel, out_shape=(out, out), grid=(tall // step,)...  2.21 us
    pallas_call x1, Pallas kernels, weights(): pl.pallas_call(weight_kernel, out_shape=out, in_specs=[pl.BlockSpec(memor...  1.81 us
    pallas_call x1, Pallas kernels, contract(): pl.pallas_call(functools.partial(contract_kernel, slots), out_shape=[out]...  1.61 us
  transfers between devices with their start and end apart: 15, of which 11 were waited for; matrix products, arithmetic and copies ran while one was open for 1% of the time, Pallas kernels for 7%

profile of v5, /device:TPU:5, one launch (start us, length us, event | category | flops | bytes accessed | tf_op | source)
XLA Modules:
  0.0 60.5 jit_solution(9098208471289910283)
XLA Ops:
  0.0 0.7 %collective-permute-start = (f32[32,1024]{1,0:T(8,128)}, f32[32,1024]{1,0:T(8,128)S(1)}, u32[]{:S(2)}, u32[]{:S(2)}) collective-permute-start(f32[32,1024]{1,0:T(8,128)} %bitcast.9), channel_id=1, source_target_pairs={{0,1},{1,0},{2,3},{3,2},{4,5},{5,4},{6,7},{7,6},{8,9},{9,8},{10,11... | collective-permute-start | bytes 393224 | tf_op jit(solution)/shard_map/ppermute | solution.py:258
  0.7 0.0 copy-start.1
  0.7 0.9 %copy-done.1 = f32[1024,32]{0,1:T(8,128)S(1)} copy-done((f32[1024,32]{0,1:T(8,128)S(1)}, f32[1024,32]{0,1:T(8,128)}, u32[]{:S(2)}) %copy-start.1) | copy-done | bytes 131096
  1.6 0.3 collective-permute-done
  1.9 0.4 collective-permute-start.3
  2.3 3.1 %collective-permute-start.1 = (f32[64,1024]{1,0:T(8,128)S(1)}, f32[64,1024]{1,0:T(8,128)S(1)}, u32[]{:S(2)}, u32[]{:S(2)}) collective-permute-start(f32[64,1024]{1,0:T(8,128)S(1)} %maximum_select_fusion), channel_id=1, source_target_pairs={{0,0},{1,25},{2,8},{3,17},{4,16},{5,9},{6,24},{7,1},{8,10},{9,19},... | collective-permute-start | bytes 786440 | tf_op jit(solution)/shard_map/ppermute | solution.py:258
  5.5 4.2 %collective-permute-start.2 = (f32[64,1024]{1,0:T(8,128)S(1)}, f32[64,1024]{1,0:T(8,128)S(1)}, u32[]{:S(2)}, u32[]{:S(2)}) collective-permute-start(f32[64,1024]{1,0:T(8,128)S(1)} %maximum_select_fusion), channel_id=1, source_target_pairs={{0,8},{1,17},{2,0},{3,25},{4,24},{5,1},{6,16},{7,9},{8,2},{9,27},{... | collective-permute-start | bytes 786440 | tf_op jit(solution)/shard_map/ppermute | solution.py:258
  9.7 0.1 pad_add_fusion.2.place
  9.8 0.0 copy-start
  9.8 1.6 %copy-done = f32[1024,512]{1,0:T(8,128)S(1)} copy-done((f32[1024,512]{1,0:T(8,128)S(1)}, f32[1024,512]{1,0:T(8,128)}, u32[]{:S(2)}) %copy-start) | copy-done | bytes 2097176
  11.4 1.1 %prepare.2 = (bf16[512,1024]{1,0:T(8,128)(2,1)S(1)}, bf16[512,1024]{1,0:T(8,128)(2,1)S(1)}) custom-call(f32[1024,512]{1,0:T(8,128)S(1)} %copy-done), custom_call_target="tpu_custom_call" | custom-call | bytes 4194304 | tf_op jit(solution)/shard_map/prepare/pallas_call | solution.py:42
  12.5 0.0 collective-permute-done.3.block_ref
  12.5 1.1 %prepare.3 = (bf16[512,1024]{1,0:T(8,128)(2,1)S(1)}, bf16[512,1024]{1,0:T(8,128)(2,1)S(1)}) custom-call(f32[1024,512]{1,0:T(8,128)S(1)} %collective-permute-done.3.block_ref), custom_call_target="tpu_custom_call" | custom-call | bytes 4194304 | tf_op jit(solution)/shard_map/prepare/pallas_call | solution.py:42
  13.6 1.0 %collective-permute-done.1.refs_0_ = f32[64,1024]{1,0:T(8,128)S(1)} collective-permute-done((f32[64,1024]{1,0:T(8,128)S(1)}, f32[64,1024]{1,0:T(8,128)S(1)}, u32[]{:S(2)}, u32[]{:S(2)}) %collective-permute-start.1) | collective-permute-done | bytes 262176 | tf_op jit(solution)/shard_map/ppermute | solution.py:258
  14.7 5.4 %collective-permute-done.2.refs_1_ = f32[64,1024]{1,0:T(8,128)S(1)} collective-permute-done((f32[64,1024]{1,0:T(8,128)S(1)}, f32[64,1024]{1,0:T(8,128)S(1)}, u32[]{:S(2)}, u32[]{:S(2)}) %collective-permute-start.2) | collective-permute-done | bytes 262176 | tf_op jit(solution)/shard_map/ppermute | solution.py:258
  20.1 1.6 %contract.1 = (f32[64,1024]{1,0:T(8,128)S(1)}, f32[64,1024]{1,0:T(8,128)S(1)}) custom-call(s32[3]{0:T(128)S(1)} %pad_add_fusion.2.place, f32[64,1024]{1,0:T(8,128)S(1)} %collective-permute-done.1.refs_0_, f32[64,1024]{1,0:T(8,128)S(1)} %collective-permute-done.2.refs_1_, bf16[512,1024]{1,0:T(8,128)(2,1)S(1)} %get-tuple-element.24.refs_2_, ...), custom_call_target="tpu_custom_call" | custom-call | flops 805306368 | bytes 4194304 | tf_op jit(solution)/shard_map/contract/pallas_call | solution.py:83
  21.7 0.0 copy-start.5
  21.7 0.0 copy-start.2
  21.7 0.0 copy-start.3
  21.7 0.0 copy-start.4
  21.7 2.1 %collective-permute-start.4 = (f32[64,1024]{1,0:T(8,128)S(1)}, f32[64,1024]{1,0:T(8,128)S(1)}, u32[]{:S(2)}, u32[]{:S(2)}) collective-permute-start(f32[64,1024]{1,0:T(8,128)S(1)} %get-tuple-element.28), channel_id=1, source_target_pairs={{0,0},{1,7},{2,2},{3,5},{4,4},{5,3},{6,6},{7,1},{8,8},{9,15},{10,1... | collective-permute-start | bytes 786440 | tf_op jit(solution)/shard_map/ppermute | solution.py:258
  23.8 0.5 collective-permute-start.5
  24.3 5.7 %collective-permute-done.4 = f32[64,1024]{1,0:T(8,128)S(1)} collective-permute-done((f32[64,1024]{1,0:T(8,128)S(1)}, f32[64,1024]{1,0:T(8,128)S(1)}, u32[]{:S(2)}, u32[]{:S(2)}) %collective-permute-start.4) | collective-permute-done | bytes 262176 | tf_op jit(solution)/shard_map/ppermute | solution.py:258
  30.0 1.9 %collective-permute-done.5 = f32[64,1024]{1,0:T(8,128)S(1)} collective-permute-done((f32[64,1024]{1,0:T(8,128)S(1)}, f32[64,1024]{1,0:T(8,128)S(1)}, u32[]{:S(2)}, u32[]{:S(2)}) %collective-permute-start.5) | collective-permute-done | bytes 262176 | tf_op jit(solution)/shard_map/ppermute | solution.py:258
  31.9 0.1 collective-permute-start.6
  32.0 1.5 %collective-permute-done.6 = f32[64,1024]{1,0:T(8,128)S(1)} collective-permute-done((f32[64,1024]{1,0:T(8,128)S(1)}, f32[64,1024]{1,0:T(8,128)S(1)}, u32[]{:S(2)}, u32[]{:S(2)}) %collective-permute-start.6) | collective-permute-done | bytes 262176 | tf_op jit(solution)/shard_map/ppermute | solution.py:258
  33.6 2.1 %collective-permute-start.7 = (f32[64,1024]{1,0:T(8,128)S(1)}, f32[64,1024]{1,0:T(8,128)S(1)}, u32[]{:S(2)}, u32[]{:S(2)}) collective-permute-start(f32[64,1024]{1,0:T(8,128)S(1)} %add.23), channel_id=1, source_target_pairs={{0,0},{1,25},{2,8},{3,17},{4,16},{5,9},{6,24},{7,1},{8,10},{9,19},... | collective-permute-start | bytes 786440 | tf_op jit(solution)/shard_map/ppermute | solution.py:258
  35.7 6.7 %collective-permute-start.8 = (f32[64,1024]{1,0:T(8,128)S(1)}, f32[64,1024]{1,0:T(8,128)S(1)}, u32[]{:S(2)}, u32[]{:S(2)}) collective-permute-start(f32[64,1024]{1,0:T(8,128)S(1)} %add.23), channel_id=1, source_target_pairs={{0,0},{1,7},{2,2},{3,5},{4,4},{5,3},{6,6},{7,1},{8,8},{9,15},{10,1... | collective-permute-start | bytes 786440 | tf_op jit(solution)/shard_map/ppermute | solution.py:258
  42.5 0.1 collective-permute-start.9
  42.6 3.3 %collective-permute-start.12 = (f32[64,1024]{1,0:T(8,128)S(1)}, f32[64,1024]{1,0:T(8,128)S(1)}, u32[]{:S(2)}, u32[]{:S(2)}) collective-permute-start(f32[64,1024]{1,0:T(8,128)S(1)} %add.23), channel_id=1, source_target_pairs={{0,8},{1,17},{2,0},{3,25},{4,24},{5,1},{6,16},{7,9},{8,2},{9,27},{... | collective-permute-start | bytes 786440 | tf_op jit(solution)/shard_map/ppermute | solution.py:258
  45.9 0.0 copy-done.5
  45.9 0.1 pad_add_fusion.3.place
  46.0 0.0 copy-done.2
  46.0 0.0 copy-done.3
  46.0 0.0 copy-done.4
  46.0 1.8 %weights.1.weights_ref = f32[1024,512]{1,0:T(8,128)S(1)} custom-call(s32[2]{0:T(128)S(1)} %pad_add_fusion.3.place, s32[1,4096]{1,0:T(1,128)S(1)} %bitcast.11, s32[1,4096]{1,0:T(1,128)S(1)} %bitcast.12, f32[1,128]{1,0:T(1,128)S(1)} %pad_bitcast_fusion.occ_table, f32[16,128]{1,0:T(8,128)S(1)} %bitcast.13), custom_call_target="tpu_custom_call" | custom-call | bytes 2097152 | tf_op jit(solution)/shard_map/weights/pallas_call | solution.py:150
  47.9 0.0 collective-permute-done.7.refs_0_
  47.9 4.3 %collective-permute-done.8.refs_0_ = f32[64,1024]{1,0:T(8,128)S(1)} collective-permute-done((f32[64,1024]{1,0:T(8,128)S(1)}, f32[64,1024]{1,0:T(8,128)S(1)}, u32[]{:S(2)}, u32[]{:S(2)}) %collective-permute-start.8) | collective-permute-done | bytes 262176 | tf_op jit(solution)/shard_map/ppermute | solution.py:258
  52.2 2.6 %collective-permute-done.9.refs_1_ = f32[64,1024]{1,0:T(8,128)S(1)} collective-permute-done((f32[64,1024]{1,0:T(8,128)S(1)}, f32[64,1024]{1,0:T(8,128)S(1)}, u32[]{:S(2)}, u32[]{:S(2)}) %collective-permute-start.9) | collective-permute-done | bytes 262176 | tf_op jit(solution)/shard_map/ppermute | solution.py:258
  54.9 0.0 collective-permute-start.10
  54.9 0.5 collective-permute-start.11
  55.4 0.0 collective-permute-start.13
  55.4 0.0 collective-permute-done.12.refs_1_
  55.4 0.5 collective-permute-start.14
  55.9 0.1 broadcast_xor_fusion
  56.0 0.2 select_reduce_fusion
  56.1 0.1 pad_add_fusion.1.place
  56.2 0.2 collective-permute-done.10.refs_2_
  56.4 0.4 collective-permute-done.11.refs_3_
  56.8 0.3 left_parts.1
  57.1 0.0 collective-permute-done.13.refs_2_
  57.1 0.4 collective-permute-done.14.refs_3_
  57.5 3.0 %outer.1 = f32[1024,512]{1,0:T(8,128)} custom-call(s32[5]{0:T(128)S(1)} %pad_add_fusion.1.place, f32[1024,512]{1,0:T(8,128)S(1)} %weights.1.weights_ref, bf16[1024,256]{1,0:T(8,128)(2,1)S(1)} %get-tuple-element.36.left_high, bf16[1024,256]{1,0:T(8,128)(2,1)S(1)} %get-tuple-element.37.left_low, f32[64,1024]{1,0:T(8,128)S(1)} %collective-permute-done.7.refs_0_, ...), custom_call_target="tpu_custom_call" | custom-call | flops 805306368 | bytes 2097152 | tf_op jit(solution)/shard_map/outer/pallas_call | solution.py:225
  (8 shorter events, 0.1 us)
Async XLA Ops:
  0.0 1.9 %collective-permute-start = (f32[32,1024]{1,0:T(8,128)}, f32[32,1024]{1,0:T(8,128)S(1)}, u32[]{:S(2)}, u32[]{:S(2)}) collective-permute-start(f32[32,1024]{1,0:T(8,128)} %bitcast.9), channel_id=1, source_target_pairs={{0,1},{1,0},{2,3},{3,2},{4,5},{5,4},{6,7},{7,6},{8,9},{9,8},{10,11... | collective-permute-start | bytes 393224 | tf_op jit(solution)/shard_map/ppermute | solution.py:258
  0.7 0.9 %copy-start.1 = (f32[1024,32]{0,1:T(8,128)S(1)}, f32[1024,32]{0,1:T(8,128)}, u32[]{:S(2)}) copy-start(f32[1024,32]{0,1:T(8,128)} %param.7) | copy-start | bytes 393220
  1.9 10.6 %collective-permute-start.3 = (f32[1024,512]{1,0:T(8,128)}, f32[1024,512]{1,0:T(8,128)S(1)}, u32[]{:S(2)}, u32[]{:S(2)}) collective-permute-start(f32[1024,512]{1,0:T(8,128)} %block_ref), channel_id=1, source_target_pairs={{0,1},{1,0},{2,3},{3,2},{4,5},{5,4},{6,7},{7,6},{8,9},{9,8},{10,11... | collective-permute-start | bytes 6291464 | tf_op jit(solution)/shard_map/ppermute | solution.py:258
  2.3 12.3 %collective-permute-start.1 = (f32[64,1024]{1,0:T(8,128)S(1)}, f32[64,1024]{1,0:T(8,128)S(1)}, u32[]{:S(2)}, u32[]{:S(2)}) collective-permute-start(f32[64,1024]{1,0:T(8,128)S(1)} %maximum_select_fusion), channel_id=1, source_target_pairs={{0,0},{1,25},{2,8},{3,17},{4,16},{5,9},{6,24},{7,1},{8,10},{9,19},... | collective-permute-start | bytes 786440 | tf_op jit(solution)/shard_map/ppermute | solution.py:258
  5.5 14.6 %collective-permute-start.2 = (f32[64,1024]{1,0:T(8,128)S(1)}, f32[64,1024]{1,0:T(8,128)S(1)}, u32[]{:S(2)}, u32[]{:S(2)}) collective-permute-start(f32[64,1024]{1,0:T(8,128)S(1)} %maximum_select_fusion), channel_id=1, source_target_pairs={{0,8},{1,17},{2,0},{3,25},{4,24},{5,1},{6,16},{7,9},{8,2},{9,27},{... | collective-permute-start | bytes 786440 | tf_op jit(solution)/shard_map/ppermute | solution.py:258
  9.8 1.6 %copy-start = (f32[1024,512]{1,0:T(8,128)S(1)}, f32[1024,512]{1,0:T(8,128)}, u32[]{:S(2)}) copy-start(f32[1024,512]{1,0:T(8,128)} %block_ref) | copy-start | bytes 6291460
  21.7 24.2 %copy-start.5 = (f32[64]{0:T(128)S(1)}, f32[64]{0:T(128)}, u32[]{:S(2)}) copy-start(f32[64]{0:T(128)} %param.10) | copy-start | bytes 772
  21.7 24.3 %copy-start.2 = (s32[4096]{0:T(1024)S(1)}, s32[4096]{0:T(1024)}, u32[]{:S(2)}) copy-start(s32[4096]{0:T(1024)} %param.8) | copy-start | bytes 49156
  21.7 24.3 %copy-start.3 = (s32[4096]{0:T(1024)S(1)}, s32[4096]{0:T(1024)}, u32[]{:S(2)}) copy-start(s32[4096]{0:T(1024)} %param.9) | copy-start | bytes 49156
  21.7 24.3 %copy-start.4 = (f32[2048]{0:T(1024)S(1)}, f32[2048]{0:T(1024)}, u32[]{:S(2)}) copy-start(f32[2048]{0:T(1024)} %param.11) | copy-start | bytes 24580
  21.7 8.3 %collective-permute-start.4 = (f32[64,1024]{1,0:T(8,128)S(1)}, f32[64,1024]{1,0:T(8,128)S(1)}, u32[]{:S(2)}, u32[]{:S(2)}) collective-permute-start(f32[64,1024]{1,0:T(8,128)S(1)} %get-tuple-element.28), channel_id=1, source_target_pairs={{0,0},{1,7},{2,2},{3,5},{4,4},{5,3},{6,6},{7,1},{8,8},{9,15},{10,1... | collective-permute-start | bytes 786440 | tf_op jit(solution)/shard_map/ppermute | solution.py:258
  23.8 8.1 %collective-permute-start.5 = (f32[64,1024]{1,0:T(8,128)S(1)}, f32[64,1024]{1,0:T(8,128)S(1)}, u32[]{:S(2)}, u32[]{:S(2)}) collective-permute-start(f32[64,1024]{1,0:T(8,128)S(1)} %get-tuple-element.29), channel_id=1, source_target_pairs={{0,2},{1,5},{2,0},{3,7},{4,6},{5,1},{6,4},{7,3},{8,10},{9,13},{10,... | collective-permute-start | bytes 786440 | tf_op jit(solution)/shard_map/ppermute | solution.py:258
  31.9 1.6 %collective-permute-start.6 = (f32[64,1024]{1,0:T(8,128)S(1)}, f32[64,1024]{1,0:T(8,128)S(1)}, u32[]{:S(2)}, u32[]{:S(2)}) collective-permute-start(f32[64,1024]{1,0:T(8,128)S(1)} %add.21), channel_id=1, source_target_pairs={{0,1},{1,0},{2,3},{3,2},{4,5},{5,4},{6,7},{7,6},{8,9},{9,8},{10,11... | collective-permute-start | bytes 786440 | tf_op jit(solution)/shard_map/ppermute | solution.py:258
  33.6 14.3 %collective-permute-start.7 = (f32[64,1024]{1,0:T(8,128)S(1)}, f32[64,1024]{1,0:T(8,128)S(1)}, u32[]{:S(2)}, u32[]{:S(2)}) collective-permute-start(f32[64,1024]{1,0:T(8,128)S(1)} %add.23), channel_id=1, source_target_pairs={{0,0},{1,25},{2,8},{3,17},{4,16},{5,9},{6,24},{7,1},{8,10},{9,19},... | collective-permute-start | bytes 786440 | tf_op jit(solution)/shard_map/ppermute | solution.py:258
  35.7 16.5 %collective-permute-start.8 = (f32[64,1024]{1,0:T(8,128)S(1)}, f32[64,1024]{1,0:T(8,128)S(1)}, u32[]{:S(2)}, u32[]{:S(2)}) collective-permute-start(f32[64,1024]{1,0:T(8,128)S(1)} %add.23), channel_id=1, source_target_pairs={{0,0},{1,7},{2,2},{3,5},{4,4},{5,3},{6,6},{7,1},{8,8},{9,15},{10,1... | collective-permute-start | bytes 786440 | tf_op jit(solution)/shard_map/ppermute | solution.py:258
  42.5 12.4 %collective-permute-start.9 = (f32[64,1024]{1,0:T(8,128)S(1)}, f32[64,1024]{1,0:T(8,128)S(1)}, u32[]{:S(2)}, u32[]{:S(2)}) collective-permute-start(f32[64,1024]{1,0:T(8,128)S(1)} %add.23), channel_id=1, source_target_pairs={{0,2},{1,5},{2,0},{3,7},{4,6},{5,1},{6,4},{7,3},{8,10},{9,13},{10,... | collective-permute-start | bytes 786440 | tf_op jit(solution)/shard_map/ppermute | solution.py:258
  42.6 12.8 %collective-permute-start.12 = (f32[64,1024]{1,0:T(8,128)S(1)}, f32[64,1024]{1,0:T(8,128)S(1)}, u32[]{:S(2)}, u32[]{:S(2)}) collective-permute-start(f32[64,1024]{1,0:T(8,128)S(1)} %add.23), channel_id=1, source_target_pairs={{0,8},{1,17},{2,0},{3,25},{4,24},{5,1},{6,16},{7,9},{8,2},{9,27},{... | collective-permute-start | bytes 786440 | tf_op jit(solution)/shard_map/ppermute | solution.py:258
  54.9 1.5 %collective-permute-start.10 = (f32[64,1024]{1,0:T(8,128)S(1)}, f32[64,1024]{1,0:T(8,128)S(1)}, u32[]{:S(2)}, u32[]{:S(2)}) collective-permute-start(f32[64,1024]{1,0:T(8,128)S(1)} %collective-permute-done.8.refs_0_), channel_id=1, source_target_pairs={{0,1},{1,0},{2,3},{3,2},{4,5},{5,4},{6,7},{7,6},{8,9},{9,8},{10,11... | collective-permute-start | bytes 786440 | tf_op jit(solution)/shard_map/ppermute | solution.py:258
  54.9 1.9 %collective-permute-start.11 = (f32[64,1024]{1,0:T(8,128)S(1)}, f32[64,1024]{1,0:T(8,128)S(1)}, u32[]{:S(2)}, u32[]{:S(2)}) collective-permute-start(f32[64,1024]{1,0:T(8,128)S(1)} %collective-permute-done.9.refs_1_), channel_id=1, source_target_pairs={{0,1},{1,0},{2,3},{3,2},{4,5},{5,4},{6,7},{7,6},{8,9},{9,8},{10,11... | collective-permute-start | bytes 786440 | tf_op jit(solution)/shard_map/ppermute | solution.py:258
  55.4 1.8 %collective-permute-start.13 = (f32[64,1024]{1,0:T(8,128)S(1)}, f32[64,1024]{1,0:T(8,128)S(1)}, u32[]{:S(2)}, u32[]{:S(2)}) collective-permute-start(f32[64,1024]{1,0:T(8,128)S(1)} %collective-permute-done.7.refs_0_), channel_id=1, source_target_pairs={{0,1},{1,0},{2,3},{3,2},{4,5},{5,4},{6,7},{7,6},{8,9},{9,8},{10,11... | collective-permute-start | bytes 786440 | tf_op jit(solution)/shard_map/ppermute | solution.py:258
  55.4 2.1 %collective-permute-start.14 = (f32[64,1024]{1,0:T(8,128)S(1)}, f32[64,1024]{1,0:T(8,128)S(1)}, u32[]{:S(2)}, u32[]{:S(2)}) collective-permute-start(f32[64,1024]{1,0:T(8,128)S(1)} %collective-permute-done.12.refs_1_), channel_id=1, source_target_pairs={{0,1},{1,0},{2,3},{3,2},{4,5},{5,4},{6,7},{7,6},{8,9},{9,8},{10,11... | collective-permute-start | bytes 786440 | tf_op jit(solution)/shard_map/ppermute | solution.py:258

commit v6 on v4

--- a/solution.py
+++ b/solution.py
@@ -82,6 +82,23 @@
     )(core.reshape(1), *arrays)
 
 
+def fetch_kernel(x_ref, out_ref):
+    out_ref[...] = x_ref[...]
+
+
+def fetch(x):
+    return pl.pallas_call(
+        fetch_kernel,
+        out_shape=shape_of(x.shape),
+        grid=(1,),
+        in_specs=[pl.BlockSpec(x.shape, lambda i: (0, 0))],
+        out_specs=pl.BlockSpec(memory_space=pltpu.VMEM),
+        compiler_params=params(x, x),
+        cost_estimate=pl.CostEstimate(flops=0, bytes_accessed=x.size * 8, transcendentals=0),
+        name="fetch",
+    )(x)
+
+
 def pick(table, index):
     rows, lanes = table.shape
     length = index.shape[1]
@@ -156,57 +173,50 @@
     )(*left)
 
 
-CHUNKS = 4
-
-
 def outer_kernel(slots, place, weights_ref, left_high, left_low, *refs):
     right = refs[:slots]
-    out_ref, high_ref, low_ref, result_ref, sems = refs[slots:]
+    out_ref, high_ref, low_ref = refs[slots:]
     depth = right[0].shape[0]
-    total, wide = out_ref.shape
-    mine = pl.ds(pl.multiple_of(place[0] * wide, wide), wide)
-    for slot in range(slots):
-        high, low = split(right[slot][:, mine])
-        here = pl.ds(pl.multiple_of(place[1 + slot] * depth, depth), depth)
-        high_ref[here, :] = high
-        low_ref[here, :] = low
-    tall = total // CHUNKS
-    copies = []
-    for chunk in range(CHUNKS):
-        here = pl.ds(chunk * tall, tall)
-        high, low = left_high[here, :], left_low[here, :]
-        value = jnp.dot(low, high_ref[...], preferred_element_type=jnp.float32)
-        value += jnp.dot(high, low_ref[...], preferred_element_type=jnp.float32)
-        value += jnp.dot(high, high_ref[...], preferred_element_type=jnp.float32)
-        result_ref[here, :] = value * weights_ref[here, :]
-        copies.append(
-            pltpu.make_async_copy(result_ref.at[here, :], out_ref.at[here, :], sems.at[chunk])
-        )
-        copies[-1].start()
-    for copy in copies:
-        copy.wait()
+    tall, wide = out_ref.shape
+    step = pl.program_id(0)
+
+    @pl.when(step == 0)
+    def _():
+        mine = pl.ds(pl.multiple_of(place[0] * wide, wide), wide)
+        for slot in range(slots):
+            high, low = split(right[slot][:, mine])
+            here = pl.ds(pl.multiple_of(place[1 + slot] * depth, depth), depth)
+            high_ref[here, :] = high
+            low_ref[here, :] = low
+
+    here = pl.ds(pl.multiple_of(step * tall, tall), tall)
+    high, low = left_high[here, :], left_low[here, :]
+    value = jnp.dot(low, high_ref[...], preferred_element_type=jnp.float32)
+    value += jnp.dot(high, low_ref[...], preferred_element_type=jnp.float32)
+    value += jnp.dot(high, high_ref[...], preferred_element_type=jnp.float32)
+    out_ref[...] = value * weights_ref[here, :]
 
 
 def outer(place, weights, left_high, left_low, right):
     slots = len(right)
     depth, total = right[0].shape
     wide = weights.shape[1]
+    tall = min(1024, total)
     arrays = [weights, left_high, left_low, *right]
     out = shape_of((total, wide))
     parts = pltpu.VMEM((slots * depth, wide), jnp.bfloat16)
     return pl.pallas_call(
         functools.partial(outer_kernel, slots),
         out_shape=out,
-        in_specs=[pl.BlockSpec(memory_space=pltpu.SMEM)] + whole_specs(len(arrays)),
-        out_specs=pl.BlockSpec(memory_space=pl.ANY),
-        scratch_shapes=[
-            parts,
-            parts,
-            pltpu.VMEM((total, wide), jnp.float32),
-            pltpu.SemaphoreType.DMA((CHUNKS,)),
-        ],
+        grid_spec=pltpu.PrefetchScalarGridSpec(
+            num_scalar_prefetch=1,
+            grid=(total // tall,),
+            in_specs=whole_specs(len(arrays)),
+            out_specs=pl.BlockSpec((tall, wide), lambda step, place: (step, 0)),
+            scratch_shapes=[parts, parts],
+        ),
         compiler_params=pltpu.CompilerParams(
-            vmem_limit_bytes=sum(a.size * a.dtype.itemsize for a in arrays) + out.size * 8 + 8 * MIB
+            vmem_limit_bytes=sum(a.size * a.dtype.itemsize for a in arrays) + 20 * tall * wide + 4 * MIB
         ),
         cost_estimate=pl.CostEstimate(
             flops=6 * out.size * slots * depth, bytes_accessed=out.size * 4, transcendentals=0
@@ -224,7 +234,6 @@
         return z * cols + j * cores + s
 
     def turn(i, s):
-        i = share - 1 - i
         return i if s == 0 else rows - 1 - i
 
     def move(x, to):
@@ -248,17 +257,19 @@
     core = col_index % cores
     tall, wide = amplitudes.shape
 
-    def share_of(x):
+    def share_of(x, mine):
         other = swap(x)
         return jnp.where(
-            core == 0, jnp.concatenate([x, other], axis=0), jnp.concatenate([other, x], axis=0)
+            core == 0, jnp.concatenate([mine, other], axis=0), jnp.concatenate([other, mine], axis=0)
         )
 
-    pieces = share_of(factors.T)
+    first = jnp.arange(share, dtype=jnp.int32)
+    pieces = share_of(factors.T, fetch(factors.T))
     received = [transposed(pieces, i) for i in turns]
     amplitudes, pieces = lax.optimization_barrier((amplitudes, pieces))
     blocks = prepare(amplitudes), prepare(swap(amplitudes))
-    arrived = [reduced(contract(core, received[i], *blocks), i) for i in turns]
+    partial = [contract(core, x, *blocks) for x in received]
+    arrived = [reduced(partial[i], i) for i in turns]
     total = functools.reduce(jnp.add, arrived)
     total = total + swap(total)
     total, occ_index, vir_index = lax.optimization_barrier((total, occ_index, vir_index))
@@ -268,11 +279,10 @@
     )
     right = [transposed(dressed, i) for i in turns]
     left = [across(dressed, i) for i in turns]
-    right[0], left, factor = lax.optimization_barrier((right[0], left[::-1], factor))
-    left = left[::-1]
+    left[1], right[0], factor = lax.optimization_barrier((left[1], right[0], factor))
+    right[0], left[0] = lax.optimization_barrier((right[0], left[0]))
     left += [swap(x) for x in left]
     right += [swap(x) for x in right]
-    first = share - 1 - jnp.arange(share, dtype=jnp.int32)
     first = jnp.where(core == 0, first, rows - 1 - first)
     order = jnp.concatenate([first, rows - 1 - first])
     wanted = row_index ^ order

time: 59.4 us -> 57.9 us (0.975)
  the two profiles are of different devices: /device:TPU:5 before, /device:TPU:13 now
where the time goes in v6:
time: 57.9 us; the launch traced here: 57.5 us
  starting transfers between devices  28.1 us (49%)
  waiting for transfers between devices  17.3 us (30%)
  Pallas kernels  8.86 us (15%)
  local copies, waits for them, and re-layouts  2.52 us (4%)
    ppermute x15, starting transfers between devices, move(): lax.ppermute(x, AXES, [(number(*at), number(*to(*at))) for at in chips])  28.1 us
    ppermute x15, waiting for transfers between devices, move(): lax.ppermute(x, AXES, [(number(*at), number(*to(*at))) for at in chips])  17.3 us
    pallas_call x1, Pallas kernels, outer(): pl.pallas_call(functools.partial(outer_kernel, slots), out_shape=out, gri...  2.92 us
    unnamed x12, local copies, waits for them, and re-layouts  2.52 us
    pallas_call x2, Pallas kernels, prepare(): pl.pallas_call(prepare_kernel, out_shape=(out, out), grid=(tall // step,)...  2.2 us
    pallas_call x1, Pallas kernels, weights(): pl.pallas_call(weight_kernel, out_shape=out, in_specs=[pl.BlockSpec(memor...  1.81 us
    pallas_call x2, Pallas kernels, contract(): pl.pallas_call(contract_kernel, out_shape=out, in_specs=[pl.BlockSpec(mem...  1.58 us
  transfers between devices with their start and end apart: 15, of which 8 were waited for; matrix products, arithmetic and copies ran while one was open for 1% of the time, Pallas kernels for 10%

profile of v6, /device:TPU:13, one launch (start us, length us, event | category | flops | bytes accessed | tf_op | source)
XLA Modules:
  0.0 57.5 jit_solution(2368327219087572874)
XLA Ops:
  0.0 0.7 %collective-permute-start = (f32[32,1024]{1,0:T(8,128)}, f32[32,1024]{1,0:T(8,128)S(1)}, u32[]{:S(2)}, u32[]{:S(2)}) collective-permute-start(f32[32,1024]{1,0:T(8,128)} %bitcast.9), channel_id=1, source_target_pairs={{0,1},{1,0},{2,3},{3,2},{4,5},{5,4},{6,7},{7,6},{8,9},{9,8},{10,11... | collective-permute-start | bytes 393224 | tf_op jit(solution)/shard_map/ppermute | solution.py:240
  0.7 0.0 copy-start.1
  0.7 0.9 %copy-done.1 = f32[1024,32]{0,1:T(8,128)S(1)} copy-done((f32[1024,32]{0,1:T(8,128)S(1)}, f32[1024,32]{0,1:T(8,128)}, u32[]{:S(2)}) %copy-start.1) | copy-done | bytes 131096
  1.6 0.3 collective-permute-done
  1.9 0.4 collective-permute-start.2
  2.3 3.0 %collective-permute-start.4 = (f32[64,1024]{1,0:T(8,128)S(1)}, f32[64,1024]{1,0:T(8,128)S(1)}, u32[]{:S(2)}, u32[]{:S(2)}) collective-permute-start(f32[64,1024]{1,0:T(8,128)S(1)} %maximum_select_fusion), channel_id=1, source_target_pairs={{0,8},{1,17},{2,0},{3,25},{4,24},{5,1},{6,16},{7,9},{8,2},{9,27},{... | collective-permute-start | bytes 786440 | tf_op jit(solution)/shard_map/ppermute | solution.py:240
  5.4 5.1 %collective-permute-start.1 = (f32[64,1024]{1,0:T(8,128)S(1)}, f32[64,1024]{1,0:T(8,128)S(1)}, u32[]{:S(2)}, u32[]{:S(2)}) collective-permute-start(f32[64,1024]{1,0:T(8,128)S(1)} %maximum_select_fusion), channel_id=1, source_target_pairs={{0,0},{1,25},{2,8},{3,17},{4,16},{5,9},{6,24},{7,1},{8,10},{9,19},... | collective-permute-start | bytes 786440 | tf_op jit(solution)/shard_map/ppermute | solution.py:240
  10.5 0.0 copy-start
  10.5 1.6 %copy-done = f32[1024,512]{1,0:T(8,128)S(1)} copy-done((f32[1024,512]{1,0:T(8,128)S(1)}, f32[1024,512]{1,0:T(8,128)}, u32[]{:S(2)}) %copy-start) | copy-done | bytes 2097176
  12.1 1.1 %prepare.2 = (bf16[512,1024]{1,0:T(8,128)(2,1)S(1)}, bf16[512,1024]{1,0:T(8,128)(2,1)S(1)}) custom-call(f32[1024,512]{1,0:T(8,128)S(1)} %copy-done), custom_call_target="tpu_custom_call" | custom-call | bytes 4194304 | tf_op jit(solution)/shard_map/prepare/pallas_call | solution.py:42
  13.2 0.0 collective-permute-done.2.block_ref
  13.2 1.1 %prepare.3 = (bf16[512,1024]{1,0:T(8,128)(2,1)S(1)}, bf16[512,1024]{1,0:T(8,128)(2,1)S(1)}) custom-call(f32[1024,512]{1,0:T(8,128)S(1)} %collective-permute-done.2.block_ref), custom_call_target="tpu_custom_call" | custom-call | bytes 4194304 | tf_op jit(solution)/shard_map/prepare/pallas_call | solution.py:42
  14.3 2.0 %collective-permute-done.4.factors_ref = f32[64,1024]{1,0:T(8,128)S(1)} collective-permute-done((f32[64,1024]{1,0:T(8,128)S(1)}, f32[64,1024]{1,0:T(8,128)S(1)}, u32[]{:S(2)}, u32[]{:S(2)}) %collective-permute-start.4) | collective-permute-done | bytes 262176 | tf_op jit(solution)/shard_map/ppermute | solution.py:240
  16.3 0.8 %contract.3 = f32[64,1024]{1,0:T(8,128)S(1)} custom-call(s32[1]{0:T(128)} %bitcast.core, f32[64,1024]{1,0:T(8,128)S(1)} %collective-permute-done.4.factors_ref, bf16[512,1024]{1,0:T(8,128)(2,1)S(1)} %get-tuple-element.23.refs_0_, bf16[512,1024]{1,0:T(8,128)(2,1)S(1)} %get-tuple-element.24.refs_1_, bf16[512,1024]{1,0:T(8,128)(2,1)S(1)} %get-tuple-element.25.refs_2_, ...), custom_call_target="tpu_custom_call" | custom-call | flops 402653184 | bytes 4194304 | tf_op jit(solution)/shard_map/contract/pallas_call | solution.py:72
  17.0 1.9 %collective-permute-start.5 = (f32[64,1024]{1,0:T(8,128)S(1)}, f32[64,1024]{1,0:T(8,128)S(1)}, u32[]{:S(2)}, u32[]{:S(2)}) collective-permute-start(f32[64,1024]{1,0:T(8,128)S(1)} %contract.3), channel_id=1, source_target_pairs={{0,2},{1,5},{2,0},{3,7},{4,6},{5,1},{6,4},{7,3},{8,8},{9,15},{10,1... | collective-permute-start | bytes 786440 | tf_op jit(solution)/shard_map/ppermute | solution.py:240
  19.0 0.0 collective-permute-done.1.factors_ref
  19.0 0.8 %contract.2 = f32[64,1024]{1,0:T(8,128)S(1)} custom-call(s32[1]{0:T(128)} %bitcast.core, f32[64,1024]{1,0:T(8,128)S(1)} %collective-permute-done.1.factors_ref, bf16[512,1024]{1,0:T(8,128)(2,1)S(1)} %get-tuple-element.23.refs_0_, bf16[512,1024]{1,0:T(8,128)(2,1)S(1)} %get-tuple-element.24.refs_1_, bf16[512,1024]{1,0:T(8,128)(2,1)S(1)} %get-tuple-element.25.refs_2_, ...), custom_call_target="tpu_custom_call" | custom-call | flops 402653184 | bytes 4194304 | tf_op jit(solution)/shard_map/contract/pallas_call | solution.py:72
  19.8 0.0 copy-start.5
  19.8 0.0 copy-start.2
  19.8 0.0 copy-start.3
  19.8 0.0 copy-start.4
  19.8 2.6 %collective-permute-start.3 = (f32[64,1024]{1,0:T(8,128)S(1)}, f32[64,1024]{1,0:T(8,128)S(1)}, u32[]{:S(2)}, u32[]{:S(2)}) collective-permute-start(f32[64,1024]{1,0:T(8,128)S(1)} %contract.2), channel_id=1, source_target_pairs={{0,0},{1,7},{2,2},{3,5},{4,4},{5,3},{6,6},{7,1},{8,10},{9,13},{10,... | collective-permute-start | bytes 786440 | tf_op jit(solution)/shard_map/ppermute | solution.py:240
  22.4 4.2 %collective-permute-done.5 = f32[64,1024]{1,0:T(8,128)S(1)} collective-permute-done((f32[64,1024]{1,0:T(8,128)S(1)}, f32[64,1024]{1,0:T(8,128)S(1)}, u32[]{:S(2)}, u32[]{:S(2)}) %collective-permute-start.5) | collective-permute-done | bytes 262176 | tf_op jit(solution)/shard_map/ppermute | solution.py:240
  26.6 1.9 %collective-permute-done.3 = f32[64,1024]{1,0:T(8,128)S(1)} collective-permute-done((f32[64,1024]{1,0:T(8,128)S(1)}, f32[64,1024]{1,0:T(8,128)S(1)}, u32[]{:S(2)}, u32[]{:S(2)}) %collective-permute-start.3) | collective-permute-done | bytes 262176 | tf_op jit(solution)/shard_map/ppermute | solution.py:240
  28.6 0.7 %collective-permute-start.6 = (f32[64,1024]{1,0:T(8,128)S(1)}, f32[64,1024]{1,0:T(8,128)S(1)}, u32[]{:S(2)}, u32[]{:S(2)}) collective-permute-start(f32[64,1024]{1,0:T(8,128)S(1)} %add.16), channel_id=1, source_target_pairs={{0,1},{1,0},{2,3},{3,2},{4,5},{5,4},{6,7},{7,6},{8,9},{9,8},{10,11... | collective-permute-start | bytes 786440 | tf_op jit(solution)/shard_map/ppermute | solution.py:240
  29.3 1.2 %collective-permute-done.6 = f32[64,1024]{1,0:T(8,128)S(1)} collective-permute-done((f32[64,1024]{1,0:T(8,128)S(1)}, f32[64,1024]{1,0:T(8,128)S(1)}, u32[]{:S(2)}, u32[]{:S(2)}) %collective-permute-start.6) | collective-permute-done | bytes 262176 | tf_op jit(solution)/shard_map/ppermute | solution.py:240
  30.6 0.1 collective-permute-start.7
  30.6 3.2 %collective-permute-start.8 = (f32[64,1024]{1,0:T(8,128)S(1)}, f32[64,1024]{1,0:T(8,128)S(1)}, u32[]{:S(2)}, u32[]{:S(2)}) collective-permute-start(f32[64,1024]{1,0:T(8,128)S(1)} %add.18), channel_id=1, source_target_pairs={{0,0},{1,25},{2,8},{3,17},{4,16},{5,9},{6,24},{7,1},{8,10},{9,19},... | collective-permute-start | bytes 786440 | tf_op jit(solution)/shard_map/ppermute | solution.py:240
  33.8 7.7 %collective-permute-start.9 = (f32[64,1024]{1,0:T(8,128)S(1)}, f32[64,1024]{1,0:T(8,128)S(1)}, u32[]{:S(2)}, u32[]{:S(2)}) collective-permute-start(f32[64,1024]{1,0:T(8,128)S(1)} %add.18), channel_id=1, source_target_pairs={{0,0},{1,7},{2,2},{3,5},{4,4},{5,3},{6,6},{7,1},{8,8},{9,15},{10,1... | collective-permute-start | bytes 786440 | tf_op jit(solution)/shard_map/ppermute | solution.py:240
  41.6 1.9 %collective-permute-start.12 = (f32[64,1024]{1,0:T(8,128)S(1)}, f32[64,1024]{1,0:T(8,128)S(1)}, u32[]{:S(2)}, u32[]{:S(2)}) collective-permute-start(f32[64,1024]{1,0:T(8,128)S(1)} %add.18), channel_id=1, source_target_pairs={{0,8},{1,17},{2,0},{3,25},{4,24},{5,1},{6,16},{7,9},{8,2},{9,27},{... | collective-permute-start | bytes 786440 | tf_op jit(solution)/shard_map/ppermute | solution.py:240
  43.5 0.0 copy-done.5
  43.5 0.1 pad_add_fusion.2.place
  43.6 0.0 copy-done.2
  43.6 0.0 copy-done.3
  43.6 0.0 copy-done.4
  43.6 1.8 %weights.1.weights_ref = f32[1024,512]{1,0:T(8,128)S(1)} custom-call(s32[2]{0:T(128)S(1)} %pad_add_fusion.2.place, s32[1,4096]{1,0:T(1,128)S(1)} %bitcast.11, s32[1,4096]{1,0:T(1,128)S(1)} %bitcast.12, f32[1,128]{1,0:T(1,128)S(1)} %pad_bitcast_fusion.occ_table, f32[16,128]{1,0:T(8,128)S(1)} %bitcast.13), custom_call_target="tpu_custom_call" | custom-call | bytes 2097152 | tf_op jit(solution)/shard_map/weights/pallas_call | solution.py:138
  45.4 0.0 collective-permute-done.7.refs_1_
  45.4 0.0 collective-permute-done.8.refs_0_
  45.5 0.8 %collective-permute-done.9.refs_0_ = f32[64,1024]{1,0:T(8,128)S(1)} collective-permute-done((f32[64,1024]{1,0:T(8,128)S(1)}, f32[64,1024]{1,0:T(8,128)S(1)}, u32[]{:S(2)}, u32[]{:S(2)}) %collective-permute-start.9) | collective-permute-done | bytes 262176 | tf_op jit(solution)/shard_map/ppermute | solution.py:240
  46.2 0.2 collective-permute-start.10
  46.4 0.4 collective-permute-start.11
  46.8 0.2 collective-permute-start.13
  46.9 6.2 %collective-permute-done.12.refs_1_ = f32[64,1024]{1,0:T(8,128)S(1)} collective-permute-done((f32[64,1024]{1,0:T(8,128)S(1)}, f32[64,1024]{1,0:T(8,128)S(1)}, u32[]{:S(2)}, u32[]{:S(2)}) %collective-permute-start.12) | collective-permute-done | bytes 262176 | tf_op jit(solution)/shard_map/ppermute | solution.py:240
  53.1 0.0 collective-permute-start.14
  53.1 0.1 broadcast_xor_fusion
  53.1 0.2 select_reduce_fusion
  53.3 0.1 pad_add_fusion.1.place
  53.4 0.0 collective-permute-done.10.refs_2_
  53.4 0.0 collective-permute-done.11.refs_3_
  53.4 0.3 left_parts.1
  53.8 0.0 collective-permute-done.13.refs_2_
  53.8 0.8 %collective-permute-done.14.refs_3_ = f32[64,1024]{1,0:T(8,128)S(1)} collective-permute-done((f32[64,1024]{1,0:T(8,128)S(1)}, f32[64,1024]{1,0:T(8,128)S(1)}, u32[]{:S(2)}, u32[]{:S(2)}) %collective-permute-start.14) | collective-permute-done | bytes 262176 | tf_op jit(solution)/shard_map/ppermute | solution.py:240
  54.6 2.9 %outer.1 = f32[1024,512]{1,0:T(8,128)} custom-call(s32[5]{0:T(128)S(1)} %pad_add_fusion.1.place, f32[1024,512]{1,0:T(8,128)S(1)} %weights.1.weights_ref, bf16[1024,256]{1,0:T(8,128)(2,1)S(1)} %get-tuple-element.34.left_high, bf16[1024,256]{1,0:T(8,128)(2,1)S(1)} %get-tuple-element.35.left_low, f32[64,1024]{1,0:T(8,128)S(1)} %collective-permute-done.8.refs_0_, ...), custom_call_target="tpu_custom_call" | custom-call | flops 805306368 | bytes 2097152 | tf_op jit(solution)/shard_map/outer/pallas_call | solution.py:208
  (7 shorter events, 0.1 us)
Async XLA Ops:
  0.0 1.9 %collective-permute-start = (f32[32,1024]{1,0:T(8,128)}, f32[32,1024]{1,0:T(8,128)S(1)}, u32[]{:S(2)}, u32[]{:S(2)}) collective-permute-start(f32[32,1024]{1,0:T(8,128)} %bitcast.9), channel_id=1, source_target_pairs={{0,1},{1,0},{2,3},{3,2},{4,5},{5,4},{6,7},{7,6},{8,9},{9,8},{10,11... | collective-permute-start | bytes 393224 | tf_op jit(solution)/shard_map/ppermute | solution.py:240
  0.7 0.9 %copy-start.1 = (f32[1024,32]{0,1:T(8,128)S(1)}, f32[1024,32]{0,1:T(8,128)}, u32[]{:S(2)}) copy-start(f32[1024,32]{0,1:T(8,128)} %param.7) | copy-start | bytes 393220
  1.9 11.3 %collective-permute-start.2 = (f32[1024,512]{1,0:T(8,128)}, f32[1024,512]{1,0:T(8,128)S(1)}, u32[]{:S(2)}, u32[]{:S(2)}) collective-permute-start(f32[1024,512]{1,0:T(8,128)} %block_ref), channel_id=1, source_target_pairs={{0,1},{1,0},{2,3},{3,2},{4,5},{5,4},{6,7},{7,6},{8,9},{9,8},{10,11... | collective-permute-start | bytes 6291464 | tf_op jit(solution)/shard_map/ppermute | solution.py:240
  2.3 13.9 %collective-permute-start.4 = (f32[64,1024]{1,0:T(8,128)S(1)}, f32[64,1024]{1,0:T(8,128)S(1)}, u32[]{:S(2)}, u32[]{:S(2)}) collective-permute-start(f32[64,1024]{1,0:T(8,128)S(1)} %maximum_select_fusion), channel_id=1, source_target_pairs={{0,8},{1,17},{2,0},{3,25},{4,24},{5,1},{6,16},{7,9},{8,2},{9,27},{... | collective-permute-start | bytes 786440 | tf_op jit(solution)/shard_map/ppermute | solution.py:240
  5.4 13.6 %collective-permute-start.1 = (f32[64,1024]{1,0:T(8,128)S(1)}, f32[64,1024]{1,0:T(8,128)S(1)}, u32[]{:S(2)}, u32[]{:S(2)}) collective-permute-start(f32[64,1024]{1,0:T(8,128)S(1)} %maximum_select_fusion), channel_id=1, source_target_pairs={{0,0},{1,25},{2,8},{3,17},{4,16},{5,9},{6,24},{7,1},{8,10},{9,19},... | collective-permute-start | bytes 786440 | tf_op jit(solution)/shard_map/ppermute | solution.py:240
  10.5 1.6 %copy-start = (f32[1024,512]{1,0:T(8,128)S(1)}, f32[1024,512]{1,0:T(8,128)}, u32[]{:S(2)}) copy-start(f32[1024,512]{1,0:T(8,128)} %block_ref) | copy-start | bytes 6291460
  17.0 9.6 %collective-permute-start.5 = (f32[64,1024]{1,0:T(8,128)S(1)}, f32[64,1024]{1,0:T(8,128)S(1)}, u32[]{:S(2)}, u32[]{:S(2)}) collective-permute-start(f32[64,1024]{1,0:T(8,128)S(1)} %contract.3), channel_id=1, source_target_pairs={{0,2},{1,5},{2,0},{3,7},{4,6},{5,1},{6,4},{7,3},{8,8},{9,15},{10,1... | collective-permute-start | bytes 786440 | tf_op jit(solution)/shard_map/ppermute | solution.py:240
  19.8 23.7 %copy-start.5 = (f32[64]{0:T(128)S(1)}, f32[64]{0:T(128)}, u32[]{:S(2)}) copy-start(f32[64]{0:T(128)} %param.10) | copy-start | bytes 772
  19.8 23.8 %copy-start.2 = (s32[4096]{0:T(1024)S(1)}, s32[4096]{0:T(1024)}, u32[]{:S(2)}) copy-start(s32[4096]{0:T(1024)} %param.8) | copy-start | bytes 49156
  19.8 23.8 %copy-start.3 = (s32[4096]{0:T(1024)S(1)}, s32[4096]{0:T(1024)}, u32[]{:S(2)}) copy-start(s32[4096]{0:T(1024)} %param.9) | copy-start | bytes 49156
  19.8 23.8 %copy-start.4 = (f32[2048]{0:T(1024)S(1)}, f32[2048]{0:T(1024)}, u32[]{:S(2)}) copy-start(f32[2048]{0:T(1024)} %param.11) | copy-start | bytes 24580
  19.8 8.7 %collective-permute-start.3 = (f32[64,1024]{1,0:T(8,128)S(1)}, f32[64,1024]{1,0:T(8,128)S(1)}, u32[]{:S(2)}, u32[]{:S(2)}) collective-permute-start(f32[64,1024]{1,0:T(8,128)S(1)} %contract.2), channel_id=1, source_target_pairs={{0,0},{1,7},{2,2},{3,5},{4,4},{5,3},{6,6},{7,1},{8,10},{9,13},{10,... | collective-permute-start | bytes 786440 | tf_op jit(solution)/shard_map/ppermute | solution.py:240
  28.6 1.9 %collective-permute-start.6 = (f32[64,1024]{1,0:T(8,128)S(1)}, f32[64,1024]{1,0:T(8,128)S(1)}, u32[]{:S(2)}, u32[]{:S(2)}) collective-permute-start(f32[64,1024]{1,0:T(8,128)S(1)} %add.16), channel_id=1, source_target_pairs={{0,1},{1,0},{2,3},{3,2},{4,5},{5,4},{6,7},{7,6},{8,9},{9,8},{10,11... | collective-permute-start | bytes 786440 | tf_op jit(solution)/shard_map/ppermute | solution.py:240
  30.6 14.9 %collective-permute-start.7 = (f32[64,1024]{1,0:T(8,128)S(1)}, f32[64,1024]{1,0:T(8,128)S(1)}, u32[]{:S(2)}, u32[]{:S(2)}) collective-permute-start(f32[64,1024]{1,0:T(8,128)S(1)} %add.18), channel_id=1, source_target_pairs={{0,2},{1,5},{2,0},{3,7},{4,6},{5,1},{6,4},{7,3},{8,10},{9,13},{10,... | collective-permute-start | bytes 786440 | tf_op jit(solution)/shard_map/ppermute | solution.py:240
  30.6 14.8 %collective-permute-start.8 = (f32[64,1024]{1,0:T(8,128)S(1)}, f32[64,1024]{1,0:T(8,128)S(1)}, u32[]{:S(2)}, u32[]{:S(2)}) collective-permute-start(f32[64,1024]{1,0:T(8,128)S(1)} %add.18), channel_id=1, source_target_pairs={{0,0},{1,25},{2,8},{3,17},{4,16},{5,9},{6,24},{7,1},{8,10},{9,19},... | collective-permute-start | bytes 786440 | tf_op jit(solution)/shard_map/ppermute | solution.py:240
  33.8 12.4 %collective-permute-start.9 = (f32[64,1024]{1,0:T(8,128)S(1)}, f32[64,1024]{1,0:T(8,128)S(1)}, u32[]{:S(2)}, u32[]{:S(2)}) collective-permute-start(f32[64,1024]{1,0:T(8,128)S(1)} %add.18), channel_id=1, source_target_pairs={{0,0},{1,7},{2,2},{3,5},{4,4},{5,3},{6,6},{7,1},{8,8},{9,15},{10,1... | collective-permute-start | bytes 786440 | tf_op jit(solution)/shard_map/ppermute | solution.py:240
  41.6 11.5 %collective-permute-start.12 = (f32[64,1024]{1,0:T(8,128)S(1)}, f32[64,1024]{1,0:T(8,128)S(1)}, u32[]{:S(2)}, u32[]{:S(2)}) collective-permute-start(f32[64,1024]{1,0:T(8,128)S(1)} %add.18), channel_id=1, source_target_pairs={{0,8},{1,17},{2,0},{3,25},{4,24},{5,1},{6,16},{7,9},{8,2},{9,27},{... | collective-permute-start | bytes 786440 | tf_op jit(solution)/shard_map/ppermute | solution.py:240
  46.2 7.2 %collective-permute-start.10 = (f32[64,1024]{1,0:T(8,128)S(1)}, f32[64,1024]{1,0:T(8,128)S(1)}, u32[]{:S(2)}, u32[]{:S(2)}) collective-permute-start(f32[64,1024]{1,0:T(8,128)S(1)} %collective-permute-done.9.refs_0_), channel_id=1, source_target_pairs={{0,1},{1,0},{2,3},{3,2},{4,5},{5,4},{6,7},{7,6},{8,9},{9,8},{10,11... | collective-permute-start | bytes 786440 | tf_op jit(solution)/shard_map/ppermute | solution.py:240
  46.4 7.0 %collective-permute-start.11 = (f32[64,1024]{1,0:T(8,128)S(1)}, f32[64,1024]{1,0:T(8,128)S(1)}, u32[]{:S(2)}, u32[]{:S(2)}) collective-permute-start(f32[64,1024]{1,0:T(8,128)S(1)} %collective-permute-done.7.refs_1_), channel_id=1, source_target_pairs={{0,1},{1,0},{2,3},{3,2},{4,5},{5,4},{6,7},{7,6},{8,9},{9,8},{10,11... | collective-permute-start | bytes 786440 | tf_op jit(solution)/shard_map/ppermute | solution.py:240
  46.8 7.0 %collective-permute-start.13 = (f32[64,1024]{1,0:T(8,128)S(1)}, f32[64,1024]{1,0:T(8,128)S(1)}, u32[]{:S(2)}, u32[]{:S(2)}) collective-permute-start(f32[64,1024]{1,0:T(8,128)S(1)} %collective-permute-done.8.refs_0_), channel_id=1, source_target_pairs={{0,1},{1,0},{2,3},{3,2},{4,5},{5,4},{6,7},{7,6},{8,9},{9,8},{10,11... | collective-permute-start | bytes 786440 | tf_op jit(solution)/shard_map/ppermute | solution.py:240
  53.1 1.5 %collective-permute-start.14 = (f32[64,1024]{1,0:T(8,128)S(1)}, f32[64,1024]{1,0:T(8,128)S(1)}, u32[]{:S(2)}, u32[]{:S(2)}) collective-permute-start(f32[64,1024]{1,0:T(8,128)S(1)} %collective-permute-done.12.refs_1_), channel_id=1, source_target_pairs={{0,1},{1,0},{2,3},{3,2},{4,5},{5,4},{6,7},{7,6},{8,9},{9,8},{10,11... | collective-permute-start | bytes 786440 | tf_op jit(solution)/shard_map/ppermute | solution.py:240

commit v7 on v4

--- a/solution.py
+++ b/solution.py
@@ -80,6 +80,23 @@
         ),
         name="contract",
     )(core.reshape(1), *arrays)
+
+
+def fetch_kernel(x_ref, out_ref):
+    out_ref[...] = x_ref[...]
+
+
+def fetch(x):
+    return pl.pallas_call(
+        fetch_kernel,
+        out_shape=shape_of(x.shape),
+        grid=(1,),
+        in_specs=[pl.BlockSpec(x.shape, lambda i: (0, 0))],
+        out_specs=pl.BlockSpec(memory_space=pltpu.VMEM),
+        compiler_params=params(x, x),
+        cost_estimate=pl.CostEstimate(flops=0, bytes_accessed=x.size * 8, transcendentals=0),
+        name="fetch",
+    )(x)
 
 
 def pick(table, index):
@@ -224,7 +241,6 @@
         return z * cols + j * cores + s
 
     def turn(i, s):
-        i = share - 1 - i
         return i if s == 0 else rows - 1 - i
 
     def move(x, to):
@@ -233,14 +249,26 @@
     def swap(x):
         return move(x, lambda z, j, s: (z, j, 1 - s))
 
+    def turned(z, s, i):
+        low = z % share ^ i
+        return rows - 1 - low if s else low
+
     def transposed(x, i):
-        return move(x, lambda z, j, s: (j ^ z ^ turn(i, s), z, s))
+        def to(z, j, s):
+            side, low = divmod(j ^ z, share)
+            low = share - 1 - low if side else low
+            return (s ^ z // share) * share + (low ^ i), z, side
+
+        return move(x, to)
 
     def reduced(x, i):
-        return move(x, lambda z, j, s: (z, z ^ j ^ turn(i, s), s))
+        return move(x, lambda z, j, s: (z, j ^ turned(z, s, i), s))
 
     def across(x, i):
         return move(x, lambda z, j, s: (z, j ^ turn(i, s), s))
+
+    def within_half(x, v):
+        return move(x, lambda z, j, s: (z ^ v, j, s))
 
     turns = range(share)
     row_index = lax.axis_index("row").astype(jnp.int32)
@@ -248,17 +276,19 @@
     core = col_index % cores
     tall, wide = amplitudes.shape
 
-    def share_of(x):
+    def share_of(x, mine):
         other = swap(x)
         return jnp.where(
-            core == 0, jnp.concatenate([x, other], axis=0), jnp.concatenate([other, x], axis=0)
+            core == 0, jnp.concatenate([mine, other], axis=0), jnp.concatenate([other, mine], axis=0)
         )
 
-    pieces = share_of(factors.T)
+    first = jnp.arange(share, dtype=jnp.int32)
+    pieces = share_of(factors.T, fetch(factors.T))
     received = [transposed(pieces, i) for i in turns]
     amplitudes, pieces = lax.optimization_barrier((amplitudes, pieces))
     blocks = prepare(amplitudes), prepare(swap(amplitudes))
-    arrived = [reduced(contract(core, received[i], *blocks), i) for i in turns]
+    partial = [contract(core, x, *blocks) for x in received]
+    arrived = [reduced(partial[i], i) for i in turns]
     total = functools.reduce(jnp.add, arrived)
     total = total + swap(total)
     total, occ_index, vir_index = lax.optimization_barrier((total, occ_index, vir_index))
@@ -266,16 +296,20 @@
     factor = weights(
         jnp.stack([row_index, col_index]), occ_index, vir_index, occ_energy, vir_energy, tall, wide
     )
-    right = [transposed(dressed, i) for i in turns]
     left = [across(dressed, i) for i in turns]
-    right[0], left, factor = lax.optimization_barrier((right[0], left[::-1], factor))
+    right = [transposed(dressed, 0)]
+    right += [within_half(right[0], v) for v in range(1, share)]
+    left, factor = lax.optimization_barrier((left[::-1], factor))
     left = left[::-1]
     left += [swap(x) for x in left]
     right += [swap(x) for x in right]
-    first = share - 1 - jnp.arange(share, dtype=jnp.int32)
-    first = jnp.where(core == 0, first, rows - 1 - first)
-    order = jnp.concatenate([first, rows - 1 - first])
-    wanted = row_index ^ order
+    order = jnp.where(core == 0, first, rows - 1 - first)
+    order = jnp.concatenate([order, rows - 1 - order])
+    low = row_index % share ^ first
+    lower, upper = low, rows - 1 - low
+    wanted = jnp.concatenate(
+        [jnp.where(core == 0, lower, upper), jnp.where(core == 0, upper, lower)]
+    )
     at = jnp.sum(
         jnp.where(wanted[:, None] == order[None, :], jnp.arange(rows, dtype=jnp.int32)[None, :], 0), axis=1
     )

time: 59.4 us -> 55.4 us (0.933)
  starting transfers between devices: 28.9 us -> 21.7 us
  waiting for transfers between devices: 18.3 us -> 21.6 us
  other arithmetic: 1.53 us -> 0.62 us
  local copies, waits for them, and re-layouts: 1.62 us -> 2.52 us
    ppermute x15, starting transfers between devices: 28.9 us -> 21.7 us  [move(): lax.ppermute(x, AXES, [(number(*at), number(*to(*at))) for at in chips])]
    ppermute x15, waiting for transfers between devices: 18.3 us -> 21.6 us  [move(): lax.ppermute(x, AXES, [(number(*at), number(*to(*at))) for at in chips])]
    select_n x2 -> x3, other arithmetic: 1.01 us -> 0.03 us  [the longest x1 0.02 us: share_of(): jnp.where(core == 0, jnp.concatenate([mine, other], axis=0), jnp.concaten...]
    unnamed x10 -> x12, local copies, waits for them, and re-layouts: 1.61 us -> 2.52 us
  transfers between devices with their start and end apart: 15 -> 15, of which waited for: 9 -> 9; matrix products, arithmetic and copies ran while one was open for 1% -> 1% of each run, Pallas kernels for 10% -> 11%
where the time goes in v7:
time: 55.4 us; the launch traced here: 55.1 us
  starting transfers between devices  21.7 us (39%)
  waiting for transfers between devices  21.6 us (39%)
  Pallas kernels  8.38 us (15%)
  local copies, waits for them, and re-layouts  2.52 us (5%)
  other arithmetic  0.62 us (1%)
    ppermute x15, starting transfers between devices, move(): lax.ppermute(x, AXES, [(number(*at), number(*to(*at))) for at in chips])  21.7 us
    ppermute x15, waiting for transfers between devices, move(): lax.ppermute(x, AXES, [(number(*at), number(*to(*at))) for at in chips])  21.6 us
    unnamed x12, local copies, waits for them, and re-layouts  2.52 us
    pallas_call x1, Pallas kernels, outer(): pl.pallas_call(functools.partial(outer_kernel, slots), out_shape=out, in_...  2.44 us
    pallas_call x2, Pallas kernels, prepare(): pl.pallas_call(prepare_kernel, out_shape=(out, out), grid=(tall // step,)...  2.2 us
    pallas_call x1, Pallas kernels, weights(): pl.pallas_call(weight_kernel, out_shape=out, in_specs=[pl.BlockSpec(memor...  1.81 us
    pallas_call x2, Pallas kernels, contract(): pl.pallas_call(contract_kernel, out_shape=out, in_specs=[pl.BlockSpec(mem...  1.58 us
  transfers between devices with their start and end apart: 15, of which 9 were waited for; matrix products, arithmetic and copies ran while one was open for 1% of the time, Pallas kernels for 11%

profile of v7, /device:TPU:5, one launch (start us, length us, event | category | flops | bytes accessed | tf_op | source)
XLA Modules:
  0.0 55.1 jit_solution(10115555295734071650)
XLA Ops:
  0.0 0.7 %collective-permute-start = (f32[32,1024]{1,0:T(8,128)}, f32[32,1024]{1,0:T(8,128)S(1)}, u32[]{:S(2)}, u32[]{:S(2)}) collective-permute-start(f32[32,1024]{1,0:T(8,128)} %bitcast.9), channel_id=1, source_target_pairs={{0,1},{1,0},{2,3},{3,2},{4,5},{5,4},{6,7},{7,6},{8,9},{9,8},{10,11... | collective-permute-start | bytes 393224 | tf_op jit(solution)/shard_map/ppermute | solution.py:247
  0.7 0.0 copy-start.1
  0.7 0.9 %copy-done.1 = f32[1024,32]{0,1:T(8,128)S(1)} copy-done((f32[1024,32]{0,1:T(8,128)S(1)}, f32[1024,32]{0,1:T(8,128)}, u32[]{:S(2)}) %copy-start.1) | copy-done | bytes 131096
  1.6 0.3 collective-permute-done
  1.9 0.4 collective-permute-start.2
  2.3 4.1 %collective-permute-start.4 = (f32[64,1024]{1,0:T(8,128)S(1)}, f32[64,1024]{1,0:T(8,128)S(1)}, u32[]{:S(2)}, u32[]{:S(2)}) collective-permute-start(f32[64,1024]{1,0:T(8,128)S(1)} %maximum_select_fusion), channel_id=1, source_target_pairs={{0,8},{1,24},{2,0},{3,16},{4,1},{5,17},{6,9},{7,25},{8,2},{9,18},{... | collective-permute-start | bytes 786440 | tf_op jit(solution)/shard_map/ppermute | solution.py:247
  6.5 4.9 %collective-permute-start.1 = (f32[64,1024]{1,0:T(8,128)S(1)}, f32[64,1024]{1,0:T(8,128)S(1)}, u32[]{:S(2)}, u32[]{:S(2)}) collective-permute-start(f32[64,1024]{1,0:T(8,128)S(1)} %maximum_select_fusion), channel_id=1, source_target_pairs={{0,0},{1,16},{2,8},{3,24},{4,9},{5,25},{6,1},{7,17},{8,10},{9,26},... | collective-permute-start | bytes 786440 | tf_op jit(solution)/shard_map/ppermute | solution.py:247
  11.3 0.0 copy-start
  11.4 1.6 %copy-done = f32[1024,512]{1,0:T(8,128)S(1)} copy-done((f32[1024,512]{1,0:T(8,128)S(1)}, f32[1024,512]{1,0:T(8,128)}, u32[]{:S(2)}) %copy-start) | copy-done | bytes 2097176
  12.9 1.1 %prepare.2 = (bf16[512,1024]{1,0:T(8,128)(2,1)S(1)}, bf16[512,1024]{1,0:T(8,128)(2,1)S(1)}) custom-call(f32[1024,512]{1,0:T(8,128)S(1)} %copy-done), custom_call_target="tpu_custom_call" | custom-call | bytes 4194304 | tf_op jit(solution)/shard_map/prepare/pallas_call | solution.py:42
  14.0 0.0 collective-permute-done.2.block_ref
  14.0 1.1 %prepare.3 = (bf16[512,1024]{1,0:T(8,128)(2,1)S(1)}, bf16[512,1024]{1,0:T(8,128)(2,1)S(1)}) custom-call(f32[1024,512]{1,0:T(8,128)S(1)} %collective-permute-done.2.block_ref), custom_call_target="tpu_custom_call" | custom-call | bytes 4194304 | tf_op jit(solution)/shard_map/prepare/pallas_call | solution.py:42
  15.2 0.0 collective-permute-done.4.factors_ref
  15.2 0.8 %contract.3 = f32[64,1024]{1,0:T(8,128)S(1)} custom-call(s32[1]{0:T(128)} %bitcast.core, f32[64,1024]{1,0:T(8,128)S(1)} %collective-permute-done.4.factors_ref, bf16[512,1024]{1,0:T(8,128)(2,1)S(1)} %get-tuple-element.21.refs_0_, bf16[512,1024]{1,0:T(8,128)(2,1)S(1)} %get-tuple-element.22.refs_1_, bf16[512,1024]{1,0:T(8,128)(2,1)S(1)} %get-tuple-element.23.refs_2_, ...), custom_call_target="tpu_custom_call" | custom-call | flops 402653184 | bytes 4194304 | tf_op jit(solution)/shard_map/contract/pallas_call | solution.py:72
  16.0 1.9 %collective-permute-start.5 = (f32[64,1024]{1,0:T(8,128)S(1)}, f32[64,1024]{1,0:T(8,128)S(1)}, u32[]{:S(2)}, u32[]{:S(2)}) collective-permute-start(f32[64,1024]{1,0:T(8,128)S(1)} %contract.3), channel_id=1, source_target_pairs={{0,2},{1,5},{2,0},{3,7},{4,6},{5,1},{6,4},{7,3},{8,8},{9,15},{10,1... | collective-permute-start | bytes 786440 | tf_op jit(solution)/shard_map/ppermute | solution.py:247
  17.9 2.9 %collective-permute-done.1.factors_ref = f32[64,1024]{1,0:T(8,128)S(1)} collective-permute-done((f32[64,1024]{1,0:T(8,128)S(1)}, f32[64,1024]{1,0:T(8,128)S(1)}, u32[]{:S(2)}, u32[]{:S(2)}) %collective-permute-start.1) | collective-permute-done | bytes 262176 | tf_op jit(solution)/shard_map/ppermute | solution.py:247
  20.8 0.8 %contract.2 = f32[64,1024]{1,0:T(8,128)S(1)} custom-call(s32[1]{0:T(128)} %bitcast.core, f32[64,1024]{1,0:T(8,128)S(1)} %collective-permute-done.1.factors_ref, bf16[512,1024]{1,0:T(8,128)(2,1)S(1)} %get-tuple-element.21.refs_0_, bf16[512,1024]{1,0:T(8,128)(2,1)S(1)} %get-tuple-element.22.refs_1_, bf16[512,1024]{1,0:T(8,128)(2,1)S(1)} %get-tuple-element.23.refs_2_, ...), custom_call_target="tpu_custom_call" | custom-call | flops 402653184 | bytes 4194304 | tf_op jit(solution)/shard_map/contract/pallas_call | solution.py:72
  21.6 0.0 copy-start.5
  21.6 0.0 copy-start.2
  21.6 0.0 copy-start.3
  21.6 0.0 copy-start.4
  21.7 2.1 %collective-permute-start.3 = (f32[64,1024]{1,0:T(8,128)S(1)}, f32[64,1024]{1,0:T(8,128)S(1)}, u32[]{:S(2)}, u32[]{:S(2)}) collective-permute-start(f32[64,1024]{1,0:T(8,128)S(1)} %contract.2), channel_id=1, source_target_pairs={{0,0},{1,7},{2,2},{3,5},{4,4},{5,3},{6,6},{7,1},{8,10},{9,13},{10,... | collective-permute-start | bytes 786440 | tf_op jit(solution)/shard_map/ppermute | solution.py:247
  23.7 0.2 collective-permute-done.5
  23.9 5.9 %collective-permute-done.3 = f32[64,1024]{1,0:T(8,128)S(1)} collective-permute-done((f32[64,1024]{1,0:T(8,128)S(1)}, f32[64,1024]{1,0:T(8,128)S(1)}, u32[]{:S(2)}, u32[]{:S(2)}) %collective-permute-start.3) | collective-permute-done | bytes 262176 | tf_op jit(solution)/shard_map/ppermute | solution.py:247
  29.8 0.1 collective-permute-start.6
  29.9 1.5 %collective-permute-done.6 = f32[64,1024]{1,0:T(8,128)S(1)} collective-permute-done((f32[64,1024]{1,0:T(8,128)S(1)}, f32[64,1024]{1,0:T(8,128)S(1)}, u32[]{:S(2)}, u32[]{:S(2)}) %collective-permute-start.6) | collective-permute-done | bytes 262176 | tf_op jit(solution)/shard_map/ppermute | solution.py:247
  31.5 3.2 %collective-permute-start.11 = (f32[64,1024]{1,0:T(8,128)S(1)}, f32[64,1024]{1,0:T(8,128)S(1)}, u32[]{:S(2)}, u32[]{:S(2)}) collective-permute-start(f32[64,1024]{1,0:T(8,128)S(1)} %add.22), channel_id=1, source_target_pairs={{0,0},{1,16},{2,8},{3,24},{4,9},{5,25},{6,1},{7,17},{8,10},{9,26},... | collective-permute-start | bytes 786440 | tf_op jit(solution)/shard_map/ppermute | solution.py:247
  34.7 0.0 copy-done.5
  34.8 0.1 collective-permute-start.7
  34.9 3.3 %collective-permute-start.8 = (f32[64,1024]{1,0:T(8,128)S(1)}, f32[64,1024]{1,0:T(8,128)S(1)}, u32[]{:S(2)}, u32[]{:S(2)}) collective-permute-start(f32[64,1024]{1,0:T(8,128)S(1)} %add.22), channel_id=1, source_target_pairs={{0,0},{1,7},{2,2},{3,5},{4,4},{5,3},{6,6},{7,1},{8,8},{9,15},{10,1... | collective-permute-start | bytes 786440 | tf_op jit(solution)/shard_map/ppermute | solution.py:247
  38.2 4.6 %collective-permute-done.11.refs_0_ = f32[64,1024]{1,0:T(8,128)S(1)} collective-permute-done((f32[64,1024]{1,0:T(8,128)S(1)}, f32[64,1024]{1,0:T(8,128)S(1)}, u32[]{:S(2)}, u32[]{:S(2)}) %collective-permute-start.11) | collective-permute-done | bytes 262176 | tf_op jit(solution)/shard_map/ppermute | solution.py:247
  42.8 0.0 collective-permute-start.12
  42.8 0.1 pad_add_fusion.3.place
  42.9 0.1 pad_add_fusion
  43.0 0.0 copy-done.2
  43.0 0.0 copy-done.3
  43.0 0.0 copy-done.4
  43.0 1.8 %weights.1.weights_ref = f32[1024,512]{1,0:T(8,128)S(1)} custom-call(s32[2]{0:T(128)S(1)} %pad_add_fusion.3.place, s32[1,4096]{1,0:T(1,128)S(1)} %bitcast.11, s32[1,4096]{1,0:T(1,128)S(1)} %bitcast.12, f32[1,128]{1,0:T(1,128)S(1)} %pad_bitcast_fusion.occ_table, f32[16,128]{1,0:T(8,128)S(1)} %bitcast.13), custom_call_target="tpu_custom_call" | custom-call | bytes 2097152 | tf_op jit(solution)/shard_map/weights/pallas_call | solution.py:138
  44.8 1.2 %collective-permute-done.7.refs_1_ = f32[64,1024]{1,0:T(8,128)S(1)} collective-permute-done((f32[64,1024]{1,0:T(8,128)S(1)}, f32[64,1024]{1,0:T(8,128)S(1)}, u32[]{:S(2)}, u32[]{:S(2)}) %collective-permute-start.7) | collective-permute-done | bytes 262176 | tf_op jit(solution)/shard_map/ppermute | solution.py:247
  46.0 0.0 collective-permute-done.8.refs_0_
  46.0 0.0 collective-permute-start.10
  46.0 0.5 collective-permute-start.9
  46.5 0.0 collective-permute-start.13
  46.5 4.6 %collective-permute-done.12.refs_1_ = f32[64,1024]{1,0:T(8,128)S(1)} collective-permute-done((f32[64,1024]{1,0:T(8,128)S(1)}, f32[64,1024]{1,0:T(8,128)S(1)}, u32[]{:S(2)}, u32[]{:S(2)}) %collective-permute-start.12) | collective-permute-done | bytes 262176 | tf_op jit(solution)/shard_map/ppermute | solution.py:247
  51.1 0.4 collective-permute-start.14
  51.5 0.1 pad_add_fusion.1
  51.6 0.2 select_reduce_fusion
  51.8 0.1 pad_add_fusion.2.place
  51.8 0.0 collective-permute-done.10.refs_3_
  51.8 0.0 collective-permute-done.9.refs_2_
  51.8 0.3 left_parts.1
  52.2 0.0 collective-permute-done.13.refs_2_
  52.2 0.5 collective-permute-done.14.refs_3_
  52.7 2.4 %outer.1 = f32[1024,512]{1,0:T(8,128)} custom-call(s32[5]{0:T(128)S(1)} %pad_add_fusion.2.place, f32[1024,512]{1,0:T(8,128)S(1)} %weights.1.weights_ref, bf16[1024,256]{1,0:T(8,128)(2,1)S(1)} %get-tuple-element.31.left_high, bf16[1024,256]{1,0:T(8,128)(2,1)S(1)} %get-tuple-element.32.left_low, f32[64,1024]{1,0:T(8,128)S(1)} %collective-permute-done.11.refs_0_, ...), custom_call_target="tpu_custom_call" | custom-call | flops 805306368 | bytes 2097152 | tf_op jit(solution)/shard_map/outer/pallas_call | solution.py:214
  (8 shorter events, 0.1 us)
Async XLA Ops:
  0.0 1.9 %collective-permute-start = (f32[32,1024]{1,0:T(8,128)}, f32[32,1024]{1,0:T(8,128)S(1)}, u32[]{:S(2)}, u32[]{:S(2)}) collective-permute-start(f32[32,1024]{1,0:T(8,128)} %bitcast.9), channel_id=1, source_target_pairs={{0,1},{1,0},{2,3},{3,2},{4,5},{5,4},{6,7},{7,6},{8,9},{9,8},{10,11... | collective-permute-start | bytes 393224 | tf_op jit(solution)/shard_map/ppermute | solution.py:247
  0.7 0.9 %copy-start.1 = (f32[1024,32]{0,1:T(8,128)S(1)}, f32[1024,32]{0,1:T(8,128)}, u32[]{:S(2)}) copy-start(f32[1024,32]{0,1:T(8,128)} %param.7) | copy-start | bytes 393220
  1.9 12.1 %collective-permute-start.2 = (f32[1024,512]{1,0:T(8,128)}, f32[1024,512]{1,0:T(8,128)S(1)}, u32[]{:S(2)}, u32[]{:S(2)}) collective-permute-start(f32[1024,512]{1,0:T(8,128)} %block_ref), channel_id=1, source_target_pairs={{0,1},{1,0},{2,3},{3,2},{4,5},{5,4},{6,7},{7,6},{8,9},{9,8},{10,11... | collective-permute-start | bytes 6291464 | tf_op jit(solution)/shard_map/ppermute | solution.py:247
  2.3 12.8 %collective-permute-start.4 = (f32[64,1024]{1,0:T(8,128)S(1)}, f32[64,1024]{1,0:T(8,128)S(1)}, u32[]{:S(2)}, u32[]{:S(2)}) collective-permute-start(f32[64,1024]{1,0:T(8,128)S(1)} %maximum_select_fusion), channel_id=1, source_target_pairs={{0,8},{1,24},{2,0},{3,16},{4,1},{5,17},{6,9},{7,25},{8,2},{9,18},{... | collective-permute-start | bytes 786440 | tf_op jit(solution)/shard_map/ppermute | solution.py:247
  6.5 14.3 %collective-permute-start.1 = (f32[64,1024]{1,0:T(8,128)S(1)}, f32[64,1024]{1,0:T(8,128)S(1)}, u32[]{:S(2)}, u32[]{:S(2)}) collective-permute-start(f32[64,1024]{1,0:T(8,128)S(1)} %maximum_select_fusion), channel_id=1, source_target_pairs={{0,0},{1,16},{2,8},{3,24},{4,9},{5,25},{6,1},{7,17},{8,10},{9,26},... | collective-permute-start | bytes 786440 | tf_op jit(solution)/shard_map/ppermute | solution.py:247
  11.3 1.6 %copy-start = (f32[1024,512]{1,0:T(8,128)S(1)}, f32[1024,512]{1,0:T(8,128)}, u32[]{:S(2)}) copy-start(f32[1024,512]{1,0:T(8,128)} %block_ref) | copy-start | bytes 6291460
  16.0 7.9 %collective-permute-start.5 = (f32[64,1024]{1,0:T(8,128)S(1)}, f32[64,1024]{1,0:T(8,128)S(1)}, u32[]{:S(2)}, u32[]{:S(2)}) collective-permute-start(f32[64,1024]{1,0:T(8,128)S(1)} %contract.3), channel_id=1, source_target_pairs={{0,2},{1,5},{2,0},{3,7},{4,6},{5,1},{6,4},{7,3},{8,8},{9,15},{10,1... | collective-permute-start | bytes 786440 | tf_op jit(solution)/shard_map/ppermute | solution.py:247
  21.6 13.1 %copy-start.5 = (f32[64]{0:T(128)S(1)}, f32[64]{0:T(128)}, u32[]{:S(2)}) copy-start(f32[64]{0:T(128)} %param.10) | copy-start | bytes 772
  21.6 21.3 %copy-start.2 = (s32[4096]{0:T(1024)S(1)}, s32[4096]{0:T(1024)}, u32[]{:S(2)}) copy-start(s32[4096]{0:T(1024)} %param.8) | copy-start | bytes 49156
  21.6 21.3 %copy-start.3 = (s32[4096]{0:T(1024)S(1)}, s32[4096]{0:T(1024)}, u32[]{:S(2)}) copy-start(s32[4096]{0:T(1024)} %param.9) | copy-start | bytes 49156
  21.6 21.3 %copy-start.4 = (f32[2048]{0:T(1024)S(1)}, f32[2048]{0:T(1024)}, u32[]{:S(2)}) copy-start(f32[2048]{0:T(1024)} %param.11) | copy-start | bytes 24580
  21.7 8.1 %collective-permute-start.3 = (f32[64,1024]{1,0:T(8,128)S(1)}, f32[64,1024]{1,0:T(8,128)S(1)}, u32[]{:S(2)}, u32[]{:S(2)}) collective-permute-start(f32[64,1024]{1,0:T(8,128)S(1)} %contract.2), channel_id=1, source_target_pairs={{0,0},{1,7},{2,2},{3,5},{4,4},{5,3},{6,6},{7,1},{8,10},{9,13},{10,... | collective-permute-start | bytes 786440 | tf_op jit(solution)/shard_map/ppermute | solution.py:247
  29.8 1.6 %collective-permute-start.6 = (f32[64,1024]{1,0:T(8,128)S(1)}, f32[64,1024]{1,0:T(8,128)S(1)}, u32[]{:S(2)}, u32[]{:S(2)}) collective-permute-start(f32[64,1024]{1,0:T(8,128)S(1)} %add.20), channel_id=1, source_target_pairs={{0,1},{1,0},{2,3},{3,2},{4,5},{5,4},{6,7},{7,6},{8,9},{9,8},{10,11... | collective-permute-start | bytes 786440 | tf_op jit(solution)/shard_map/ppermute | solution.py:247
  31.5 11.3 %collective-permute-start.11 = (f32[64,1024]{1,0:T(8,128)S(1)}, f32[64,1024]{1,0:T(8,128)S(1)}, u32[]{:S(2)}, u32[]{:S(2)}) collective-permute-start(f32[64,1024]{1,0:T(8,128)S(1)} %add.22), channel_id=1, source_target_pairs={{0,0},{1,16},{2,8},{3,24},{4,9},{5,25},{6,1},{7,17},{8,10},{9,26},... | collective-permute-start | bytes 786440 | tf_op jit(solution)/shard_map/ppermute | solution.py:247
  34.8 11.2 %collective-permute-start.7 = (f32[64,1024]{1,0:T(8,128)S(1)}, f32[64,1024]{1,0:T(8,128)S(1)}, u32[]{:S(2)}, u32[]{:S(2)}) collective-permute-start(f32[64,1024]{1,0:T(8,128)S(1)} %add.22), channel_id=1, source_target_pairs={{0,2},{1,5},{2,0},{3,7},{4,6},{5,1},{6,4},{7,3},{8,10},{9,13},{10,... | collective-permute-start | bytes 786440 | tf_op jit(solution)/shard_map/ppermute | solution.py:247
  34.9 11.1 %collective-permute-start.8 = (f32[64,1024]{1,0:T(8,128)S(1)}, f32[64,1024]{1,0:T(8,128)S(1)}, u32[]{:S(2)}, u32[]{:S(2)}) collective-permute-start(f32[64,1024]{1,0:T(8,128)S(1)} %add.22), channel_id=1, source_target_pairs={{0,0},{1,7},{2,2},{3,5},{4,4},{5,3},{6,6},{7,1},{8,8},{9,15},{10,1... | collective-permute-start | bytes 786440 | tf_op jit(solution)/shard_map/ppermute | solution.py:247
  42.8 8.3 %collective-permute-start.12 = (f32[64,1024]{1,0:T(8,128)S(1)}, f32[64,1024]{1,0:T(8,128)S(1)}, u32[]{:S(2)}, u32[]{:S(2)}) collective-permute-start(f32[64,1024]{1,0:T(8,128)S(1)} %collective-permute-done.11.refs_0_), channel_id=1, source_target_pairs={{0,8},{1,9},{2,10},{3,11},{4,12},{5,13},{6,14},{7,15},{8,0},{9,1},... | collective-permute-start | bytes 786440 | tf_op jit(solution)/shard_map/ppermute | solution.py:247
  46.0 5.8 %collective-permute-start.10 = (f32[64,1024]{1,0:T(8,128)S(1)}, f32[64,1024]{1,0:T(8,128)S(1)}, u32[]{:S(2)}, u32[]{:S(2)}) collective-permute-start(f32[64,1024]{1,0:T(8,128)S(1)} %collective-permute-done.7.refs_1_), channel_id=1, source_target_pairs={{0,1},{1,0},{2,3},{3,2},{4,5},{5,4},{6,7},{7,6},{8,9},{9,8},{10,11... | collective-permute-start | bytes 786440 | tf_op jit(solution)/shard_map/ppermute | solution.py:247
  46.0 5.8 %collective-permute-start.9 = (f32[64,1024]{1,0:T(8,128)S(1)}, f32[64,1024]{1,0:T(8,128)S(1)}, u32[]{:S(2)}, u32[]{:S(2)}) collective-permute-start(f32[64,1024]{1,0:T(8,128)S(1)} %collective-permute-done.8.refs_0_), channel_id=1, source_target_pairs={{0,1},{1,0},{2,3},{3,2},{4,5},{5,4},{6,7},{7,6},{8,9},{9,8},{10,11... | collective-permute-start | bytes 786440 | tf_op jit(solution)/shard_map/ppermute | solution.py:247
  46.5 5.7 %collective-permute-start.13 = (f32[64,1024]{1,0:T(8,128)S(1)}, f32[64,1024]{1,0:T(8,128)S(1)}, u32[]{:S(2)}, u32[]{:S(2)}) collective-permute-start(f32[64,1024]{1,0:T(8,128)S(1)} %collective-permute-done.11.refs_0_), channel_id=1, source_target_pairs={{0,1},{1,0},{2,3},{3,2},{4,5},{5,4},{6,7},{7,6},{8,9},{9,8},{10,11... | collective-permute-start | bytes 786440 | tf_op jit(solution)/shard_map/ppermute | solution.py:247
  51.1 1.6 %collective-permute-start.14 = (f32[64,1024]{1,0:T(8,128)S(1)}, f32[64,1024]{1,0:T(8,128)S(1)}, u32[]{:S(2)}, u32[]{:S(2)}) collective-permute-start(f32[64,1024]{1,0:T(8,128)S(1)} %collective-permute-done.12.refs_1_), channel_id=1, source_target_pairs={{0,1},{1,0},{2,3},{3,2},{4,5},{5,4},{6,7},{7,6},{8,9},{9,8},{10,11... | collective-permute-start | bytes 786440 | tf_op jit(solution)/shard_map/ppermute | solution.py:247

commit v8 on v7

--- a/solution.py
+++ b/solution.py
@@ -176,15 +176,14 @@
 CHUNKS = 4
 
 
-def outer_kernel(slots, place, weights_ref, left_high, left_low, *refs):
-    right = refs[:slots]
-    out_ref, high_ref, low_ref, result_ref, sems = refs[slots:]
-    depth = right[0].shape[0]
+def outer_kernel(spots, depth, place, weights_ref, left_high, left_low, *refs):
+    right = refs[: len(spots)]
+    out_ref, high_ref, low_ref, result_ref, sems = refs[len(spots) :]
     total, wide = out_ref.shape
     mine = pl.ds(pl.multiple_of(place[0] * wide, wide), wide)
-    for slot in range(slots):
-        high, low = split(right[slot][:, mine])
-        here = pl.ds(pl.multiple_of(place[1 + slot] * depth, depth), depth)
+    for ref, (slot, offset) in zip(right, spots):
+        high, low = split(ref[:, mine])
+        here = pl.ds(pl.multiple_of(place[1 + slot] * depth + offset, ref.shape[0]), ref.shape[0])
         high_ref[here, :] = high
         low_ref[here, :] = low
     tall = total // CHUNKS
@@ -204,15 +203,15 @@
         copy.wait()
 
 
-def outer(place, weights, left_high, left_low, right):
-    slots = len(right)
-    depth, total = right[0].shape
+def outer(place, weights, left_high, left_low, right, spots):
+    total, inner = left_high.shape
+    depth = right[0].shape[0]
     wide = weights.shape[1]
     arrays = [weights, left_high, left_low, *right]
     out = shape_of((total, wide))
-    parts = pltpu.VMEM((slots * depth, wide), jnp.bfloat16)
-    return pl.pallas_call(
-        functools.partial(outer_kernel, slots),
+    parts = pltpu.VMEM((inner, wide), jnp.bfloat16)
+    return pl.pallas_call(
+        functools.partial(outer_kernel, spots, depth),
         out_shape=out,
         in_specs=[pl.BlockSpec(memory_space=pltpu.SMEM)] + whole_specs(len(arrays)),
         out_specs=pl.BlockSpec(memory_space=pl.ANY),
@@ -226,7 +225,7 @@
             vmem_limit_bytes=sum(a.size * a.dtype.itemsize for a in arrays) + out.size * 8 + 8 * MIB
         ),
         cost_estimate=pl.CostEstimate(
-            flops=6 * out.size * slots * depth, bytes_accessed=out.size * 4, transcendentals=0
+            flops=6 * out.size * inner, bytes_accessed=out.size * 4, transcendentals=0
         ),
         name="outer",
     )(place, *arrays)
@@ -297,10 +296,13 @@
         jnp.stack([row_index, col_index]), occ_index, vir_index, occ_energy, vir_energy, tall, wide
     )
     left = [across(dressed, i) for i in turns]
-    right = [transposed(dressed, 0)]
-    right += [within_half(right[0], v) for v in range(1, share)]
-    left, factor = lax.optimization_barrier((left[::-1], factor))
-    left = left[::-1]
+    part = dressed.shape[0] // 2
+    right, spots = [transposed(dressed, 0)], [(0, 0)]
+    for v in range(1, share):
+        right += [transposed(dressed[part:], v), within_half(right[0][:part], v)]
+        spots += [(v, part), (v, 0)]
+    spots += [(share + slot, offset) for slot, offset in spots]
+    left[1], factor = lax.optimization_barrier((left[1], factor))
     left += [swap(x) for x in left]
     right += [swap(x) for x in right]
     order = jnp.where(core == 0, first, rows - 1 - first)
@@ -315,7 +317,7 @@
     )
     place = jnp.concatenate([core[None], at]).astype(jnp.int32)
     left_high, left_low = left_parts(left)
-    return outer(place, factor, left_high, left_low, right)
+    return outer(place, factor, left_high, left_low, right, spots)
 
 
 def solution(mesh):

time: 55.4 us -> 52.9 us (0.955)
  waiting for transfers between devices: 21.6 us -> 13.1 us
  starting transfers between devices: 21.7 us -> 27.2 us
    ppermute x15 -> x17, waiting for transfers between devices: 21.6 us -> 13.1 us  [move(): lax.ppermute(x, AXES, [(number(*at), number(*to(*at))) for at in chips])]
    ppermute x15 -> x17, starting transfers between devices: 21.7 us -> 27.2 us  [move(): lax.ppermute(x, AXES, [(number(*at), number(*to(*at))) for at in chips])]
  transfers between devices with their start and end apart: 15 -> 17, of which waited for: 9 -> 8; matrix products, arithmetic and copies ran while one was open for 1% -> 1% of each run, Pallas kernels for 11% -> 11%
where the time goes in v8:
time: 52.9 us; the launch traced here: 52.1 us
  starting transfers between devices  27.2 us (51%)
  waiting for transfers between devices  13.1 us (25%)
  Pallas kernels  8.36 us (16%)
  local copies, waits for them, and re-layouts  2.54 us (5%)
  other arithmetic  0.62 us (1%)
    ppermute x17, starting transfers between devices, move(): lax.ppermute(x, AXES, [(number(*at), number(*to(*at))) for at in chips])  27.2 us
    ppermute x17, waiting for transfers between devices, move(): lax.ppermute(x, AXES, [(number(*at), number(*to(*at))) for at in chips])  13.1 us
    unnamed x12, local copies, waits for them, and re-layouts  2.52 us
    pallas_call x1, Pallas kernels, outer(): pl.pallas_call(functools.partial(outer_kernel, spots, depth), out_shape=o...  2.44 us
    pallas_call x2, Pallas kernels, prepare(): pl.pallas_call(prepare_kernel, out_shape=(out, out), grid=(tall // step,)...  2.2 us
    pallas_call x1, Pallas kernels, weights(): pl.pallas_call(weight_kernel, out_shape=out, in_specs=[pl.BlockSpec(memor...  1.81 us
    pallas_call x2, Pallas kernels, contract(): pl.pallas_call(contract_kernel, out_shape=out, in_specs=[pl.BlockSpec(mem...  1.57 us
  transfers between devices with their start and end apart: 17, of which 8 were waited for; matrix products, arithmetic and copies ran while one was open for 1% of the time, Pallas kernels for 11%

profile of v8, /device:TPU:5, one launch (start us, length us, event | category | flops | bytes accessed | tf_op | source)
XLA Modules:
  0.0 52.1 jit_solution(8429841742121704592)
XLA Ops:
  0.0 0.7 %collective-permute-start = (f32[32,1024]{1,0:T(8,128)}, f32[32,1024]{1,0:T(8,128)S(1)}, u32[]{:S(2)}, u32[]{:S(2)}) collective-permute-start(f32[32,1024]{1,0:T(8,128)} %bitcast.9), channel_id=1, source_target_pairs={{0,1},{1,0},{2,3},{3,2},{4,5},{5,4},{6,7},{7,6},{8,9},{9,8},{10,11... | collective-permute-start | bytes 393224 | tf_op jit(solution)/shard_map/ppermute | solution.py:246
  0.7 0.0 copy-start.1
  0.7 0.9 %copy-done.1 = f32[1024,32]{0,1:T(8,128)S(1)} copy-done((f32[1024,32]{0,1:T(8,128)S(1)}, f32[1024,32]{0,1:T(8,128)}, u32[]{:S(2)}) %copy-start.1) | copy-done | bytes 131096
  1.6 0.3 collective-permute-done
  1.9 0.4 collective-permute-start.2
  2.3 4.1 %collective-permute-start.4 = (f32[64,1024]{1,0:T(8,128)S(1)}, f32[64,1024]{1,0:T(8,128)S(1)}, u32[]{:S(2)}, u32[]{:S(2)}) collective-permute-start(f32[64,1024]{1,0:T(8,128)S(1)} %maximum_select_fusion), channel_id=1, source_target_pairs={{0,8},{1,24},{2,0},{3,16},{4,1},{5,17},{6,9},{7,25},{8,2},{9,18},{... | collective-permute-start | bytes 786440 | tf_op jit(solution)/shard_map/ppermute | solution.py:246
  6.5 4.9 %collective-permute-start.1 = (f32[64,1024]{1,0:T(8,128)S(1)}, f32[64,1024]{1,0:T(8,128)S(1)}, u32[]{:S(2)}, u32[]{:S(2)}) collective-permute-start(f32[64,1024]{1,0:T(8,128)S(1)} %maximum_select_fusion), channel_id=1, source_target_pairs={{0,0},{1,16},{2,8},{3,24},{4,9},{5,25},{6,1},{7,17},{8,10},{9,26},... | collective-permute-start | bytes 786440 | tf_op jit(solution)/shard_map/ppermute | solution.py:246
  11.3 0.0 copy-start
  11.4 1.6 %copy-done = f32[1024,512]{1,0:T(8,128)S(1)} copy-done((f32[1024,512]{1,0:T(8,128)S(1)}, f32[1024,512]{1,0:T(8,128)}, u32[]{:S(2)}) %copy-start) | copy-done | bytes 2097176
  12.9 1.1 %prepare.2 = (bf16[512,1024]{1,0:T(8,128)(2,1)S(1)}, bf16[512,1024]{1,0:T(8,128)(2,1)S(1)}) custom-call(f32[1024,512]{1,0:T(8,128)S(1)} %copy-done), custom_call_target="tpu_custom_call" | custom-call | bytes 4194304 | tf_op jit(solution)/shard_map/prepare/pallas_call | solution.py:42
  14.0 0.0 collective-permute-done.2.block_ref
  14.0 1.1 %prepare.3 = (bf16[512,1024]{1,0:T(8,128)(2,1)S(1)}, bf16[512,1024]{1,0:T(8,128)(2,1)S(1)}) custom-call(f32[1024,512]{1,0:T(8,128)S(1)} %collective-permute-done.2.block_ref), custom_call_target="tpu_custom_call" | custom-call | bytes 4194304 | tf_op jit(solution)/shard_map/prepare/pallas_call | solution.py:42
  15.2 0.0 collective-permute-done.4.factors_ref
  15.2 0.8 %contract.3 = f32[64,1024]{1,0:T(8,128)S(1)} custom-call(s32[1]{0:T(128)} %bitcast.core, f32[64,1024]{1,0:T(8,128)S(1)} %collective-permute-done.4.factors_ref, bf16[512,1024]{1,0:T(8,128)(2,1)S(1)} %get-tuple-element.20.refs_0_, bf16[512,1024]{1,0:T(8,128)(2,1)S(1)} %get-tuple-element.21.refs_1_, bf16[512,1024]{1,0:T(8,128)(2,1)S(1)} %get-tuple-element.22.refs_2_, ...), custom_call_target="tpu_custom_call" | custom-call | flops 402653184 | bytes 4194304 | tf_op jit(solution)/shard_map/contract/pallas_call | solution.py:72
  16.0 1.9 %collective-permute-start.5 = (f32[64,1024]{1,0:T(8,128)S(1)}, f32[64,1024]{1,0:T(8,128)S(1)}, u32[]{:S(2)}, u32[]{:S(2)}) collective-permute-start(f32[64,1024]{1,0:T(8,128)S(1)} %contract.3), channel_id=1, source_target_pairs={{0,2},{1,5},{2,0},{3,7},{4,6},{5,1},{6,4},{7,3},{8,8},{9,15},{10,1... | collective-permute-start | bytes 786440 | tf_op jit(solution)/shard_map/ppermute | solution.py:246
  17.9 2.9 %collective-permute-done.1.factors_ref = f32[64,1024]{1,0:T(8,128)S(1)} collective-permute-done((f32[64,1024]{1,0:T(8,128)S(1)}, f32[64,1024]{1,0:T(8,128)S(1)}, u32[]{:S(2)}, u32[]{:S(2)}) %collective-permute-start.1) | collective-permute-done | bytes 262176 | tf_op jit(solution)/shard_map/ppermute | solution.py:246
  20.8 0.8 %contract.2 = f32[64,1024]{1,0:T(8,128)S(1)} custom-call(s32[1]{0:T(128)} %bitcast.core, f32[64,1024]{1,0:T(8,128)S(1)} %collective-permute-done.1.factors_ref, bf16[512,1024]{1,0:T(8,128)(2,1)S(1)} %get-tuple-element.20.refs_0_, bf16[512,1024]{1,0:T(8,128)(2,1)S(1)} %get-tuple-element.21.refs_1_, bf16[512,1024]{1,0:T(8,128)(2,1)S(1)} %get-tuple-element.22.refs_2_, ...), custom_call_target="tpu_custom_call" | custom-call | flops 402653184 | bytes 4194304 | tf_op jit(solution)/shard_map/contract/pallas_call | solution.py:72
  21.6 0.0 copy-start.5
  21.6 0.0 copy-start.2
  21.6 0.0 copy-start.3
  21.6 0.0 copy-start.4
  21.7 2.1 %collective-permute-start.3 = (f32[64,1024]{1,0:T(8,128)S(1)}, f32[64,1024]{1,0:T(8,128)S(1)}, u32[]{:S(2)}, u32[]{:S(2)}) collective-permute-start(f32[64,1024]{1,0:T(8,128)S(1)} %contract.2), channel_id=1, source_target_pairs={{0,0},{1,7},{2,2},{3,5},{4,4},{5,3},{6,6},{7,1},{8,10},{9,13},{10,... | collective-permute-start | bytes 786440 | tf_op jit(solution)/shard_map/ppermute | solution.py:246
  23.7 0.2 collective-permute-done.5
  23.9 5.9 %collective-permute-done.3 = f32[64,1024]{1,0:T(8,128)S(1)} collective-permute-done((f32[64,1024]{1,0:T(8,128)S(1)}, f32[64,1024]{1,0:T(8,128)S(1)}, u32[]{:S(2)}, u32[]{:S(2)}) %collective-permute-start.3) | collective-permute-done | bytes 262176 | tf_op jit(solution)/shard_map/ppermute | solution.py:246
  29.8 0.1 collective-permute-start.6
  29.9 1.5 %collective-permute-done.6 = f32[64,1024]{1,0:T(8,128)S(1)} collective-permute-done((f32[64,1024]{1,0:T(8,128)S(1)}, f32[64,1024]{1,0:T(8,128)S(1)}, u32[]{:S(2)}, u32[]{:S(2)}) %collective-permute-start.6) | collective-permute-done | bytes 262176 | tf_op jit(solution)/shard_map/ppermute | solution.py:246
  31.5 3.2 %collective-permute-start.11 = (f32[64,1024]{1,0:T(8,128)S(1)}, f32[64,1024]{1,0:T(8,128)S(1)}, u32[]{:S(2)}, u32[]{:S(2)}) collective-permute-start(f32[64,1024]{1,0:T(8,128)S(1)} %add.22), channel_id=1, source_target_pairs={{0,0},{1,16},{2,8},{3,24},{4,9},{5,25},{6,1},{7,17},{8,10},{9,26},... | collective-permute-start | bytes 786440 | tf_op jit(solution)/shard_map/ppermute | solution.py:246
  34.7 0.0 copy-done.5
  34.8 0.1 collective-permute-start.7
  34.8 3.3 %collective-permute-start.8 = (f32[64,1024]{1,0:T(8,128)S(1)}, f32[64,1024]{1,0:T(8,128)S(1)}, u32[]{:S(2)}, u32[]{:S(2)}) collective-permute-start(f32[64,1024]{1,0:T(8,128)S(1)} %add.22), channel_id=1, source_target_pairs={{0,0},{1,7},{2,2},{3,5},{4,4},{5,3},{6,6},{7,1},{8,8},{9,15},{10,1... | collective-permute-start | bytes 786440 | tf_op jit(solution)/shard_map/ppermute | solution.py:246
  38.2 0.1 pad_add_fusion.3.place
  38.3 4.8 %collective-permute-start.12 = (f32[32,1024]{1,0:T(8,128)S(1)}, f32[32,1024]{1,0:T(8,128)S(1)}, u32[]{:S(2)}, u32[]{:S(2)}) collective-permute-start(f32[32,1024]{1,0:T(8,128)S(1)} %slice.8), channel_id=1, source_target_pairs={{0,8},{1,24},{2,0},{3,16},{4,1},{5,17},{6,9},{7,25},{8,2},{9,18},{... | collective-permute-start | bytes 393224 | tf_op jit(solution)/shard_map/ppermute | solution.py:246
  43.1 0.0 collective-permute-done.11.refs_0_
  43.1 0.3 collective-permute-start.13
  43.4 0.1 pad_add_fusion
  43.5 0.0 copy-done.2
  43.5 0.0 copy-done.3
  43.5 0.0 copy-done.4
  43.5 1.8 %weights.1.weights_ref = f32[1024,512]{1,0:T(8,128)S(1)} custom-call(s32[2]{0:T(128)S(1)} %pad_add_fusion.3.place, s32[1,4096]{1,0:T(1,128)S(1)} %bitcast.11, s32[1,4096]{1,0:T(1,128)S(1)} %bitcast.12, f32[1,128]{1,0:T(1,128)S(1)} %pad_bitcast_fusion.occ_table, f32[16,128]{1,0:T(8,128)S(1)} %bitcast.13), custom_call_target="tpu_custom_call" | custom-call | bytes 2097152 | tf_op jit(solution)/shard_map/weights/pallas_call | solution.py:138
  45.3 0.0 collective-permute-done.7.refs_1_
  45.3 0.7 %collective-permute-start.10 = (f32[64,1024]{1,0:T(8,128)S(1)}, f32[64,1024]{1,0:T(8,128)S(1)}, u32[]{:S(2)}, u32[]{:S(2)}) collective-permute-start(f32[64,1024]{1,0:T(8,128)S(1)} %collective-permute-done.7.refs_1_), channel_id=1, source_target_pairs={{0,1},{1,0},{2,3},{3,2},{4,5},{5,4},{6,7},{7,6},{8,9},{9,8},{10,11... | collective-permute-start | bytes 786440 | tf_op jit(solution)/shard_map/ppermute | solution.py:246
  46.0 0.1 collective-permute-start.14
  46.1 1.7 %collective-permute-done.8.refs_0_ = f32[64,1024]{1,0:T(8,128)S(1)} collective-permute-done((f32[64,1024]{1,0:T(8,128)S(1)}, f32[64,1024]{1,0:T(8,128)S(1)}, u32[]{:S(2)}, u32[]{:S(2)}) %collective-permute-start.8) | collective-permute-done | bytes 262176 | tf_op jit(solution)/shard_map/ppermute | solution.py:246
  47.8 0.0 collective-permute-start.9
  47.8 0.1 pad_add_fusion.1
  47.8 0.0 collective-permute-done.12.refs_1_
  47.8 0.5 collective-permute-start.15
  48.3 0.0 collective-permute-done.13.refs_2_
  48.4 0.1 collective-permute-start.16
  48.5 0.2 select_reduce_fusion
  48.7 0.1 pad_add_fusion.2.place
  48.7 0.0 collective-permute-done.10.refs_3_
  48.7 0.6 %collective-permute-done.9.refs_2_ = f32[64,1024]{1,0:T(8,128)S(1)} collective-permute-done((f32[64,1024]{1,0:T(8,128)S(1)}, f32[64,1024]{1,0:T(8,128)S(1)}, u32[]{:S(2)}, u32[]{:S(2)}) %collective-permute-start.9) | collective-permute-done | bytes 262176 | tf_op jit(solution)/shard_map/ppermute | solution.py:246
  49.3 0.3 left_parts.1
  49.6 0.0 collective-permute-done.15.refs_4_
  49.6 0.1 collective-permute-done.16.refs_5_
  49.7 0.0 collective-permute-done.14.refs_3_
  49.7 2.4 %outer.1 = f32[1024,512]{1,0:T(8,128)} custom-call(s32[5]{0:T(128)S(1)} %pad_add_fusion.2.place, f32[1024,512]{1,0:T(8,128)S(1)} %weights.1.weights_ref, bf16[1024,256]{1,0:T(8,128)(2,1)S(1)} %get-tuple-element.29.left_high, bf16[1024,256]{1,0:T(8,128)(2,1)S(1)} %get-tuple-element.30.left_low, f32[64,1024]{1,0:T(8,128)S(1)} %collective-permute-done.11.refs_0_, ...), custom_call_target="tpu_custom_call" | custom-call | flops 805306368 | bytes 2097152 | tf_op jit(solution)/shard_map/outer/pallas_call | solution.py:213
  (10 shorter events, 0.2 us)
Async XLA Ops:
  0.0 1.9 %collective-permute-start = (f32[32,1024]{1,0:T(8,128)}, f32[32,1024]{1,0:T(8,128)S(1)}, u32[]{:S(2)}, u32[]{:S(2)}) collective-permute-start(f32[32,1024]{1,0:T(8,128)} %bitcast.9), channel_id=1, source_target_pairs={{0,1},{1,0},{2,3},{3,2},{4,5},{5,4},{6,7},{7,6},{8,9},{9,8},{10,11... | collective-permute-start | bytes 393224 | tf_op jit(solution)/shard_map/ppermute | solution.py:246
  0.7 0.9 %copy-start.1 = (f32[1024,32]{0,1:T(8,128)S(1)}, f32[1024,32]{0,1:T(8,128)}, u32[]{:S(2)}) copy-start(f32[1024,32]{0,1:T(8,128)} %param.7) | copy-start | bytes 393220
  1.9 12.1 %collective-permute-start.2 = (f32[1024,512]{1,0:T(8,128)}, f32[1024,512]{1,0:T(8,128)S(1)}, u32[]{:S(2)}, u32[]{:S(2)}) collective-permute-start(f32[1024,512]{1,0:T(8,128)} %block_ref), channel_id=1, source_target_pairs={{0,1},{1,0},{2,3},{3,2},{4,5},{5,4},{6,7},{7,6},{8,9},{9,8},{10,11... | collective-permute-start | bytes 6291464 | tf_op jit(solution)/shard_map/ppermute | solution.py:246
  2.3 12.8 %collective-permute-start.4 = (f32[64,1024]{1,0:T(8,128)S(1)}, f32[64,1024]{1,0:T(8,128)S(1)}, u32[]{:S(2)}, u32[]{:S(2)}) collective-permute-start(f32[64,1024]{1,0:T(8,128)S(1)} %maximum_select_fusion), channel_id=1, source_target_pairs={{0,8},{1,24},{2,0},{3,16},{4,1},{5,17},{6,9},{7,25},{8,2},{9,18},{... | collective-permute-start | bytes 786440 | tf_op jit(solution)/shard_map/ppermute | solution.py:246
  6.5 14.3 %collective-permute-start.1 = (f32[64,1024]{1,0:T(8,128)S(1)}, f32[64,1024]{1,0:T(8,128)S(1)}, u32[]{:S(2)}, u32[]{:S(2)}) collective-permute-start(f32[64,1024]{1,0:T(8,128)S(1)} %maximum_select_fusion), channel_id=1, source_target_pairs={{0,0},{1,16},{2,8},{3,24},{4,9},{5,25},{6,1},{7,17},{8,10},{9,26},... | collective-permute-start | bytes 786440 | tf_op jit(solution)/shard_map/ppermute | solution.py:246
  11.3 1.6 %copy-start = (f32[1024,512]{1,0:T(8,128)S(1)}, f32[1024,512]{1,0:T(8,128)}, u32[]{:S(2)}) copy-start(f32[1024,512]{1,0:T(8,128)} %block_ref) | copy-start | bytes 6291460
  16.0 7.9 %collective-permute-start.5 = (f32[64,1024]{1,0:T(8,128)S(1)}, f32[64,1024]{1,0:T(8,128)S(1)}, u32[]{:S(2)}, u32[]{:S(2)}) collective-permute-start(f32[64,1024]{1,0:T(8,128)S(1)} %contract.3), channel_id=1, source_target_pairs={{0,2},{1,5},{2,0},{3,7},{4,6},{5,1},{6,4},{7,3},{8,8},{9,15},{10,1... | collective-permute-start | bytes 786440 | tf_op jit(solution)/shard_map/ppermute | solution.py:246
  21.6 13.1 %copy-start.5 = (f32[64]{0:T(128)S(1)}, f32[64]{0:T(128)}, u32[]{:S(2)}) copy-start(f32[64]{0:T(128)} %param.10) | copy-start | bytes 772
  21.6 21.9 %copy-start.2 = (s32[4096]{0:T(1024)S(1)}, s32[4096]{0:T(1024)}, u32[]{:S(2)}) copy-start(s32[4096]{0:T(1024)} %param.8) | copy-start | bytes 49156
  21.6 21.9 %copy-start.3 = (s32[4096]{0:T(1024)S(1)}, s32[4096]{0:T(1024)}, u32[]{:S(2)}) copy-start(s32[4096]{0:T(1024)} %param.9) | copy-start | bytes 49156
  21.6 21.9 %copy-start.4 = (f32[2048]{0:T(1024)S(1)}, f32[2048]{0:T(1024)}, u32[]{:S(2)}) copy-start(f32[2048]{0:T(1024)} %param.11) | copy-start | bytes 24580
  21.7 8.1 %collective-permute-start.3 = (f32[64,1024]{1,0:T(8,128)S(1)}, f32[64,1024]{1,0:T(8,128)S(1)}, u32[]{:S(2)}, u32[]{:S(2)}) collective-permute-start(f32[64,1024]{1,0:T(8,128)S(1)} %contract.2), channel_id=1, source_target_pairs={{0,0},{1,7},{2,2},{3,5},{4,4},{5,3},{6,6},{7,1},{8,10},{9,13},{10,... | collective-permute-start | bytes 786440 | tf_op jit(solution)/shard_map/ppermute | solution.py:246
  29.8 1.6 %collective-permute-start.6 = (f32[64,1024]{1,0:T(8,128)S(1)}, f32[64,1024]{1,0:T(8,128)S(1)}, u32[]{:S(2)}, u32[]{:S(2)}) collective-permute-start(f32[64,1024]{1,0:T(8,128)S(1)} %add.20), channel_id=1, source_target_pairs={{0,1},{1,0},{2,3},{3,2},{4,5},{5,4},{6,7},{7,6},{8,9},{9,8},{10,11... | collective-permute-start | bytes 786440 | tf_op jit(solution)/shard_map/ppermute | solution.py:246
  31.5 11.6 %collective-permute-start.11 = (f32[64,1024]{1,0:T(8,128)S(1)}, f32[64,1024]{1,0:T(8,128)S(1)}, u32[]{:S(2)}, u32[]{:S(2)}) collective-permute-start(f32[64,1024]{1,0:T(8,128)S(1)} %add.22), channel_id=1, source_target_pairs={{0,0},{1,16},{2,8},{3,24},{4,9},{5,25},{6,1},{7,17},{8,10},{9,26},... | collective-permute-start | bytes 786440 | tf_op jit(solution)/shard_map/ppermute | solution.py:246
  34.8 10.6 %collective-permute-start.7 = (f32[64,1024]{1,0:T(8,128)S(1)}, f32[64,1024]{1,0:T(8,128)S(1)}, u32[]{:S(2)}, u32[]{:S(2)}) collective-permute-start(f32[64,1024]{1,0:T(8,128)S(1)} %add.22), channel_id=1, source_target_pairs={{0,2},{1,5},{2,0},{3,7},{4,6},{5,1},{6,4},{7,3},{8,10},{9,13},{10,... | collective-permute-start | bytes 786440 | tf_op jit(solution)/shard_map/ppermute | solution.py:246
  34.8 12.9 %collective-permute-start.8 = (f32[64,1024]{1,0:T(8,128)S(1)}, f32[64,1024]{1,0:T(8,128)S(1)}, u32[]{:S(2)}, u32[]{:S(2)}) collective-permute-start(f32[64,1024]{1,0:T(8,128)S(1)} %add.22), channel_id=1, source_target_pairs={{0,0},{1,7},{2,2},{3,5},{4,4},{5,3},{6,6},{7,1},{8,8},{9,15},{10,1... | collective-permute-start | bytes 786440 | tf_op jit(solution)/shard_map/ppermute | solution.py:246
  38.3 9.6 %collective-permute-start.12 = (f32[32,1024]{1,0:T(8,128)S(1)}, f32[32,1024]{1,0:T(8,128)S(1)}, u32[]{:S(2)}, u32[]{:S(2)}) collective-permute-start(f32[32,1024]{1,0:T(8,128)S(1)} %slice.8), channel_id=1, source_target_pairs={{0,8},{1,24},{2,0},{3,16},{4,1},{5,17},{6,9},{7,25},{8,2},{9,18},{... | collective-permute-start | bytes 393224 | tf_op jit(solution)/shard_map/ppermute | solution.py:246
  43.1 5.3 %collective-permute-start.13 = (f32[32,1024]{1,0:T(8,128)S(1)}, f32[32,1024]{1,0:T(8,128)S(1)}, u32[]{:S(2)}, u32[]{:S(2)}) collective-permute-start(f32[32,1024]{1,0:T(8,128)S(1)} %slice.9), channel_id=1, source_target_pairs={{0,8},{1,9},{2,10},{3,11},{4,12},{5,13},{6,14},{7,15},{8,0},{9,1},... | collective-permute-start | bytes 393224 | tf_op jit(solution)/shard_map/ppermute | solution.py:246
  45.3 3.4 %collective-permute-start.10 = (f32[64,1024]{1,0:T(8,128)S(1)}, f32[64,1024]{1,0:T(8,128)S(1)}, u32[]{:S(2)}, u32[]{:S(2)}) collective-permute-start(f32[64,1024]{1,0:T(8,128)S(1)} %collective-permute-done.7.refs_1_), channel_id=1, source_target_pairs={{0,1},{1,0},{2,3},{3,2},{4,5},{5,4},{6,7},{7,6},{8,9},{9,8},{10,11... | collective-permute-start | bytes 786440 | tf_op jit(solution)/shard_map/ppermute | solution.py:246
  46.0 3.7 %collective-permute-start.14 = (f32[64,1024]{1,0:T(8,128)S(1)}, f32[64,1024]{1,0:T(8,128)S(1)}, u32[]{:S(2)}, u32[]{:S(2)}) collective-permute-start(f32[64,1024]{1,0:T(8,128)S(1)} %collective-permute-done.11.refs_0_), channel_id=1, source_target_pairs={{0,1},{1,0},{2,3},{3,2},{4,5},{5,4},{6,7},{7,6},{8,9},{9,8},{10,11... | collective-permute-start | bytes 786440 | tf_op jit(solution)/shard_map/ppermute | solution.py:246
  47.8 1.5 %collective-permute-start.9 = (f32[64,1024]{1,0:T(8,128)S(1)}, f32[64,1024]{1,0:T(8,128)S(1)}, u32[]{:S(2)}, u32[]{:S(2)}) collective-permute-start(f32[64,1024]{1,0:T(8,128)S(1)} %collective-permute-done.8.refs_0_), channel_id=1, source_target_pairs={{0,1},{1,0},{2,3},{3,2},{4,5},{5,4},{6,7},{7,6},{8,9},{9,8},{10,11... | collective-permute-start | bytes 786440 | tf_op jit(solution)/shard_map/ppermute | solution.py:246
  47.8 1.8 %collective-permute-start.15 = (f32[32,1024]{1,0:T(8,128)S(1)}, f32[32,1024]{1,0:T(8,128)S(1)}, u32[]{:S(2)}, u32[]{:S(2)}) collective-permute-start(f32[32,1024]{1,0:T(8,128)S(1)} %collective-permute-done.12.refs_1_), channel_id=1, source_target_pairs={{0,1},{1,0},{2,3},{3,2},{4,5},{5,4},{6,7},{7,6},{8,9},{9,8},{10,11... | collective-permute-start | bytes 393224 | tf_op jit(solution)/shard_map/ppermute | solution.py:246
  48.4 1.3 %collective-permute-start.16 = (f32[32,1024]{1,0:T(8,128)S(1)}, f32[32,1024]{1,0:T(8,128)S(1)}, u32[]{:S(2)}, u32[]{:S(2)}) collective-permute-start(f32[32,1024]{1,0:T(8,128)S(1)} %collective-permute-done.13.refs_2_), channel_id=1, source_target_pairs={{0,1},{1,0},{2,3},{3,2},{4,5},{5,4},{6,7},{7,6},{8,9},{9,8},{10,11... | collective-permute-start | bytes 393224 | tf_op jit(solution)/shard_map/ppermute | solution.py:246

commit v9 on v8

--- a/solution.py
+++ b/solution.py
@@ -252,11 +252,11 @@
         low = z % share ^ i
         return rows - 1 - low if s else low
 
-    def transposed(x, i):
+    def transposed(x, i, swapped=lambda z: z // share):
         def to(z, j, s):
             side, low = divmod(j ^ z, share)
             low = share - 1 - low if side else low
-            return (s ^ z // share) * share + (low ^ i), z, side
+            return (s ^ swapped(z)) * share + (low ^ i), z, side
 
         return move(x, to)
 
@@ -287,22 +287,22 @@
     amplitudes, pieces = lax.optimization_barrier((amplitudes, pieces))
     blocks = prepare(amplitudes), prepare(swap(amplitudes))
     partial = [contract(core, x, *blocks) for x in received]
+    partial[1], occ_index, vir_index = lax.optimization_barrier((partial[1], occ_index, vir_index))
     arrived = [reduced(partial[i], i) for i in turns]
+    factor = weights(
+        jnp.stack([row_index, col_index]), occ_index, vir_index, occ_energy, vir_energy, tall, wide
+    )
+    arrived[1], factor = lax.optimization_barrier((arrived[1], factor))
     total = functools.reduce(jnp.add, arrived)
     total = total + swap(total)
-    total, occ_index, vir_index = lax.optimization_barrier((total, occ_index, vir_index))
     dressed = pieces + total
-    factor = weights(
-        jnp.stack([row_index, col_index]), occ_index, vir_index, occ_energy, vir_energy, tall, wide
-    )
     left = [across(dressed, i) for i in turns]
     part = dressed.shape[0] // 2
-    right, spots = [transposed(dressed, 0)], [(0, 0)]
+    right, spots = [transposed(dressed, 0, lambda z: z % 2)], [(0, 0)]
     for v in range(1, share):
         right += [transposed(dressed[part:], v), within_half(right[0][:part], v)]
         spots += [(v, part), (v, 0)]
     spots += [(share + slot, offset) for slot, offset in spots]
-    left[1], factor = lax.optimization_barrier((left[1], factor))
     left += [swap(x) for x in left]
     right += [swap(x) for x in right]
     order = jnp.where(core == 0, first, rows - 1 - first)

time: 52.9 us -> 52.5 us (level)
  starting transfers between devices: 27.2 us -> 25.3 us
  waiting for transfers between devices: 13.1 us -> 14.9 us
    ppermute x17, starting transfers between devices: 27.2 us -> 25.3 us  [move(): lax.ppermute(x, AXES, [(number(*at), number(*to(*at))) for at in chips])]
    ppermute x17, waiting for transfers between devices: 13.1 us -> 14.9 us  [move(): lax.ppermute(x, AXES, [(number(*at), number(*to(*at))) for at in chips])]
  transfers between devices with their start and end apart: 17 -> 17, of which waited for: 8 -> 9; matrix products, arithmetic and copies ran while one was open for 1% -> 1% of each run, Pallas kernels for 11% -> 11%
where the time goes in v9:
time: 52.5 us; the launch traced here: 52 us
  starting transfers between devices  25.3 us (48%)
  waiting for transfers between devices  14.9 us (28%)
  Pallas kernels  8.37 us (16%)
  local copies, waits for them, and re-layouts  2.54 us (5%)
  other arithmetic  0.61 us (1%)
    ppermute x17, starting transfers between devices, move(): lax.ppermute(x, AXES, [(number(*at), number(*to(*at))) for at in chips])  25.3 us
    ppermute x17, waiting for transfers between devices, move(): lax.ppermute(x, AXES, [(number(*at), number(*to(*at))) for at in chips])  14.9 us
    unnamed x12, local copies, waits for them, and re-layouts  2.52 us
    pallas_call x1, Pallas kernels, outer(): pl.pallas_call(functools.partial(outer_kernel, spots, depth), out_shape=o...  2.43 us
    pallas_call x2, Pallas kernels, prepare(): pl.pallas_call(prepare_kernel, out_shape=(out, out), grid=(tall // step,)...  2.2 us
    pallas_call x1, Pallas kernels, weights(): pl.pallas_call(weight_kernel, out_shape=out, in_specs=[pl.BlockSpec(memor...  1.81 us
    pallas_call x2, Pallas kernels, contract(): pl.pallas_call(contract_kernel, out_shape=out, in_specs=[pl.BlockSpec(mem...  1.58 us
  transfers between devices with their start and end apart: 17, of which 9 were waited for; matrix products, arithmetic and copies ran while one was open for 1% of the time, Pallas kernels for 11%

profile of v9, /device:TPU:5, one launch (start us, length us, event | category | flops | bytes accessed | tf_op | source)
XLA Modules:
  0.0 52.0 jit_solution(9169677037220651814)
XLA Ops:
  0.0 0.7 %collective-permute-start = (f32[32,1024]{1,0:T(8,128)}, f32[32,1024]{1,0:T(8,128)S(1)}, u32[]{:S(2)}, u32[]{:S(2)}) collective-permute-start(f32[32,1024]{1,0:T(8,128)} %bitcast.9), channel_id=1, source_target_pairs={{0,1},{1,0},{2,3},{3,2},{4,5},{5,4},{6,7},{7,6},{8,9},{9,8},{10,11... | collective-permute-start | bytes 393224 | tf_op jit(solution)/shard_map/ppermute | solution.py:246
  0.7 0.0 copy-start.1
  0.7 0.9 %copy-done.1 = f32[1024,32]{0,1:T(8,128)S(1)} copy-done((f32[1024,32]{0,1:T(8,128)S(1)}, f32[1024,32]{0,1:T(8,128)}, u32[]{:S(2)}) %copy-start.1) | copy-done | bytes 131096
  1.6 0.3 collective-permute-done
  1.9 0.4 collective-permute-start.2
  2.3 4.1 %collective-permute-start.1 = (f32[64,1024]{1,0:T(8,128)S(1)}, f32[64,1024]{1,0:T(8,128)S(1)}, u32[]{:S(2)}, u32[]{:S(2)}) collective-permute-start(f32[64,1024]{1,0:T(8,128)S(1)} %maximum_select_fusion), channel_id=1, source_target_pairs={{0,8},{1,24},{2,0},{3,16},{4,1},{5,17},{6,9},{7,25},{8,2},{9,18},{... | collective-permute-start | bytes 786440 | tf_op jit(solution)/shard_map/ppermute | solution.py:246
  6.5 4.9 %collective-permute-start.4 = (f32[64,1024]{1,0:T(8,128)S(1)}, f32[64,1024]{1,0:T(8,128)S(1)}, u32[]{:S(2)}, u32[]{:S(2)}) collective-permute-start(f32[64,1024]{1,0:T(8,128)S(1)} %maximum_select_fusion), channel_id=1, source_target_pairs={{0,0},{1,16},{2,8},{3,24},{4,9},{5,25},{6,1},{7,17},{8,10},{9,26},... | collective-permute-start | bytes 786440 | tf_op jit(solution)/shard_map/ppermute | solution.py:246
  11.3 0.0 copy-start
  11.4 1.6 %copy-done = f32[1024,512]{1,0:T(8,128)S(1)} copy-done((f32[1024,512]{1,0:T(8,128)S(1)}, f32[1024,512]{1,0:T(8,128)}, u32[]{:S(2)}) %copy-start) | copy-done | bytes 2097176
  12.9 1.1 %prepare.2 = (bf16[512,1024]{1,0:T(8,128)(2,1)S(1)}, bf16[512,1024]{1,0:T(8,128)(2,1)S(1)}) custom-call(f32[1024,512]{1,0:T(8,128)S(1)} %copy-done), custom_call_target="tpu_custom_call" | custom-call | bytes 4194304 | tf_op jit(solution)/shard_map/prepare/pallas_call | solution.py:42
  14.0 0.0 collective-permute-done.2.block_ref
  14.0 1.1 %prepare.3 = (bf16[512,1024]{1,0:T(8,128)(2,1)S(1)}, bf16[512,1024]{1,0:T(8,128)(2,1)S(1)}) custom-call(f32[1024,512]{1,0:T(8,128)S(1)} %collective-permute-done.2.block_ref), custom_call_target="tpu_custom_call" | custom-call | bytes 4194304 | tf_op jit(solution)/shard_map/prepare/pallas_call | solution.py:42
  15.2 0.0 collective-permute-done.1.factors_ref
  15.2 0.8 %contract.2 = f32[64,1024]{1,0:T(8,128)S(1)} custom-call(s32[1]{0:T(128)} %bitcast.core, f32[64,1024]{1,0:T(8,128)S(1)} %collective-permute-done.1.factors_ref, bf16[512,1024]{1,0:T(8,128)(2,1)S(1)} %get-tuple-element.19.refs_0_, bf16[512,1024]{1,0:T(8,128)(2,1)S(1)} %get-tuple-element.20.refs_1_, bf16[512,1024]{1,0:T(8,128)(2,1)S(1)} %get-tuple-element.21.refs_2_, ...), custom_call_target="tpu_custom_call" | custom-call | flops 402653184 | bytes 4194304 | tf_op jit(solution)/shard_map/contract/pallas_call | solution.py:72
  16.0 0.0 copy-start.5
  16.0 0.0 copy-start.2
  16.0 0.0 copy-start.3
  16.0 0.0 copy-start.4
  16.0 2.1 %collective-permute-start.3 = (f32[64,1024]{1,0:T(8,128)S(1)}, f32[64,1024]{1,0:T(8,128)S(1)}, u32[]{:S(2)}, u32[]{:S(2)}) collective-permute-start(f32[64,1024]{1,0:T(8,128)S(1)} %contract.2), channel_id=1, source_target_pairs={{0,2},{1,5},{2,0},{3,7},{4,6},{5,1},{6,4},{7,3},{8,8},{9,15},{10,1... | collective-permute-start | bytes 786440 | tf_op jit(solution)/shard_map/ppermute | solution.py:246
  18.1 2.7 %collective-permute-done.4.factors_ref = f32[64,1024]{1,0:T(8,128)S(1)} collective-permute-done((f32[64,1024]{1,0:T(8,128)S(1)}, f32[64,1024]{1,0:T(8,128)S(1)}, u32[]{:S(2)}, u32[]{:S(2)}) %collective-permute-start.4) | collective-permute-done | bytes 262176 | tf_op jit(solution)/shard_map/ppermute | solution.py:246
  20.8 0.8 %contract.3 = f32[64,1024]{1,0:T(8,128)S(1)} custom-call(s32[1]{0:T(128)} %bitcast.core, f32[64,1024]{1,0:T(8,128)S(1)} %collective-permute-done.4.factors_ref, bf16[512,1024]{1,0:T(8,128)(2,1)S(1)} %get-tuple-element.19.refs_0_, bf16[512,1024]{1,0:T(8,128)(2,1)S(1)} %get-tuple-element.20.refs_1_, bf16[512,1024]{1,0:T(8,128)(2,1)S(1)} %get-tuple-element.21.refs_2_, ...), custom_call_target="tpu_custom_call" | custom-call | flops 402653184 | bytes 4194304 | tf_op jit(solution)/shard_map/contract/pallas_call | solution.py:72
  21.6 1.9 %collective-permute-start.5 = (f32[64,1024]{1,0:T(8,128)S(1)}, f32[64,1024]{1,0:T(8,128)S(1)}, u32[]{:S(2)}, u32[]{:S(2)}) collective-permute-start(f32[64,1024]{1,0:T(8,128)S(1)} %contract.3), channel_id=1, source_target_pairs={{0,0},{1,7},{2,2},{3,5},{4,4},{5,3},{6,6},{7,1},{8,10},{9,13},{10,... | collective-permute-start | bytes 786440 | tf_op jit(solution)/shard_map/ppermute | solution.py:246
  23.5 0.0 copy-done.5
  23.5 0.1 pad_add_fusion.3.place
  23.6 0.0 copy-done.2
  23.6 0.0 copy-done.3
  23.6 0.0 copy-done.4
  23.6 1.8 %weights.1.weights_ref = f32[1024,512]{1,0:T(8,128)S(1)} custom-call(s32[2]{0:T(128)S(1)} %pad_add_fusion.3.place, s32[1,4096]{1,0:T(1,128)S(1)} %bitcast.11, s32[1,4096]{1,0:T(1,128)S(1)} %bitcast.12, f32[1,128]{1,0:T(1,128)S(1)} %pad_bitcast_fusion.occ_table, f32[16,128]{1,0:T(8,128)S(1)} %bitcast.13), custom_call_target="tpu_custom_call" | custom-call | bytes 2097152 | tf_op jit(solution)/shard_map/weights/pallas_call | solution.py:138
  25.4 0.0 collective-permute-done.3
  25.5 4.1 %collective-permute-done.5 = f32[64,1024]{1,0:T(8,128)S(1)} collective-permute-done((f32[64,1024]{1,0:T(8,128)S(1)}, f32[64,1024]{1,0:T(8,128)S(1)}, u32[]{:S(2)}, u32[]{:S(2)}) %collective-permute-start.5) | collective-permute-done | bytes 262176 | tf_op jit(solution)/shard_map/ppermute | solution.py:246
  29.6 0.1 collective-permute-start.6
  29.7 1.5 %collective-permute-done.6 = f32[64,1024]{1,0:T(8,128)S(1)} collective-permute-done((f32[64,1024]{1,0:T(8,128)S(1)}, f32[64,1024]{1,0:T(8,128)S(1)}, u32[]{:S(2)}, u32[]{:S(2)}) %collective-permute-start.6) | collective-permute-done | bytes 262176 | tf_op jit(solution)/shard_map/ppermute | solution.py:246
  31.2 0.1 add_add_fusion
  31.3 3.6 %collective-permute-start.11 = (f32[64,1024]{1,0:T(8,128)S(1)}, f32[64,1024]{1,0:T(8,128)S(1)}, u32[]{:S(2)}, u32[]{:S(2)}) collective-permute-start(f32[64,1024]{1,0:T(8,128)S(1)} %add_add_fusion), channel_id=1, source_target_pairs={{0,0},{1,16},{2,8},{3,24},{4,9},{5,25},{6,1},{7,17},{8,26},{9,10},... | collective-permute-start | bytes 786440 | tf_op jit(solution)/shard_map/ppermute | solution.py:246
  34.9 0.1 collective-permute-start.8
  35.0 3.3 %collective-permute-start.7 = (f32[64,1024]{1,0:T(8,128)S(1)}, f32[64,1024]{1,0:T(8,128)S(1)}, u32[]{:S(2)}, u32[]{:S(2)}) collective-permute-start(f32[64,1024]{1,0:T(8,128)S(1)} %add_add_fusion), channel_id=1, source_target_pairs={{0,0},{1,7},{2,2},{3,5},{4,4},{5,3},{6,6},{7,1},{8,8},{9,15},{10,1... | collective-permute-start | bytes 786440 | tf_op jit(solution)/shard_map/ppermute | solution.py:246
  38.4 2.5 %collective-permute-start.12 = (f32[32,1024]{1,0:T(8,128)S(1)}, f32[32,1024]{1,0:T(8,128)S(1)}, u32[]{:S(2)}, u32[]{:S(2)}) collective-permute-start(f32[32,1024]{1,0:T(8,128)S(1)} %slice.8), channel_id=1, source_target_pairs={{0,8},{1,24},{2,0},{3,16},{4,1},{5,17},{6,9},{7,25},{8,2},{9,18},{... | collective-permute-start | bytes 393224 | tf_op jit(solution)/shard_map/ppermute | solution.py:246
  40.9 1.7 %collective-permute-done.11.refs_0_ = f32[64,1024]{1,0:T(8,128)S(1)} collective-permute-done((f32[64,1024]{1,0:T(8,128)S(1)}, f32[64,1024]{1,0:T(8,128)S(1)}, u32[]{:S(2)}, u32[]{:S(2)}) %collective-permute-start.11) | collective-permute-done | bytes 262176 | tf_op jit(solution)/shard_map/ppermute | solution.py:246
  42.6 0.5 %collective-permute-start.13 = (f32[32,1024]{1,0:T(8,128)S(1)}, f32[32,1024]{1,0:T(8,128)S(1)}, u32[]{:S(2)}, u32[]{:S(2)}) collective-permute-start(f32[32,1024]{1,0:T(8,128)S(1)} %slice.9), channel_id=1, source_target_pairs={{0,8},{1,9},{2,10},{3,11},{4,12},{5,13},{6,14},{7,15},{8,0},{9,1},... | collective-permute-start | bytes 393224 | tf_op jit(solution)/shard_map/ppermute | solution.py:246
  43.2 0.1 pad_add_fusion
  43.2 0.5 %collective-permute-start.14 = (f32[64,1024]{1,0:T(8,128)S(1)}, f32[64,1024]{1,0:T(8,128)S(1)}, u32[]{:S(2)}, u32[]{:S(2)}) collective-permute-start(f32[64,1024]{1,0:T(8,128)S(1)} %collective-permute-done.11.refs_0_), channel_id=1, source_target_pairs={{0,1},{1,0},{2,3},{3,2},{4,5},{5,4},{6,7},{7,6},{8,9},{9,8},{10,11... | collective-permute-start | bytes 786440 | tf_op jit(solution)/shard_map/ppermute | solution.py:246
  43.8 0.0 collective-permute-done.8.refs_1_
  43.8 0.1 collective-permute-start.10
  43.9 3.3 %collective-permute-done.7.refs_0_ = f32[64,1024]{1,0:T(8,128)S(1)} collective-permute-done((f32[64,1024]{1,0:T(8,128)S(1)}, f32[64,1024]{1,0:T(8,128)S(1)}, u32[]{:S(2)}, u32[]{:S(2)}) %collective-permute-start.7) | collective-permute-done | bytes 262176 | tf_op jit(solution)/shard_map/ppermute | solution.py:246
  47.1 0.0 collective-permute-start.9
  47.2 0.1 pad_add_fusion.1
  47.2 0.6 %collective-permute-done.12.refs_1_ = f32[32,1024]{1,0:T(8,128)S(1)} collective-permute-done((f32[32,1024]{1,0:T(8,128)S(1)}, f32[32,1024]{1,0:T(8,128)S(1)}, u32[]{:S(2)}, u32[]{:S(2)}) %collective-permute-start.12) | collective-permute-done | bytes 131104 | tf_op jit(solution)/shard_map/ppermute | solution.py:246
  47.8 0.0 collective-permute-start.15
  47.8 0.4 collective-permute-done.13.refs_2_
  48.2 0.4 collective-permute-start.16
  48.6 0.2 select_reduce_fusion
  48.8 0.1 pad_add_fusion.2.place
  48.9 0.0 collective-permute-done.10.refs_3_
  48.9 0.0 collective-permute-done.9.refs_2_
  48.9 0.3 left_parts.1
  49.2 0.0 collective-permute-done.15.refs_4_
  49.2 0.4 collective-permute-done.16.refs_5_
  49.6 0.0 collective-permute-done.14.refs_3_
  49.6 2.4 %outer.1 = f32[1024,512]{1,0:T(8,128)} custom-call(s32[5]{0:T(128)S(1)} %pad_add_fusion.2.place, f32[1024,512]{1,0:T(8,128)S(1)} %weights.1.weights_ref, bf16[1024,256]{1,0:T(8,128)(2,1)S(1)} %get-tuple-element.29.left_high, bf16[1024,256]{1,0:T(8,128)(2,1)S(1)} %get-tuple-element.30.left_low, f32[64,1024]{1,0:T(8,128)S(1)} %collective-permute-done.11.refs_0_, ...), custom_call_target="tpu_custom_call" | custom-call | flops 805306368 | bytes 2097152 | tf_op jit(solution)/shard_map/outer/pallas_call | solution.py:213
  (8 shorter events, 0.1 us)
Async XLA Ops:
  0.0 1.9 %collective-permute-start = (f32[32,1024]{1,0:T(8,128)}, f32[32,1024]{1,0:T(8,128)S(1)}, u32[]{:S(2)}, u32[]{:S(2)}) collective-permute-start(f32[32,1024]{1,0:T(8,128)} %bitcast.9), channel_id=1, source_target_pairs={{0,1},{1,0},{2,3},{3,2},{4,5},{5,4},{6,7},{7,6},{8,9},{9,8},{10,11... | collective-permute-start | bytes 393224 | tf_op jit(solution)/shard_map/ppermute | solution.py:246
  0.7 0.9 %copy-start.1 = (f32[1024,32]{0,1:T(8,128)S(1)}, f32[1024,32]{0,1:T(8,128)}, u32[]{:S(2)}) copy-start(f32[1024,32]{0,1:T(8,128)} %param.7) | copy-start | bytes 393220
  1.9 12.1 %collective-permute-start.2 = (f32[1024,512]{1,0:T(8,128)}, f32[1024,512]{1,0:T(8,128)S(1)}, u32[]{:S(2)}, u32[]{:S(2)}) collective-permute-start(f32[1024,512]{1,0:T(8,128)} %block_ref), channel_id=1, source_target_pairs={{0,1},{1,0},{2,3},{3,2},{4,5},{5,4},{6,7},{7,6},{8,9},{9,8},{10,11... | collective-permute-start | bytes 6291464 | tf_op jit(solution)/shard_map/ppermute | solution.py:246
  2.3 12.8 %collective-permute-start.1 = (f32[64,1024]{1,0:T(8,128)S(1)}, f32[64,1024]{1,0:T(8,128)S(1)}, u32[]{:S(2)}, u32[]{:S(2)}) collective-permute-start(f32[64,1024]{1,0:T(8,128)S(1)} %maximum_select_fusion), channel_id=1, source_target_pairs={{0,8},{1,24},{2,0},{3,16},{4,1},{5,17},{6,9},{7,25},{8,2},{9,18},{... | collective-permute-start | bytes 786440 | tf_op jit(solution)/shard_map/ppermute | solution.py:246
  6.5 14.3 %collective-permute-start.4 = (f32[64,1024]{1,0:T(8,128)S(1)}, f32[64,1024]{1,0:T(8,128)S(1)}, u32[]{:S(2)}, u32[]{:S(2)}) collective-permute-start(f32[64,1024]{1,0:T(8,128)S(1)} %maximum_select_fusion), channel_id=1, source_target_pairs={{0,0},{1,16},{2,8},{3,24},{4,9},{5,25},{6,1},{7,17},{8,10},{9,26},... | collective-permute-start | bytes 786440 | tf_op jit(solution)/shard_map/ppermute | solution.py:246
  11.3 1.6 %copy-start = (f32[1024,512]{1,0:T(8,128)S(1)}, f32[1024,512]{1,0:T(8,128)}, u32[]{:S(2)}) copy-start(f32[1024,512]{1,0:T(8,128)} %block_ref) | copy-start | bytes 6291460
  16.0 7.5 %copy-start.5 = (f32[64]{0:T(128)S(1)}, f32[64]{0:T(128)}, u32[]{:S(2)}) copy-start(f32[64]{0:T(128)} %param.10) | copy-start | bytes 772
  16.0 7.6 %copy-start.2 = (s32[4096]{0:T(1024)S(1)}, s32[4096]{0:T(1024)}, u32[]{:S(2)}) copy-start(s32[4096]{0:T(1024)} %param.8) | copy-start | bytes 49156
  16.0 7.6 %copy-start.3 = (s32[4096]{0:T(1024)S(1)}, s32[4096]{0:T(1024)}, u32[]{:S(2)}) copy-start(s32[4096]{0:T(1024)} %param.9) | copy-start | bytes 49156
  16.0 7.6 %copy-start.4 = (f32[2048]{0:T(1024)S(1)}, f32[2048]{0:T(1024)}, u32[]{:S(2)}) copy-start(f32[2048]{0:T(1024)} %param.11) | copy-start | bytes 24580
  16.0 9.4 %collective-permute-start.3 = (f32[64,1024]{1,0:T(8,128)S(1)}, f32[64,1024]{1,0:T(8,128)S(1)}, u32[]{:S(2)}, u32[]{:S(2)}) collective-permute-start(f32[64,1024]{1,0:T(8,128)S(1)} %contract.2), channel_id=1, source_target_pairs={{0,2},{1,5},{2,0},{3,7},{4,6},{5,1},{6,4},{7,3},{8,8},{9,15},{10,1... | collective-permute-start | bytes 786440 | tf_op jit(solution)/shard_map/ppermute | solution.py:246
  21.6 8.0 %collective-permute-start.5 = (f32[64,1024]{1,0:T(8,128)S(1)}, f32[64,1024]{1,0:T(8,128)S(1)}, u32[]{:S(2)}, u32[]{:S(2)}) collective-permute-start(f32[64,1024]{1,0:T(8,128)S(1)} %contract.3), channel_id=1, source_target_pairs={{0,0},{1,7},{2,2},{3,5},{4,4},{5,3},{6,6},{7,1},{8,10},{9,13},{10,... | collective-permute-start | bytes 786440 | tf_op jit(solution)/shard_map/ppermute | solution.py:246
  29.6 1.6 %collective-permute-start.6 = (f32[64,1024]{1,0:T(8,128)S(1)}, f32[64,1024]{1,0:T(8,128)S(1)}, u32[]{:S(2)}, u32[]{:S(2)}) collective-permute-start(f32[64,1024]{1,0:T(8,128)S(1)} %add.20), channel_id=1, source_target_pairs={{0,1},{1,0},{2,3},{3,2},{4,5},{5,4},{6,7},{7,6},{8,9},{9,8},{10,11... | collective-permute-start | bytes 786440 | tf_op jit(solution)/shard_map/ppermute | solution.py:246
  31.3 11.3 %collective-permute-start.11 = (f32[64,1024]{1,0:T(8,128)S(1)}, f32[64,1024]{1,0:T(8,128)S(1)}, u32[]{:S(2)}, u32[]{:S(2)}) collective-permute-start(f32[64,1024]{1,0:T(8,128)S(1)} %add_add_fusion), channel_id=1, source_target_pairs={{0,0},{1,16},{2,8},{3,24},{4,9},{5,25},{6,1},{7,17},{8,26},{9,10},... | collective-permute-start | bytes 786440 | tf_op jit(solution)/shard_map/ppermute | solution.py:246
  34.9 8.9 %collective-permute-start.8 = (f32[64,1024]{1,0:T(8,128)S(1)}, f32[64,1024]{1,0:T(8,128)S(1)}, u32[]{:S(2)}, u32[]{:S(2)}) collective-permute-start(f32[64,1024]{1,0:T(8,128)S(1)} %add_add_fusion), channel_id=1, source_target_pairs={{0,2},{1,5},{2,0},{3,7},{4,6},{5,1},{6,4},{7,3},{8,10},{9,13},{10,... | collective-permute-start | bytes 786440 | tf_op jit(solution)/shard_map/ppermute | solution.py:246
  35.0 12.2 %collective-permute-start.7 = (f32[64,1024]{1,0:T(8,128)S(1)}, f32[64,1024]{1,0:T(8,128)S(1)}, u32[]{:S(2)}, u32[]{:S(2)}) collective-permute-start(f32[64,1024]{1,0:T(8,128)S(1)} %add_add_fusion), channel_id=1, source_target_pairs={{0,0},{1,7},{2,2},{3,5},{4,4},{5,3},{6,6},{7,1},{8,8},{9,15},{10,1... | collective-permute-start | bytes 786440 | tf_op jit(solution)/shard_map/ppermute | solution.py:246
  38.4 9.4 %collective-permute-start.12 = (f32[32,1024]{1,0:T(8,128)S(1)}, f32[32,1024]{1,0:T(8,128)S(1)}, u32[]{:S(2)}, u32[]{:S(2)}) collective-permute-start(f32[32,1024]{1,0:T(8,128)S(1)} %slice.8), channel_id=1, source_target_pairs={{0,8},{1,24},{2,0},{3,16},{4,1},{5,17},{6,9},{7,25},{8,2},{9,18},{... | collective-permute-start | bytes 393224 | tf_op jit(solution)/shard_map/ppermute | solution.py:246
  42.6 5.6 %collective-permute-start.13 = (f32[32,1024]{1,0:T(8,128)S(1)}, f32[32,1024]{1,0:T(8,128)S(1)}, u32[]{:S(2)}, u32[]{:S(2)}) collective-permute-start(f32[32,1024]{1,0:T(8,128)S(1)} %slice.9), channel_id=1, source_target_pairs={{0,8},{1,9},{2,10},{3,11},{4,12},{5,13},{6,14},{7,15},{8,0},{9,1},... | collective-permute-start | bytes 393224 | tf_op jit(solution)/shard_map/ppermute | solution.py:246
  43.2 6.3 %collective-permute-start.14 = (f32[64,1024]{1,0:T(8,128)S(1)}, f32[64,1024]{1,0:T(8,128)S(1)}, u32[]{:S(2)}, u32[]{:S(2)}) collective-permute-start(f32[64,1024]{1,0:T(8,128)S(1)} %collective-permute-done.11.refs_0_), channel_id=1, source_target_pairs={{0,1},{1,0},{2,3},{3,2},{4,5},{5,4},{6,7},{7,6},{8,9},{9,8},{10,11... | collective-permute-start | bytes 786440 | tf_op jit(solution)/shard_map/ppermute | solution.py:246
  43.8 5.1 %collective-permute-start.10 = (f32[64,1024]{1,0:T(8,128)S(1)}, f32[64,1024]{1,0:T(8,128)S(1)}, u32[]{:S(2)}, u32[]{:S(2)}) collective-permute-start(f32[64,1024]{1,0:T(8,128)S(1)} %collective-permute-done.8.refs_1_), channel_id=1, source_target_pairs={{0,1},{1,0},{2,3},{3,2},{4,5},{5,4},{6,7},{7,6},{8,9},{9,8},{10,11... | collective-permute-start | bytes 786440 | tf_op jit(solution)/shard_map/ppermute | solution.py:246
  47.1 1.7 %collective-permute-start.9 = (f32[64,1024]{1,0:T(8,128)S(1)}, f32[64,1024]{1,0:T(8,128)S(1)}, u32[]{:S(2)}, u32[]{:S(2)}) collective-permute-start(f32[64,1024]{1,0:T(8,128)S(1)} %collective-permute-done.7.refs_0_), channel_id=1, source_target_pairs={{0,1},{1,0},{2,3},{3,2},{4,5},{5,4},{6,7},{7,6},{8,9},{9,8},{10,11... | collective-permute-start | bytes 786440 | tf_op jit(solution)/shard_map/ppermute | solution.py:246
  47.8 1.4 %collective-permute-start.15 = (f32[32,1024]{1,0:T(8,128)S(1)}, f32[32,1024]{1,0:T(8,128)S(1)}, u32[]{:S(2)}, u32[]{:S(2)}) collective-permute-start(f32[32,1024]{1,0:T(8,128)S(1)} %collective-permute-done.12.refs_1_), channel_id=1, source_target_pairs={{0,1},{1,0},{2,3},{3,2},{4,5},{5,4},{6,7},{7,6},{8,9},{9,8},{10,11... | collective-permute-start | bytes 393224 | tf_op jit(solution)/shard_map/ppermute | solution.py:246
  48.2 1.4 %collective-permute-start.16 = (f32[32,1024]{1,0:T(8,128)S(1)}, f32[32,1024]{1,0:T(8,128)S(1)}, u32[]{:S(2)}, u32[]{:S(2)}) collective-permute-start(f32[32,1024]{1,0:T(8,128)S(1)} %collective-permute-done.13.refs_2_), channel_id=1, source_target_pairs={{0,1},{1,0},{2,3},{3,2},{4,5},{5,4},{6,7},{7,6},{8,9},{9,8},{10,11... | collective-permute-start | bytes 393224 | tf_op jit(solution)/shard_map/ppermute | solution.py:246
